TPU v7x, 32 devices: a whole 2x2x4 slice. The times are simulated.
32 devices in a mesh: dp: 16 (over z, y, x), mp: 2 (over core).
Axes of the slice: x: 2, y: 2, z: 4, core: 2. Of those that a mesh axis runs over, the one named last changes fastest.
Arguments:
- tokens: bfloat16 [32768, 768], P(('dp', 'mp')), may hold values from -6 to 6
- cotangent: bfloat16 [32768, 768], P(('dp', 'mp')), may hold values from -6 to 6
- w_query: bfloat16 [768, 768], P(None, 'mp'), may hold values from -0.21875 to 0.21875
- key_projection_weight: bfloat16 [768, 768], P(None, 'mp'), may hold values from -0.21875 to 0.21875
- value_projection_weight: bfloat16 [768, 768], P(None, 'mp'), may hold values from -0.21875 to 0.21875
- w_out: bfloat16 [768, 768], P('mp'), may hold values from -1.25 to 1.25
- w_up: bfloat16 [768, 3072], P(None, 'mp'), may hold values from -0.21875 to 0.21875
- w_down: bfloat16 [3072, 768], P('mp'), may hold values from -0.109375 to 0.109375
- gain_attn: float32 [768], replicated, may hold values from 0.5 to 1.5
- gain_ffn: float32 [768], replicated, may hold values from 0.5 to 1.5
- value_pool: bfloat16 [128, 32, 768], P('dp'), may hold values from -6 to 6
- slot_index: int32 [128, 20], P('dp'), may hold values from 0 to 31
- slot_count: int32 [128], P('dp'), may hold values from 5 to 20
- pad_mask: int32 [128, 256], P('dp'), may hold values from 0 to 1, as said below
Outputs:
- block_out: bfloat16 [32768, 768], P(('dp', 'mp'))
- grad_tokens: float32 [32768, 768], P(('dp', 'mp'))
- grad_w_query: float32 [768, 768], P(None, 'mp')
- grad_w_key: float32 [768, 768], P(None, 'mp')
- grad_w_value: float32 [768, 768], P(None, 'mp')
- grad_w_out: float32 [768, 768], P('mp')
- grad_w_up: float32 [768, 3072], P(None, 'mp')
- grad_w_down: float32 [3072, 768], P('mp')
- grad_gain_attn: float32 [768], replicated
- grad_gain_ffn: float32 [768], replicated
- grad_value_pool: float32 [128, 32, 768], P('dp')
Inputs may be any that keep to these rules, and one draw needn't show every extreme that they name: `pad_mask`: each row is ones from its first position on and zeros after them, with at least 32 ones.
All inputs are finite; a program needn't handle non-finite values.
Results may differ from a plain program's by a relative error of at most 0.018.
Values may be sent and summed in bfloat16 or wider, within the bound.
No kernel may reach another device: no remote copies, remote signals or barrier semaphores. Data moves between devices by JAX's collectives and lax.ppermute only.
A program may use at most 192 MiB of HBM per device.

v0:
```python
import jax
import jax.numpy as jnp
from jax import lax
from jax.sharding import PartitionSpec as P

HDIM = 64


def rms_norm(rows, gain):
    factor = lax.rsqrt(jnp.mean(rows * rows, axis=-1, keepdims=True) + 1e-06)
    return rows * factor * gain


def smooth_gate(values):
    return jax.nn.gelu(values, approximate=True)


def attention_scores(query_heads, key_heads, key_valid, score_scale):
    scores = (
        jnp.einsum("bqhd,bkhd->bhqk", query_heads, key_heads, preferred_element_type=jnp.float32)
        * score_scale
    )
    return jnp.where(key_valid[:, None, None, :], scores, -1000000000.0)


def body(
    tokens,
    cotangent,
    w_query,
    key_projection_weight,
    value_projection_weight,
    w_out,
    w_up,
    w_down,
    gain_attn,
    gain_ffn,
    value_pool,
    slot_index,
    slot_count,
    pad_mask,
):
    seq_count, seq_len = pad_mask.shape
    slot_total = slot_index.shape[1]
    model_width = tokens.shape[1]
    group_rows = seq_count * seq_len
    local_heads = w_query.shape[1] // HDIM
    key_total = slot_total + seq_len
    score_scale = HDIM ** (-0.5)
    inputs = tokens.astype(jnp.float32)
    normed_attn = rms_norm(inputs, gain_attn).astype(jnp.bfloat16)
    attn_rows = lax.all_gather(normed_attn, "mp", axis=0, tiled=True)
    queries = jnp.dot(attn_rows, w_query, preferred_element_type=jnp.float32).astype(jnp.bfloat16)
    pool_ids = lax.broadcasted_iota(jnp.int32, (1, 1, value_pool.shape[1]), 2)
    onehot = slot_index[:, :, None] == pool_ids
    selected = jnp.einsum(
        "bsp,bpd->bsd", onehot.astype(jnp.bfloat16), value_pool, preferred_element_type=jnp.float32
    ).astype(jnp.bfloat16)
    key_source_input = jnp.concatenate(
        [selected, attn_rows.reshape(seq_count, seq_len, model_width)], axis=1
    )
    projected_key_rows = jnp.einsum(
        "guf,fi->gui", key_source_input, key_projection_weight, preferred_element_type=jnp.float32
    ).astype(jnp.bfloat16)
    projected_value_rows = jnp.einsum(
        "guf,fi->gui", key_source_input, value_projection_weight, preferred_element_type=jnp.float32
    ).astype(jnp.bfloat16)
    slot_ids = lax.broadcasted_iota(jnp.int32, (1, slot_total), 1)
    key_valid = jnp.concatenate([slot_ids < slot_count[:, None], pad_mask > 0], axis=1)
    query_heads = queries.reshape(seq_count, seq_len, local_heads, HDIM)
    key_heads = projected_key_rows.reshape(seq_count, key_total, local_heads, HDIM)
    value_heads = projected_value_rows.reshape(seq_count, key_total, local_heads, HDIM)
    scores = attention_scores(query_heads, key_heads, key_valid, score_scale)
    row_peak = jnp.max(scores, axis=-1, keepdims=True)
    raised = jnp.exp(scores - row_peak)
    row_total = jnp.sum(raised, axis=-1, keepdims=True)
    attn_probs = raised / row_total
    log_total = row_peak + jnp.log(row_total)
    mixed_heads = (
        jnp.einsum(
            "bhqk,bkhd->bqhd",
            attn_probs.astype(jnp.bfloat16),
            value_heads,
            preferred_element_type=jnp.float32,
        )
        .reshape(group_rows, -1)
        .astype(jnp.bfloat16)
    )
    middle = inputs + lax.psum_scatter(
        jnp.dot(mixed_heads, w_out, preferred_element_type=jnp.float32).astype(jnp.bfloat16),
        "mp",
        scatter_dimension=0,
        tiled=True,
    ).astype(jnp.float32)
    normed_ffn = rms_norm(middle, gain_ffn).astype(jnp.bfloat16)
    ffn_rows = lax.all_gather(normed_ffn, "mp", axis=0, tiled=True)
    ffn_inner = jnp.dot(ffn_rows, w_up, preferred_element_type=jnp.float32)
    active_f, gate_pull = jax.vjp(smooth_gate, ffn_inner)
    active = active_f.astype(jnp.bfloat16)
    block_f = middle + lax.psum_scatter(
        jnp.dot(active, w_down, preferred_element_type=jnp.float32).astype(jnp.bfloat16),
        "mp",
        scatter_dimension=0,
        tiled=True,
    ).astype(jnp.float32)
    block_out = block_f.astype(jnp.bfloat16)
    grad_rows = lax.all_gather(cotangent, "mp", axis=0, tiled=True)
    grad_w_down = jnp.einsum("rf,rd->fd", active, grad_rows, preferred_element_type=jnp.float32)
    grad_active = jnp.dot(grad_rows, w_down.T, preferred_element_type=jnp.float32)
    grad_inner = gate_pull(grad_active)[0].astype(jnp.bfloat16)
    grad_w_up = jnp.einsum("rd,rf->df", ffn_rows, grad_inner, preferred_element_type=jnp.float32)
    grad_normed_ffn = lax.psum_scatter(
        jnp.dot(grad_inner, w_up.T, preferred_element_type=jnp.float32).astype(jnp.bfloat16),
        "mp",
        scatter_dimension=0,
        tiled=True,
    ).astype(jnp.float32)
    _, norm_pull = jax.vjp(rms_norm, middle, gain_ffn)
    grad_middle_norm, grad_gain_ffn = norm_pull(grad_normed_ffn)
    grad_middle = cotangent.astype(jnp.float32) + grad_middle_norm
    grad_mid_rows = lax.all_gather(grad_middle.astype(jnp.bfloat16), "mp", axis=0, tiled=True)
    grad_w_out = jnp.einsum(
        "re,rd->ed", mixed_heads, grad_mid_rows, preferred_element_type=jnp.float32
    )
    grad_mixed = jnp.dot(grad_mid_rows, w_out.T, preferred_element_type=jnp.float32).astype(
        jnp.bfloat16
    )
    grad_mixed = grad_mixed.reshape(seq_count, seq_len, local_heads, HDIM)
    scores = attention_scores(query_heads, key_heads, key_valid, score_scale)
    attn_probs = jnp.exp(scores - log_total)
    value_rows_gradient = (
        jnp.einsum(
            "bhqk,bqhd->bkhd",
            attn_probs.astype(jnp.bfloat16),
            grad_mixed,
            preferred_element_type=jnp.float32,
        )
        .astype(jnp.bfloat16)
        .reshape(seq_count, key_total, -1)
    )
    grad_probs = jnp.einsum(
        "bqhd,bkhd->bhqk", grad_mixed, value_heads, preferred_element_type=jnp.float32
    )
    row_delta = jnp.sum(attn_probs * grad_probs, axis=-1, keepdims=True)
    grad_scores = (attn_probs * (grad_probs - row_delta)).astype(jnp.bfloat16)
    grad_queries = (
        (
            jnp.einsum(
                "bhqk,bkhd->bqhd", grad_scores, key_heads, preferred_element_type=jnp.float32
            )
            * score_scale
        )
        .astype(jnp.bfloat16)
        .reshape(group_rows, -1)
    )
    key_rows_gradient = (
        (
            jnp.einsum(
                "bhqk,bqhd->bkhd", grad_scores, query_heads, preferred_element_type=jnp.float32
            )
            * score_scale
        )
        .astype(jnp.bfloat16)
        .reshape(seq_count, key_total, -1)
    )
    grad_w_query = jnp.einsum(
        "rd,re->de", attn_rows, grad_queries, preferred_element_type=jnp.float32
    )
    grad_w_key = jnp.einsum(
        "rnw,rnp->wp", key_source_input, key_rows_gradient, preferred_element_type=jnp.float32
    )
    grad_w_value = jnp.einsum(
        "rnw,rnp->wp", key_source_input, value_rows_gradient, preferred_element_type=jnp.float32
    )
    grad_key_input = jnp.einsum(
        "fnp,vp->fnv", key_rows_gradient, key_projection_weight, preferred_element_type=jnp.float32
    ) + jnp.einsum(
        "fnp,vp->fnv",
        value_rows_gradient,
        value_projection_weight,
        preferred_element_type=jnp.float32,
    )
    grad_attn_part = jnp.dot(
        grad_queries, w_query.T, preferred_element_type=jnp.float32
    ) + grad_key_input[:, slot_total:].reshape(group_rows, model_width)
    grad_normed_attn = lax.psum_scatter(
        grad_attn_part.astype(jnp.bfloat16), "mp", scatter_dimension=0, tiled=True
    ).astype(jnp.float32)
    _, norm_pull = jax.vjp(rms_norm, inputs, gain_attn)
    grad_inputs_norm, grad_gain_attn = norm_pull(grad_normed_attn)
    grad_tokens = grad_middle + grad_inputs_norm
    grad_selected, grad_gain_attn, grad_gain_ffn = (
        lax.psum(grad_key_input[:, :slot_total].astype(jnp.bfloat16), "mp").astype(jnp.float32),
        lax.psum(grad_gain_attn.astype(jnp.bfloat16), "mp").astype(jnp.float32),
        lax.psum(grad_gain_ffn.astype(jnp.bfloat16), "mp").astype(jnp.float32),
    )
    grad_value_pool = jnp.einsum(
        "bsp,bsd->bpd", onehot.astype(jnp.float32), grad_selected, precision=lax.Precision.HIGHEST
    )
    (
        grad_w_query,
        grad_w_key,
        grad_w_value,
        grad_w_out,
        grad_w_up,
        grad_w_down,
        grad_gain_attn,
        grad_gain_ffn,
    ) = lax.psum(
        (
            grad_w_query,
            grad_w_key,
            grad_w_value,
            grad_w_out,
            grad_w_up,
            grad_w_down,
            grad_gain_attn,
            grad_gain_ffn,
        ),
        "dp",
    )
    return (
        block_out,
        grad_tokens,
        grad_w_query,
        grad_w_key,
        grad_w_value,
        grad_w_out,
        grad_w_up,
        grad_w_down,
        grad_gain_attn,
        grad_gain_ffn,
        grad_value_pool,
    )


def solution(mesh):
    placed = (
        P(("dp", "mp"), None),
        P(("dp", "mp"), None),
        P(None, "mp"),
        P(None, "mp"),
        P(None, "mp"),
        P("mp", None),
        P(None, "mp"),
        P("mp", None),
        P(),
        P(),
        P("dp", None, None),
        P("dp", None),
        P("dp"),
        P("dp", None),
    )
    return jax.shard_map(
        body,
        mesh=mesh,
        in_specs=placed,
        out_specs=(
            P(("dp", "mp"), None),
            P(("dp", "mp"), None),
            P(None, "mp"),
            P(None, "mp"),
            P(None, "mp"),
            P("mp", None),
            P(None, "mp"),
            P("mp", None),
            P(),
            P(),
            P("dp", None, None),
        ),
        check_vma=False,
    )
```

profile of v0, /device:TPU:0, one launch (start us, length us, event | category | flops | bytes accessed | tf_op | source)
XLA Modules:
  0.0 726.7 jit_solution(970985094961609212)
XLA Ops:
  10.4 3.0 fusion.18
  14.7 13.7 %all-gather.5.cloned.1.call-done = bf16[2048,768]{1,0:T(8,128)(2,1)} async-done(((bf16[1024,768]{1,0:T(8,128)(2,1)}), bf16[2048,768]{1,0:T(8,128)(2,1)}) %all-gather.5.cloned.1.call-update) | async-done | bytes 3145744 | tf_op jit(solution)/shard_map/all_gather | solution.py:51
  28.4 4.8 convolution_convert_fusion.4
  33.2 2.7 copy.38
  35.9 3.2 copy.55
  39.1 3.2 convolution_convert_fusion.5
  42.3 4.0 copy.39
  46.2 5.2 convolution_convert_fusion.6
  51.4 4.1 copy.37
  55.6 10.3 %fusion.48 = (f32[8,6,256]{2,1,0:T(8,128)S(1)}, f32[8,6,256,276]{2,3,1,0:T(8,128)}) fusion(bf16[8,276,6,64]{1,3,2,0:T(8,128)(2,1)} %bitcast.87, bf16[8,256,6,64]{1,0,3,2:T(8,128)(2,1)} %bitcast.89, pred[8,276]{1,0:T(8,128)(4,1)S(1)} %pad_add_fusion), kind=kOutput, calls=%fused_computation.93 | convolution fusion | flops 444272640 | bytes 16885920 | tf_op jit(solution)/shard_map/bqhd,bkhd->bhqk/dot_general | solution.py:20
  65.9 7.8 %fusion.7 = f32[8,6,256]{2,1,0:T(8,128)S(1)} fusion(f32[8,6,256,276]{2,3,1,0:T(8,128)} %get-tuple-element.28, f32[8,6,256]{2,1,0:T(8,128)S(1)} %get-tuple-element.27), kind=kLoop, calls=%fused_computation.16 | loop fusion | flops 6770688 | bytes 13664256 | tf_op jit(solution)/shard_map/reduce_sum | solution.py:75
  73.7 7.7 %fusion.30 = bf16[8,256,6,64]{1,3,2,0:T(8,128)(2,1)S(1)} fusion(bf16[8,276,6,64]{1,3,2,0:T(8,128)(2,1)S(1)} %bitcast.97, f32[8,6,256,276]{2,3,1,0:T(8,128)} %get-tuple-element.28, f32[8,6,256]{2,1,0:T(8,128)S(1)} %fusion.7, f32[8,6,256]{2,1,0:T(8,128)S(1)} %get-tuple-element.27), kind=kOutput, calls=%fused_computation.62 | convolution fusion | flops 445071360 | bytes 16932864 | tf_op jit(solution)/shard_map/bhqk,bkhd->bqhd/dot_general | solution.py:79
  83.9 3.5 convolution_convert_fusion
  87.9 11.8 %reduce-scatter.5.cloned.1.call-done = bf16[1024,768]{1,0:T(8,128)(2,1)} async-done(((bf16[2048,768]{1,0:T(8,128)(2,1)}), bf16[1024,768]{1,0:T(8,128)(2,1)}) %reduce-scatter.5.cloned.1.call-update) | async-done | bytes 1572880 | tf_op jit(solution)/shard_map/reduce_scatter | solution.py:88
  99.7 2.6 multiply_reduce_fusion.1
  104.9 12.8 %all-gather.7.cloned.1.call-done = bf16[2048,768]{1,0:T(8,128)(2,1)} async-done(((bf16[1024,768]{1,0:T(8,128)(2,1)}), bf16[2048,768]{1,0:T(8,128)(2,1)}) %all-gather.7.cloned.1.call-update) | async-done | bytes 3145744 | tf_op jit(solution)/shard_map/all_gather | solution.py:95
  117.7 13.1 %multiply_convert_fusion.1 = (bf16[2048,1536]{1,0:T(8,128)(2,1)}, f32[2048,1536]{1,0:T(8,128)}) fusion(bf16[2048,768]{1,0:T(8,128)(2,1)} %all-gather.7.cloned.1.call-done, bf16[768,1536]{1,0:T(8,128)(2,1)S(1)} %copy-done), kind=kOutput, calls=%fused_computation.15 | convolution fusion | flops 4860149760 | bytes 24379392 | tf_op jit(solution)/shard_map/dot_general | solution.py:96
  132.5 15.6 %fusion.6 = bf16[2048,1536]{1,0:T(8,128)(2,1)S(1)} fusion(f32[2048,1536]{1,0:T(8,128)} %get-tuple-element.32, bf16[2048,768]{1,0:T(8,128)(2,1)} %all-gather.9.cloned.1.call-done, bf16[1536,768]{1,0:T(8,128)(2,1)} %param.21), kind=kOutput, calls=%fused_computation.14 | convolution fusion | flops 4894752768 | bytes 24379392 | tf_op jit(solution)/shard_map/dot_general | solution.py:108
  148.2 2.6 copy-done.45
  150.8 6.4 convolution_convert_fusion.1
  157.5 12.0 %reduce-scatter.9.cloned.1.call-done = bf16[1024,768]{1,0:T(8,128)(2,1)} async-done(((bf16[2048,768]{1,0:T(8,128)(2,1)}), bf16[1024,768]{1,0:T(8,128)(2,1)}) %reduce-scatter.9.cloned.1.call-update) | async-done | bytes 1572880 | tf_op jit(solution)/shard_map/reduce_scatter | solution.py:111
  169.5 3.5 fusion.20
  173.0 4.2 fusion.47
  177.3 13.4 %all-gather.11.cloned.1.call-done = bf16[2048,768]{1,0:T(8,128)(2,1)} async-done(((bf16[1024,768]{1,0:T(8,128)(2,1)}), bf16[2048,768]{1,0:T(8,128)(2,1)}) %all-gather.11.cloned.1.call-update) | async-done | bytes 3145744 | tf_op jit(solution)/shard_map/all_gather | solution.py:120
  190.7 5.0 convolution_convert_fusion.3
  195.6 2.7 copy.42
  200.2 7.4 %fusion.26 = bf16[8,6,64,276]{3,2,1,0:T(8,128)(2,1)S(1)} fusion(f32[8,6,256,276]{2,3,1,0:T(8,128)} %get-tuple-element.28, f32[8,6,256]{2,1,0:T(8,128)S(1)} %log_add_fusion, bf16[8,256,6,64]{1,0,3,2:T(8,128)(2,1)S(1)} %bitcast.91), kind=kOutput, calls=%fused_computation.58 | convolution fusion | flops 441741312 | bytes 16883712 | tf_op jit(solution)/shard_map/bhqk,bqhd->bkhd/dot_general | solution.py:131
  207.6 10.4 %multiply_reduce_fusion = (f32[8,6,256]{2,1,0:T(8,128)S(1)}, f32[8,6,256,276]{2,3,1,0:T(8,128)}) fusion(f32[8,6,256,276]{2,3,1,0:T(8,128)} %get-tuple-element.28, f32[8,6,256]{2,1,0:T(8,128)S(1)} %log_add_fusion, bf16[8,276,6,64]{1,3,2,0:T(8,128)(2,1)S(1)} %bitcast.98, bf16[8,256,6,64]{1,0,3,2:T(8,128)(2,1)S(1)} %bitcast.92), kind=kOutput, calls=%fused_computation.3 | convolution fusion | flops 444272640 | bytes 30498816 | tf_op jit(solution)/shard_map/bqhd,bkhd->bhqk/dot_general | solution.py:140
  218.1 10.3 %multiply_convert_fusion = bf16[8,6,256,276]{2,3,1,0:T(8,128)(2,1)S(1)} fusion(f32[8,6,256,276]{2,3,1,0:T(8,128)} %get-tuple-element.30, f32[8,6,256,276]{2,3,1,0:T(8,128)} %get-tuple-element.28, f32[8,6,256]{2,1,0:T(8,128)S(1)} %get-tuple-element.29, f32[8,6,256]{2,1,0:T(8,128)S(1)} %log_add_fusion), kind=kLoop, calls=%fused_computation.2 | loop fusion | flops 13565952 | bytes 34013184 | tf_op jit(solution)/shard_map/convert_element_type | solution.py:144
  228.4 2.8 fusion.31
  233.5 2.4 fusion.37
  235.9 2.4 convolution_add_fusion
  238.4 2.8 copy-done.5
  241.9 6.3 slice.9
  250.9 6.8 fusion.13
  257.8 9.3 %convolution_convert_fusion.2 = bf16[2048,768]{1,0:T(8,128)(2,1)} fusion(bf16[2048,1536]{1,0:T(8,128)(2,1)} %get-tuple-element.31, bf16[1536,768]{1,0:T(8,128)(2,1)} %param.21), kind=kOutput, calls=%fused_computation.42 | convolution fusion | flops 4833411072 | bytes 11796480 | tf_op jit(solution)/shard_map/dot_general | solution.py:100
  267.1 9.8 %fusion.52 = f32[1536,768]{1,0:T(8,128)} fusion(bf16[2048,1536]{1,0:T(8,128)(2,1)} %get-tuple-element.31, bf16[2048,768]{1,0:T(8,128)(2,1)} %all-gather.9.cloned.1.call-done), kind=kOutput, calls=%fused_computation.97 | convolution fusion | flops 4831838208 | bytes 14155776 | tf_op jit(solution)/shard_map/rf,rd->fd/dot_general | solution.py:107
  277.0 9.7 %fusion.51 = f32[768,1536]{1,0:T(8,128)} fusion(bf16[2048,768]{1,0:T(8,128)(2,1)S(1)} %copy-done.41, bf16[2048,1536]{1,0:T(8,128)(2,1)} %copy-done.45), kind=kOutput, calls=%fused_computation.96 | convolution fusion | flops 4831838208 | bytes 14155776 | tf_op jit(solution)/shard_map/rd,rf->df/dot_general | solution.py:110
  286.7 2.4 fusion.50
  289.1 2.9 fusion.49
  291.9 3.7 convolution_bitcast_fusion
  295.7 3.7 convolution_bitcast_fusion.1
  302.4 2.9 fusion.21
  305.3 2.5 all-reduce.2
  307.7 45.6 %all-reduce = (f32[768]{0:T(1024)}, f32[768]{0:T(1024)}) all-reduce(bf16[768]{0:T(1024)(128)(2,1)S(1)} %get-tuple-element.23, bf16[768]{0:T(1024)(128)(2,1)S(1)} %get-tuple-element.24), channel_id=1, replica_groups=mesh['dp'=16,'mp'=2] {'dp'}, use_global_device_ids=true, to_apply=%region_19.20 | all-reduce | flops 1536 | bytes 9216 | tf_op jit(solution)/shard_map/psum | solution.py:208
  353.4 6.4 fusion.23
  359.8 349.1 %all-reduce.8.cloned.1.call-done = (f32[768,384]{1,0:T(8,128)}, f32[768,384]{1,0:T(8,128)}, f32[768,384]{1,0:T(8,128)}, f32[384,768]{1,0:T(8,128)}, f32[768,1536]{1,0:T(8,128)}, /*index=5*/f32[1536,768]{1,0:T(8,128)}) async-done(((f32[768,384]{1,0:T(8,128)}, f32[768,384]{1,0:T(8,128)}, f32[768,384]{1,0:T(8,128)}, f32[384,768]{1,0:T(8,128)}, f32[768,1536]{1,0:T(8,128)}, /*index=5*/f32[1536,768]{1,0:T(8,128)}), ...) | async-done | bytes 14155792 | tf_op jit(solution)/shard_map/psum | solution.py:208
  708.8 2.5 copy.78
  (143 shorter events, 31.0 us)
Async XLA Ops:
  7.2 110.5 %copy-start = (bf16[768,1536]{1,0:T(8,128)(2,1)S(1)}, bf16[768,1536]{1,0:T(8,128)(2,1)}, u32[]{:S(2)}) copy-start(bf16[768,1536]{1,0:T(8,128)(2,1)} %param.20) | copy-start | bytes 7077892
  7.2 6.3 copy-start.44
  7.2 6.4 copy-start.38
  7.2 6.4 copy-start.27
  7.2 6.4 copy-start.36
  7.2 21.2 %copy-start.25 = (bf16[768,384]{1,0:T(8,128)(2,1)S(1)}, bf16[768,384]{1,0:T(8,128)(2,1)}, u32[]{:S(2)}) copy-start(bf16[768,384]{1,0:T(8,128)(2,1)} %param.16) | copy-start | bytes 1769476
  7.2 21.2 %all-gather.5.cloned.1.call-start = ((), (), s32[]{:S(2)}) async-start(), calls=%async_computation.4 | async-start | bytes 4718592 | tf_op jit(solution)/shard_map/all_gather | solution.py:51
  13.4 86.3 %reduce-scatter.5.cloned.1.call-start = ((), (), s32[]{:S(2)}) async-start(), calls=%async_computation.5 | async-start | bytes 4718592 | tf_op jit(solution)/shard_map/reduce_scatter | solution.py:88
  33.2 5.9 copy-start.23
  33.2 5.9 copy-start.28
  35.9 3.2 copy-start.39
  65.9 7.8 %copy-start.13 = (bf16[8,276,384]{1,2,0:T(8,128)(2,1)S(1)}, bf16[8,276,384]{1,2,0:T(8,128)(2,1)}, u32[]{:S(2)}) copy-start(bf16[8,276,384]{1,2,0:T(8,128)(2,1)} %copy.37) | copy-start | bytes 5087236
  81.3 2.6 copy-start.43
  87.5 14.9 %copy-start.30 = (f32[768]{0:T(1024)S(1)}, f32[768]{0:T(1024)}, u32[]{:S(2)}) copy-start(f32[768]{0:T(1024)} %param.23) | copy-start | bytes 9220
  87.5 30.2 %all-gather.7.cloned.1.call-start = ((), (), s32[]{:S(2)}) async-start(), calls=%async_computation.6 | async-start | bytes 4718592 | tf_op jit(solution)/shard_map/all_gather | solution.py:95
  99.7 2.6 copy-start.2
  99.7 2.8 copy-start.4
  104.3 28.2 %all-gather.9.cloned.1.call-start = ((), (), s32[]{:S(2)}) async-start(), calls=%async_computation.8 | async-start | bytes 4718592 | tf_op jit(solution)/shard_map/all_gather | solution.py:106
  104.9 64.6 %reduce-scatter.9.cloned.1.call-start = ((), (), s32[]{:S(2)}) async-start(), calls=%async_computation.9 | async-start | bytes 4718592 | tf_op jit(solution)/shard_map/reduce_scatter | solution.py:111
  148.2 2.6 copy-start.45
  157.2 12.2 %copy-start.3 = (bf16[1024,768]{1,0:T(8,128)(2,1)S(1)}, bf16[1024,768]{1,0:T(8,128)(2,1)}, u32[]{:S(2)}) copy-start(bf16[1024,768]{1,0:T(8,128)(2,1)} %param.14) | copy-start | bytes 4718596
  157.2 33.4 %all-gather.11.cloned.1.call-start = ((), (), s32[]{:S(2)}) async-start(), calls=%async_computation.10 | async-start | bytes 4718592 | tf_op jit(solution)/shard_map/all_gather | solution.py:120
  169.5 3.5 copy-start.8
  177.2 122.2 %all-reduce.6.cloned.1.call-start = ((), (), s32[]{:S(2)}) async-start(), calls=%async_computation.12 | async-start | bytes 589824 | tf_op jit(solution)/shard_map/psum | solution.py:192
  200.2 7.4 %copy-start.14 = (bf16[8,276,384]{1,2,0:T(8,128)(2,1)S(1)}, bf16[8,276,384]{1,2,0:T(8,128)(2,1)}, u32[]{:S(2)}) copy-start(bf16[8,276,384]{1,2,0:T(8,128)(2,1)} %copy.37) | copy-start | bytes 5087236
  207.6 28.3 %copy-start.9 = (bf16[8,6,64,276]{3,2,1,0:T(8,128)(2,1)}, bf16[8,6,64,276]{3,2,1,0:T(8,128)(2,1)S(1)}, u32[]{:S(2)}) copy-start(bf16[8,6,64,276]{3,2,1,0:T(8,128)(2,1)S(1)} %fusion.26) | copy-start | bytes 5087236
  218.1 10.3 %copy-start.6 = (bf16[8,276,384]{1,2,0:T(8,128)(2,1)S(1)}, bf16[8,276,384]{1,2,0:T(8,128)(2,1)}, u32[]{:S(2)}) copy-start(bf16[8,276,384]{1,2,0:T(8,128)(2,1)} %copy.39) | copy-start | bytes 5087236
  228.4 2.8 copy-start.7
  238.4 2.8 copy-start.5
  241.9 6.3 copy-start.15
  248.2 2.7 copy-start.26
  250.9 51.5 %reduce-scatter.11.cloned.1.call-start = ((), (), s32[]{:S(2)}) async-start(), calls=%async_computation.11 | async-start | bytes 4718592 | tf_op jit(solution)/shard_map/reduce_scatter | solution.py:185
  257.7 95.7 %reduce-scatter.7.cloned.1.call-start = ((), (), s32[]{:S(2)}) async-start(), calls=%async_computation.7 | async-start | bytes 4718592 | tf_op jit(solution)/shard_map/reduce_scatter | solution.py:99
  267.1 441.8 %all-reduce.8.cloned.1.call-start = ((), (), s32[]{:S(2)}) async-start(), calls=%async_computation.13 | async-start | bytes 28311552 | tf_op jit(solution)/shard_map/psum | solution.py:208
  267.1 9.8 %copy-start.41 = (bf16[2048,768]{1,0:T(8,128)(2,1)S(1)}, bf16[2048,768]{1,0:T(8,128)(2,1)}, u32[]{:S(2)}) copy-start(bf16[2048,768]{1,0:T(8,128)(2,1)} %all-gather.7.cloned.1.call-done) | copy-start | bytes 9437188
  277.0 9.7 %copy-start.19 = (bf16[48,8,8,256]{3,1,2,0:T(8,128)(2,1)S(1)}, bf16[48,8,8,256]{3,1,2,0:T(8,128)(2,1)}, u32[]{:S(2)}) copy-start(bf16[48,8,8,256]{3,1,2,0:T(8,128)(2,1)} %copy-done.18) | copy-start | bytes 4718596
  277.0 9.7 %copy-start.42 = (bf16[2048,768]{1,0:T(8,128)(2,1)S(1)}, bf16[2048,768]{1,0:T(8,128)(2,1)}, u32[]{:S(2)}) copy-start(bf16[2048,768]{1,0:T(8,128)(2,1)} %all-gather.11.cloned.1.call-done) | copy-start | bytes 9437188
  289.1 2.9 copy-start.10
  289.1 2.9 copy-start.29
  291.9 3.7 copy-start.12
  299.4 2.9 copy-start.32
  299.4 2.9 copy-start.35
  299.4 53.9 %copy-start.34 = (f32[1024]{0:T(1024)S(1)}, f32[1024]{0:T(1024)}, u32[]{:S(2)}) copy-start(f32[1024]{0:T(1024)} %copy-done.33) | copy-start | bytes 12292
  708.8 3.5 copy-start.21
  708.8 4.5 copy-start.20
  711.3 3.6 copy-start.17
  713.4 4.0 slice-start
  715.0 4.7 copy-start.1
  (10 other events, 17.8 us)
Sparse Core Ops, SparseCore 0:
  13.5 14.8 all-gather.4
  87.6 12.0 reduce-scatter.4
  104.4 13.2 all-gather.6
  119.2 13.2 all-gather.8
  157.4 12.0 reduce-scatter.8
  177.3 13.2 all-gather.10
  251.0 19.4 all-reduce.5
  273.3 12.0 reduce-scatter.10
  287.8 12.0 reduce-scatter.6
  306.7 402.0 all-reduce.7
where the time goes:
time: 733 us; the launch traced here: 727 us
  waiting for transfers between devices  415 us (57%)
  matrix products  154 us (21%)
  local copies, waits for them, and re-layouts  49.1 us (7%)
  blocking collectives  48.1 us (7%)
  other arithmetic  44.5 us (6%)
  between operations  14.8 us (2%)
    psum x1, waiting for transfers between devices, body(): lax.psum((grad_w_query, grad_w_key, grad_w_value, grad_w_out, grad_w_up,...  349 us
    psum x1, blocking collectives, body(): lax.psum((grad_w_query, grad_w_key, grad_w_value, grad_w_out, grad_w_up,...  45.6 us
    unnamed x106, local copies, waits for them, and re-layouts  26.8 us
    dot_general x1, matrix products, body(): jnp.dot(grad_rows, w_down.T, preferred_element_type=jnp.float32)  15.6 us
  transfers between devices with their start and end apart: 10, of which 7 were waited for; matrix products, arithmetic and copies ran while one was open for 10% of the time, Pallas kernels for 0%

commit v1 on v0

v1 whole, which is shorter than its diff:
```python
import functools

import jax
import jax.numpy as jnp
from jax import lax
from jax.experimental import pallas as pl
from jax.experimental.pallas import tpu as pltpu
from jax.sharding import PartitionSpec as P

HDIM = 64
SCALE = HDIM ** (-0.5)
EPS = 1e-06
SLOT_ROWS = 32
BF = jnp.bfloat16
F32 = jnp.float32
MIB = 1 << 20

NN = (((1,), (0,)), ((), ()))
NT = (((1,), (1,)), ((), ()))
TN = (((0,), (0,)), ((), ()))
ANYWHERE = pl.BlockSpec(memory_space=pl.ANY)
IN_SMEM = pl.BlockSpec(memory_space=pltpu.SMEM)
sds = jax.ShapeDtypeStruct


def mm(left, right, dims=NN):
    return lax.dot_general(left, right, dims, preferred_element_type=F32)


def params(mib):
    return pltpu.CompilerParams(vmem_limit_bytes=mib * MIB)


def cost(us):
    return pl.CostEstimate(flops=int(us * 1.15e9), bytes_accessed=0, transcendentals=0)


def stored(shape, dtype):
    return pltpu.HBM(shape, dtype)


def streamed(*arrays):
    return [pltpu.with_memory_space_constraint(a, pltpu.HBM) for a in arrays]


def whole(shape):
    zeros = (0,) * len(shape)
    return pl.BlockSpec(shape, lambda *_: zeros)


def rows_of(rows, width):
    return pl.BlockSpec((rows, width), lambda s, *_: (s, 0))


def seq_of(*shape):
    tail = (0,) * len(shape)
    return pl.BlockSpec((1, *shape), lambda s, *_: (s, *tail))


MARK = sds((8, 128), F32)
MARK_SPEC = whole((8, 128))


def marked(refs):
    refs[-1][...] = jnp.zeros_like(refs[-1])
    return refs[:-1]


def head_masks():
    lanes = lax.broadcasted_iota(jnp.int32, (1, 2 * HDIM), 1)
    return lanes < HDIM, lanes >= HDIM


def pair_columns(width):
    return [slice(at, at + 2 * HDIM) for at in range(0, width, 2 * HDIM)]


def attend(q, k, v, bias, probs_ref):
    masks = head_masks()
    pieces = []
    for pair, cols in enumerate(pair_columns(q.shape[1])):
        qp, kp, vp = q[:, cols], k[:, cols], v[:, cols]
        mixed = None
        for half, mask in enumerate(masks):
            scores = mm(kp, jnp.where(mask, qp, 0), NT) + bias
            peak = jnp.max(scores, axis=0, keepdims=True)
            raised = jnp.exp(scores - peak)
            total = jnp.sum(raised, axis=0, keepdims=True)
            probs = (raised * (1.0 / total)).astype(BF)
            probs_ref[0, 2 * pair + half] = probs
            part = mm(probs, jnp.where(mask, vp, 0), TN)
            mixed = part if mixed is None else mixed + part
        pieces.append(mixed.astype(BF))
    return jnp.concatenate(pieces, axis=1)


def project(xn, sel, wq, wk, wv):
    rows = jnp.concatenate([xn, sel], axis=0)
    q = (mm(xn, wq) * SCALE).astype(BF)
    k = mm(rows, wk).astype(BF)
    v = mm(rows, wv).astype(BF)
    return q, k, v


def key_bias(seq, counts_ref, pads_ref, length):
    tokens = jnp.sum(pads_ref[pl.ds(seq, 1), :], axis=1, keepdims=True)
    token_ids = lax.broadcasted_iota(jnp.int32, (length, 1), 0)
    slot_ids = lax.broadcasted_iota(jnp.int32, (SLOT_ROWS, 1), 0)
    live = jnp.concatenate([token_ids < tokens, slot_ids < counts_ref[seq]], axis=0)
    return jnp.where(live, 0.0, -1e9).astype(F32)


def attn_first_kernel(
    first_ref, counts_ref, idx_ref, x_ref, gain_ref, pool_ref, pads_ref, wq_ref, wk_ref, wv_ref,
    xn_ref, sel_ref, bias_ref, hot_ref, q_ref, k_ref, v_ref, probs_ref, mixed_ref,
):
    seq = first_ref[0] + pl.program_id(0)
    x = x_ref[...].astype(F32)
    factor = lax.rsqrt(jnp.mean(x * x, axis=-1, keepdims=True) + EPS)
    xn = (x * factor * gain_ref[...].reshape(1, -1)).astype(BF)
    xn_ref[...] = xn
    spots = (pool_ref.shape[1], SLOT_ROWS)
    pool_ids = lax.broadcasted_iota(jnp.int32, spots, 0)
    slot_ids = lax.broadcasted_iota(jnp.int32, spots, 1)
    chosen = jnp.full(spots, -1, jnp.int32)
    for slot in range(idx_ref.shape[1]):
        chosen = jnp.where(slot_ids == slot, idx_ref[seq, slot], chosen)
    hot = jnp.where(chosen == pool_ids, 1.0, 0.0).astype(BF)
    hot_ref[0] = hot
    sel = mm(hot, pool_ref[0], TN).astype(BF)
    sel_ref[0] = sel
    bias = key_bias(seq, counts_ref, pads_ref, x_ref.shape[0])
    bias_ref[0] = bias
    q, k, v = project(xn, sel, wq_ref[...], wk_ref[...], wv_ref[...])
    q_ref[...] = q
    k_ref[0] = k
    v_ref[0] = v
    mixed_ref[...] = attend(q, k, v, bias, probs_ref)


def attn_second_kernel(
    x_ref, gain_ref, xn_ref, sel_ref, bias_ref, first_ref, wq_ref, wk_ref, wv_ref, woo_ref, wot_ref,
    q_ref, k_ref, v_ref, probs_ref, mixed_ref, middle_ref, nf_ref,
):
    q, k, v = project(xn_ref[...], sel_ref[0], wq_ref[...], wk_ref[...], wv_ref[...])
    q_ref[...] = q
    k_ref[0] = k
    v_ref[0] = v
    mixed = attend(q, k, v, bias_ref[0], probs_ref)
    mixed_ref[...] = mixed
    middle = x_ref[...].astype(F32) + mm(first_ref[...], woo_ref[...]) + mm(mixed, wot_ref[...])
    middle_ref[...] = middle
    factor = lax.rsqrt(jnp.mean(middle * middle, axis=-1, keepdims=True) + EPS)
    nf_ref[...] = (middle * factor * gain_ref[...].reshape(1, -1)).astype(BF)


def attention_forward(tokens, gain_attn, gain_ffn, pool, idx, counts, pads, seqs, mine, own, other):
    rows, width = tokens.shape
    length = rows // seqs
    keys = length + SLOT_ROWS
    inner = own[0].shape[1]
    heads = inner // HDIM
    row, head, key = rows_of(length, width), rows_of(length, inner), seq_of(keys, inner)
    kept = [
        (stored((rows, inner), BF), head),
        (stored((seqs, keys, inner), BF), key),
        (stored((seqs, keys, inner), BF), key),
        (stored((seqs, heads, keys, length), BF), seq_of(heads, keys, length)),
        (stored((rows, inner), BF), head),
    ]
    weight = whole((width, inner))
    outs = [
        (stored((rows, width), BF), row),
        (stored((seqs, SLOT_ROWS, width), BF), seq_of(SLOT_ROWS, width)),
        (stored((seqs, keys, 1), F32), seq_of(keys, 1)),
        (stored((seqs, pool.shape[1], SLOT_ROWS), BF), seq_of(pool.shape[1], SLOT_ROWS)),
        *kept,
    ]
    xn, sel, bias, hot, *first = pl.pallas_call(
        attn_first_kernel,
        grid_spec=pltpu.PrefetchScalarGridSpec(
            num_scalar_prefetch=3,
            grid=(seqs,),
            in_specs=[
                row,
                whole((width,)),
                pl.BlockSpec((1, *pool.shape[1:]), lambda s, first, *_: (first[0] + s, 0, 0)),
                whole(pads.shape),
                weight, weight, weight,
            ],
            out_specs=[o[1] for o in outs],
        ),
        out_shape=[o[0] for o in outs],
        compiler_params=params(14),
        cost_estimate=cost(12),
        name="attn_first",
    )(mine, counts, idx, *streamed(tokens, gain_attn, pool, pads, *own[:3]))
    outs = [
        *kept,
        (stored((rows, width), F32), row),
        (stored((rows, width), BF), row),
    ]
    *second, middle, nf = pl.pallas_call(
        attn_second_kernel,
        grid=(seqs,),
        out_shape=[o[0] for o in outs],
        in_specs=[
            row,
            whole((width,)),
            row,
            seq_of(SLOT_ROWS, width),
            seq_of(keys, 1),
            head,
            weight, weight, weight,
            whole((inner, width)),
            whole((inner, width)),
        ],
        out_specs=[o[1] for o in outs],
        compiler_params=params(18),
        cost_estimate=cost(12),
        name="attn_second",
    )(
        *streamed(tokens, gain_ffn),
        *streamed(xn, sel, bias, first[4]),
        *other[:3], *streamed(own[3]), other[3],
    )
    return xn, sel, hot, first, second, middle, nf


def gate_and_slope(h):
    c = 0.7978845608028654
    square = h * h
    t = jnp.tanh(h * (c + (c * 0.044715) * square))
    half = 0.5 + 0.5 * t
    slope = half + (0.5 * h) * (1.0 - t * t) * (c + (3.0 * c * 0.044715) * square)
    return h * half, slope


def ffn_kernel(own, chunk, nf_ref, cot_ref, wu_ref, wd_ref, *refs):
    rows = nf_ref.shape[0]
    units = wu_ref.shape[1]
    if own:
        got_ref, sides_ref = refs[:2]
        act_ref, di_ref, keep_ref, send_ref = marked(refs)[-4:]
    else:
        act_ref, di_ref, grad_ref = marked(refs)[-3:]
    wu, wd = wu_ref[...], wd_ref[...]
    for r in range(rows // chunk):
        at = slice(r * chunk, (r + 1) * chunk)
        act, slope = gate_and_slope(mm(nf_ref[at], wu))
        act_ref[at] = act.astype(BF)
        di_ref[at] = (mm(cot_ref[at], wd, NT) * slope).astype(BF)
    at = pl.ds(pl.multiple_of(pl.program_id(0) * units, units), units)
    down = mm(act_ref[...], cot_ref[...], TN).astype(BF)
    up = mm(nf_ref[...], di_ref[...], TN).astype(BF)
    if not own:
        grad_ref[0, at] = down
        grad_ref[1, :, at] = up
        return
    down = bf_sum(down, got_ref[0, at])
    up = bf_sum(up, got_ref[1, :, at])
    upper = sides_ref[0] == 1

    @pl.when(upper)
    def _():
        keep_ref[:, at] = up
        send_ref[at] = down

    @pl.when(jnp.logical_not(upper))
    def _():
        keep_ref[at] = down
        send_ref[:, at] = up


def ffn_part(index, nf, cot, weights, sums=(), after=()):
    rows, width = nf.shape
    own = len(sums) > 0
    units = 256
    steps = width // units
    full, square, part = whole((rows, width)), (width, width), pl.BlockSpec((rows, units), lambda j: (0, j))
    grads = [sds(square, BF)] * 2 if own else [sds((2, *square), BF)]
    extra = [whole((2, *square)), IN_SMEM] if own else []
    return pl.pallas_call(
        functools.partial(ffn_kernel, own, 256),
        grid=(steps,),
        out_shape=[*[stored((rows, width), BF)] * 2, *grads, MARK],
        in_specs=[
            full,
            full,
            pl.BlockSpec((width, units), lambda j: (0, index * steps + j)),
            pl.BlockSpec((units, width), lambda j: (index * steps + j, 0)),
            *extra,
            *[ANYWHERE] * len(after),
        ],
        out_specs=[part, part, *[whole(g.shape) for g in grads], MARK_SPEC],
        compiler_params=params(26),
        cost_estimate=cost(10),
        name="ffn_part",
    )(*streamed(nf, cot), *weights, *sums, *after)


def norm_back_kernel(cot_ref, middle_ref, gain_ref, wut_ref, wuo_ref, d0t, d0o, d1t, d1o, *refs):
    gm_ref, gmb_ref, gg_ref = marked(refs)[-3:]
    middle = middle_ref[...]
    width = middle.shape[1]
    dnf = 0.0
    for at, parts in enumerate(((d0t, d0o), (d1t, d1o))):
        cols = slice(at * width, (at + 1) * width)
        for part, wu_ref in zip(parts, (wut_ref, wuo_ref)):
            dnf += mm(part[...], wu_ref[:, cols], NT)
    factor = lax.rsqrt(jnp.mean(middle * middle, axis=-1, keepdims=True) + EPS)
    scaled = middle * factor
    e = gain_ref[...].reshape(1, -1) * dnf
    inner_mean = jnp.mean(e * scaled, axis=-1, keepdims=True)
    gm = cot_ref[...].astype(F32) + factor * (e - scaled * inner_mean)
    gm_ref[...] = gm
    gmb_ref[...] = gm.astype(BF)
    total = jnp.sum(dnf * scaled, axis=0, keepdims=True)
    gg_ref[...] = jnp.where(pl.program_id(0) == 0, 0.0, gg_ref[...]) + total


def norm_back(cot, middle, gain_ffn, wu_oth, wu_own, dis, after=()):
    rows, width = cot.shape
    block = 256
    row = rows_of(block, width)
    return pl.pallas_call(
        norm_back_kernel,
        grid=(rows // block,),
        out_shape=[stored((rows, width), F32), stored((rows, width), BF), sds((1, width), F32), MARK],
        in_specs=[
            row, row, whole((width,)), whole(wu_own.shape), whole(wu_own.shape), row, row, row, row,
            *[ANYWHERE] * len(after),
        ],
        out_specs=[row, row, whole((1, width)), MARK_SPEC],
        compiler_params=params(22),
        cost_estimate=cost(9),
        name="norm_back",
    )(*streamed(cot, middle, gain_ffn), wu_oth, *streamed(wu_own, *dis), *after)


def block_out_kernel(middle_ref, wdt_ref, wdo_ref, a0t, a0o, a1t, a1o, *refs):
    total = middle_ref[...]
    width = total.shape[1]
    for at, parts in enumerate(((a0t, a0o), (a1t, a1o))):
        for part, wd_ref in zip(parts, (wdt_ref, wdo_ref)):
            total += mm(part[...], wd_ref[at * width : (at + 1) * width])
    marked(refs)[-1][...] = total.astype(BF)


def block_output(middle, wd_oth, wd_own, acts, after=()):
    rows, width = middle.shape
    block = 256
    row = rows_of(block, width)
    return pl.pallas_call(
        block_out_kernel,
        grid=(rows // block,),
        out_shape=[stored((rows, width), BF), MARK],
        in_specs=[
            row, whole(wd_own.shape), whole(wd_own.shape), row, row, row, row, *[ANYWHERE] * len(after),
        ],
        out_specs=[row, MARK_SPEC],
        compiler_params=params(18),
        cost_estimate=cost(8),
        name="block_out",
    )(*streamed(middle), wd_oth, *streamed(wd_own, *acts), *after)


def stack_halves(grad):
    half = grad.shape[0] // 2
    return jnp.concatenate([grad[:half], grad[half:]], axis=1)


def attn_back_kernel(
    gm_ref, xn_ref, selall_ref, wo_ref, q_ref, k_ref, v_ref, p_ref, m_ref, *refs
):
    awo, aw, slots = refs[-3:]
    dq_ref, dk_ref, dv_ref, grad_ref = marked(refs[:-3])[-4:]
    step = pl.program_id(0)
    masks = head_masks()
    gm, xn = gm_ref[...], xn_ref[...]
    length = gm.shape[0]

    @pl.when(step == 0)
    def _():
        awo[...] = jnp.zeros_like(awo)
        aw[...] = jnp.zeros_like(aw)

    awo[...] += mm(m_ref[...], gm, TN)
    dmix = mm(gm, wo_ref[...], NT).astype(BF)
    dqs, dks, dvs = [], [], []
    for pair, cols in enumerate(pair_columns(dmix.shape[1])):
        qp, kp, vp, dp = q_ref[:, cols], k_ref[0, :, cols], v_ref[0, :, cols], dmix[:, cols]
        dq = dk = dv = 0.0
        for half, mask in enumerate(masks):
            probs = p_ref[0, 2 * pair + half]
            dp_head = jnp.where(mask, dp, 0)
            weighted = mm(vp, dp_head, NT)
            high = probs.astype(F32)
            delta = jnp.sum(high * weighted, axis=0, keepdims=True)
            ds = (high * (weighted - delta)).astype(BF)
            dv += mm(probs, dp_head)
            dq += mm(ds, jnp.where(mask, kp, 0), TN)
            dk += mm(ds, jnp.where(mask, qp, 0))
        dqs.append((dq * SCALE).astype(BF))
        dks.append(dk.astype(BF))
        dvs.append(dv.astype(BF))
    dq, dk, dv = [jnp.concatenate(d, axis=1) for d in (dqs, dks, dvs)]
    dq_ref[...] = dq
    dk_ref[0] = dk
    dv_ref[0] = dv
    aw[...] += mm(xn, jnp.concatenate([dq, dk[:length], dv[:length]], axis=1), TN)
    at = pl.ds(pl.multiple_of(step * SLOT_ROWS, SLOT_ROWS), SLOT_ROWS)
    slots[at] = jnp.concatenate([dk[length:], dv[length:]], axis=1)

    @pl.when(step == pl.num_programs(0) - 1)
    def _():
        inner = awo.shape[0]
        grad_ref[:inner] = awo[...].astype(BF)
        grad_ref[inner : 2 * inner] = stack_halves(aw[:, :inner].astype(BF))
        rest = (aw[:, inner:] + mm(selall_ref[...], slots[...], TN)).astype(BF)
        grad_ref[2 * inner : 3 * inner] = stack_halves(rest[:, :inner])
        grad_ref[3 * inner :] = stack_halves(rest[:, inner:])


def attn_back(gmb, xn, sel, wo, kept, us, after=()):
    rows, width = gmb.shape
    seqs, heads, keys, length = kept[3].shape
    inner = wo.shape[0]
    row, head, key = rows_of(length, width), rows_of(length, inner), seq_of(keys, inner)
    grads = sds((4 * inner, width), BF)
    outs = [
        (stored((rows, inner), BF), head),
        (stored((seqs, keys, inner), BF), key),
        (stored((seqs, keys, inner), BF), key),
        (grads, whole(grads.shape)),
        (MARK, MARK_SPEC),
    ]
    return pl.pallas_call(
        attn_back_kernel,
        grid=(seqs,),
        out_shape=[o[0] for o in outs],
        in_specs=[
            row, row, whole((seqs * SLOT_ROWS, width)), whole((inner, width)),
            head, key, key, seq_of(heads, keys, length), head, *[ANYWHERE] * len(after),
        ],
        out_specs=[o[1] for o in outs],
        scratch_shapes=[
            pltpu.VMEM((inner, width), F32),
            pltpu.VMEM((width, 3 * inner), F32),
            pltpu.VMEM((seqs * SLOT_ROWS, 2 * inner), BF),
        ],
        compiler_params=params(22),
        cost_estimate=cost(us),
        name="attn_back",
    )(*streamed(gmb, xn, sel.reshape(seqs * SLOT_ROWS, width)), wo, *streamed(*kept), *after)


def input_back_kernel(
    x_ref, gm_ref, gain_ref, hot_ref, wqo, wqt, wko, wkt, wvo, wvt,
    dqo, dqt, dko, dkt, dvo, dvt, *refs,
):
    wq, wk, wv = refs[-3:]
    gx_ref, gp_ref, gg_ref = marked(refs[:-3])[-3:]
    first = pl.program_id(0) == 0
    inner = wqo.shape[1]
    length = x_ref.shape[0]

    @pl.when(first)
    def _():
        for cat, own, oth in ((wq, wqo, wqt), (wk, wko, wkt), (wv, wvo, wvt)):
            cat[:, :inner] = own[...]
            cat[:, inner:] = oth[...]

    dkeys = mm(jnp.concatenate([dko[0], dkt[0]], axis=1), wk[...], NT)
    dkeys += mm(jnp.concatenate([dvo[0], dvt[0]], axis=1), wv[...], NT)
    dxn = dkeys[:length] + mm(jnp.concatenate([dqo[...], dqt[...]], axis=1), wq[...], NT)
    x = x_ref[...].astype(F32)
    factor = lax.rsqrt(jnp.mean(x * x, axis=-1, keepdims=True) + EPS)
    scaled = x * factor
    c = gain_ref[...].reshape(1, -1) * dxn
    inner_mean = jnp.mean(c * scaled, axis=-1, keepdims=True)
    gx_ref[...] = gm_ref[...] + factor * (c - scaled * inner_mean)
    total = jnp.sum(dxn * scaled, axis=0, keepdims=True)
    gg_ref[...] = jnp.where(first, 0.0, gg_ref[...]) + total
    gp_ref[0] = mm(hot_ref[0], dkeys[length:].astype(BF))


def input_back(tokens, gm, gain_attn, hot, own, oth, d_own, d_oth, after=()):
    rows, width = tokens.shape
    seqs, keys, inner = d_own[1].shape
    length = rows // seqs
    pool_rows = hot.shape[1]
    row, head, key = rows_of(length, width), rows_of(length, inner), seq_of(keys, inner)
    return pl.pallas_call(
        input_back_kernel,
        grid=(seqs,),
        out_shape=[
            stored((rows, width), F32),
            sds((seqs, pool_rows, width), F32),
            sds((1, width), F32),
            MARK,
        ],
        in_specs=[
            row, row, whole((width,)), seq_of(pool_rows, SLOT_ROWS),
            *[whole((width, inner))] * 6, head, head, key, key, key, key, *[ANYWHERE] * len(after),
        ],
        out_specs=[row, seq_of(pool_rows, width), whole((1, width)), MARK_SPEC],
        scratch_shapes=[pltpu.VMEM((width, 2 * inner), BF)] * 3,
        compiler_params=params(22),
        cost_estimate=cost(8),
        name="input_back",
    )(
        *streamed(tokens, gm, gain_attn), *streamed(hot),
        *[w for pair in zip(streamed(*own[:3]), oth[:3]) for w in pair],
        *streamed(d_own[0], d_oth[0], d_own[1], d_oth[1], d_own[2], d_oth[2]), *after,
    )


def bf_sum(a, b):
    return (a.astype(F32) + b.astype(F32)).astype(BF)


def grid_steps(rows):
    return next((n for n in (4, 2) if rows % (16 * n) == 0 and rows // n >= 96), 1)


def halve_kernel(level, sides_ref, a_ref, b_ref, *refs):
    keep_ref, send_ref = marked(refs)[-2:]
    low, high = bf_sum(a_ref[0], b_ref[0]), bf_sum(a_ref[1], b_ref[1])
    upper = sides_ref[level] == 1
    keep_ref[...] = jnp.where(upper, high, low)
    send_ref[...] = jnp.where(upper, low, high)


def halve(level, sides, a, b, after=()):
    rows, width = a.shape[0] // 2, a.shape[1]
    steps = grid_steps(rows)
    pair = pl.BlockSpec((2, rows // steps, width), lambda j: (0, j, 0))
    half = rows_of(rows // steps, width)
    return pl.pallas_call(
        functools.partial(halve_kernel, level),
        grid=(steps,),
        out_shape=[sds((rows, width), BF)] * 2 + [MARK],
        in_specs=[IN_SMEM, pair, pair, *[ANYWHERE] * len(after)],
        out_specs=[half, half, MARK_SPEC],
        compiler_params=params(6),
        cost_estimate=cost(0.05),
        name="halve",
    )(sides, a.reshape(2, rows, width), b.reshape(2, rows, width), *after)


def add_kernel(a_ref, b_ref, *refs):
    marked(refs)[-1][...] = (a_ref[...].astype(F32) + b_ref[...].astype(F32)).astype(a_ref.dtype)


def add(a, b, after=()):
    full = whole(a.shape)
    return pl.pallas_call(
        add_kernel,
        out_shape=[sds(a.shape, a.dtype), MARK],
        in_specs=[full, full, *[ANYWHERE] * len(after)],
        out_specs=[full, MARK_SPEC],
        compiler_params=params(2),
        cost_estimate=cost(0.05),
        name="add",
    )(a, b, *after)


def joined(level, sides_ref, mine, got):
    upper = sides_ref[level] == 1
    return jnp.where(upper, got, mine), jnp.where(upper, mine, got)


def join_kernel(level, sides_ref, mine_ref, got_ref, *refs):
    out_ref = marked(refs)[-1]
    out_ref[0], out_ref[1] = joined(level, sides_ref, mine_ref[...], got_ref[...])


def join(level, sides, mine, got, after=()):
    rows, width = mine.shape
    steps = grid_steps(rows)
    part = rows_of(rows // steps, width)
    both, mark = pl.pallas_call(
        functools.partial(join_kernel, level),
        grid=(steps,),
        out_shape=[sds((2, rows, width), BF), MARK],
        in_specs=[IN_SMEM, part, part, *[ANYWHERE] * len(after)],
        out_specs=[pl.BlockSpec((2, rows // steps, width), lambda j: (0, j, 0)), MARK_SPEC],
        compiler_params=params(6),
        cost_estimate=cost(0.05),
        name="join",
    )(sides, mine, got, *after)
    return both.reshape(2 * rows, width), mark


def pool_join_kernel(mine_ref, got_ref, *refs):
    out_ref = marked(refs)[-1]
    first = lax.axis_index("mp") == 0
    mine, got = mine_ref[...], got_ref[...]
    seqs = mine.shape[0]
    out_ref[:seqs] = jnp.where(first, mine, got)
    out_ref[seqs:] = jnp.where(first, got, mine)


def pool_join(mine, got, after=()):
    full, shape = whole(mine.shape), (2 * mine.shape[0], *mine.shape[1:])
    return pl.pallas_call(
        pool_join_kernel,
        out_shape=[stored(shape, F32), MARK],
        in_specs=[full, full, *[ANYWHERE] * len(after)],
        out_specs=[whole(shape), MARK_SPEC],
        compiler_params=params(6),
        cost_estimate=cost(1),
        name="pool_join",
    )(mine, got, *after)


def ffn_finish_kernel(sides_ref, mine_ref, got_ref, *refs):
    down_ref, up_ref = marked(refs)[-2:]
    down, up = joined(0, sides_ref, mine_ref[...], got_ref[...])
    down_ref[...] = down.astype(F32)
    up_ref[...] = up.astype(F32)


def ffn_finish(index, count, sides, mine, got, before=(), after=()):
    width = mine.shape[1]
    steps = 4
    part = rows_of(width // steps, width)
    shapes = [stored((count * width, width), F32), stored((width, count * width), F32)]
    return pl.pallas_call(
        ffn_finish_kernel,
        grid=(steps,),
        out_shape=[*shapes, MARK],
        in_specs=[IN_SMEM, part, part, *[ANYWHERE] * (len(before) + len(after))],
        out_specs=[
            pl.BlockSpec((width // steps, width), lambda j: (index * steps + j, 0)),
            pl.BlockSpec((width // steps, width), lambda j: (j, index)),
            MARK_SPEC,
        ],
        input_output_aliases={3 + at: at for at in range(len(before))},
        compiler_params=params(10),
        cost_estimate=cost(2),
        name="ffn_finish",
    )(sides, mine, got, *before, *after)


def attn_finish_kernel(sides_ref, mine_ref, got_ref, *refs):
    wq_ref, wk_ref, wv_ref, wo_ref = refs[-4:]
    inner = wo_ref.shape[0]
    low, high = joined(0, sides_ref, mine_ref[...], got_ref[...])
    wo_ref[...] = low[:inner].astype(F32)
    for ref, stacked in ((wq_ref, low[inner:]), (wk_ref, high[:inner]), (wv_ref, high[inner:])):
        ref[:inner] = stacked[:, :inner].astype(F32)
        ref[inner:] = stacked[:, inner:].astype(F32)


def attn_finish(sides, mine, got, after=()):
    rows, width = mine.shape
    inner = rows // 2
    full = whole(mine.shape)
    return pl.pallas_call(
        attn_finish_kernel,
        out_shape=[stored((width, inner), F32)] * 3 + [stored((inner, width), F32)],
        in_specs=[IN_SMEM, full, full, *[ANYWHERE] * len(after)],
        out_specs=[whole((width, inner))] * 3 + [whole((inner, width))],
        compiler_params=params(14),
        cost_estimate=cost(2),
        name="attn_finish",
    )(sides, mine, got, *after)


class ChipSum:
    def __init__(self, dp, mp):
        bits = dp.bit_length() - 1
        here = lax.axis_index("dp")
        bit = [(here >> b) & 1 for b in range(bits)]
        if bits == 4:
            orders = ([1, 2, 4, 12], [2, 1, 12, 4])
            sides = (
                [bit[0], bit[1], bit[2] ^ bit[3], bit[3]],
                [bit[1], bit[0], bit[3], bit[2]],
            )
        else:
            swap = list(range(bits))
            swap[:2] = swap[:2][::-1]
            orders = ([1 << b for b in range(bits)], [1 << b for b in swap])
            sides = (bit, [bit[b] for b in swap])
        second = lax.axis_index("mp") % 2 == 1
        self.sides = jnp.where(second, jnp.stack(sides[1]), jnp.stack(sides[0]))
        self.levels = bits
        self.pairs = [
            [
                (d * mp + m, (d ^ orders[m % 2][b]) * mp + m)
                for d in range(dp)
                for m in range(mp)
            ]
            for b in range(bits)
        ]

    def exchange(self, level, array):
        return lax.ppermute(array, ("dp", "mp"), self.pairs[level])


class Group:
    def __init__(self, chips, mine, got, at=0):
        self.chips, self.mine, self.got, self.at = chips, mine, got, at

    @property
    def done(self):
        return self.at == 2 * self.chips.levels

    def step(self, after=()):
        chips, levels = self.chips, self.chips.levels
        level = self.at if self.at < levels else 2 * levels - 1 - self.at
        if self.at < levels:
            self.mine, sent, mark = halve(level, chips.sides, self.mine, self.got, after)
        elif self.at == levels:
            self.mine, mark = add(self.mine, self.got, after)
            sent = self.mine
        else:
            self.mine, mark = join(level + 1, chips.sides, self.mine, self.got, after)
            sent = self.mine
        self.got = chips.exchange(level, sent)
        self.at += 1
        return [mark]


class Small:
    def __init__(self, chips, array, got):
        self.chips, self.mine, self.got, self.at = chips, array, got, -1

    @property
    def done(self):
        return self.at == self.chips.levels

    def step(self, after=()):
        self.mine, mark = add(self.mine, self.got, after)
        self.at += 1
        if not self.done:
            self.got = self.chips.exchange(self.at, self.mine)
        return [mark]


def body(
    dp, mp, tokens, cotangent, w_query, key_projection_weight, value_projection_weight, w_out,
    w_up, w_down, gain_attn, gain_ffn, value_pool, slot_index, slot_count, pad_mask,
):
    seqs = tokens.shape[0] // pad_mask.shape[1]
    mine = (lax.axis_index("mp") * seqs)[None]

    def core_swap(array):
        return lax.ppermute(array, "mp", [(i, i ^ 1) for i in range(mp)])

    own = (w_query, key_projection_weight, value_projection_weight, w_out)
    oth = tuple(core_swap(w) for w in own)
    wu_oth, wd_oth = core_swap(w_up), core_swap(w_down)
    xn, sel, hot, first, second, middle, nf = attention_forward(
        tokens, gain_attn, gain_ffn, value_pool, slot_index, slot_count, pad_mask, seqs, mine,
        own, oth,
    )
    chips = ChipSum(dp, mp)
    count = w_up.shape[1] // w_up.shape[0]
    weights_oth, weights_own = (wu_oth, wd_oth), streamed(w_up, w_down)
    acts, dis, swapped, ffn, mark = [], [], [], [], []
    for at in range(count):
        act, di, grad, mark = ffn_part(at, nf, cotangent, weights_oth, (), mark)
        acts.append([act])
        dis.append([di])
        swapped.append(core_swap(grad))
        mark = [mark]
    for at in range(count):
        act, di, keep, send, mark = ffn_part(
            at, nf, cotangent, weights_own, (swapped[at], chips.sides), mark
        )
        acts[at].append(act)
        dis[at].append(di)
        ffn.append(Group(chips, keep, chips.exchange(0, send), 1))
        mark = [mark]
    acts, dis = sum(acts, []), sum(dis, [])
    gm, gmb, gg_ffn, mark = norm_back(cotangent, middle, gain_ffn, wu_oth, w_up, dis, mark)
    mark = ffn[0].step([mark])
    *d_oth, a_oth, mark = attn_back(gmb, xn, sel, oth[3], second, 1, mark)
    a_got = core_swap(a_oth)
    mark = ffn[0].step(ffn[1].step([mark]))
    *d_own, a_own, mark = attn_back(gmb, xn, sel, *streamed(w_out), first, 30, mark)
    attn = Group(chips, a_own, a_got)
    mark = ffn[1].step(ffn[0].step(attn.step([mark])))
    grad_tokens, grad_pool, gg_attn, mark = input_back(
        tokens, gm, gain_attn, hot, own, oth, d_own, d_oth, mark
    )
    pool_got = core_swap(grad_pool)
    gains = jnp.concatenate([gg_attn, gg_ffn], axis=0)
    gains = Small(chips, gains, core_swap(gains))
    mark = ffn[1].step(ffn[0].step(attn.step([mark])))
    block_out, mark = block_output(middle, wd_oth, w_down, acts, mark)
    grad_value_pool, mark = pool_join(grad_pool, pool_got, [mark])
    mark = [mark]
    ready = []
    while not attn.done or len(ready) < count or not gains.done:
        for at in range(count):
            if not ffn[at].done:
                mark = ffn[at].step(mark)
            elif len(ready) == at:
                out = ffn_finish(at, count, chips.sides, ffn[at].mine, ffn[at].got, ready[-1] if ready else (), mark)
                ready.append(out[:2])
                mark = [out[2]]
        if not attn.done:
            mark = attn.step(mark)
        if not gains.done:
            mark = gains.step(mark)
    grad_wd, grad_wu = ready[-1]
    grad_wq, grad_wk, grad_wv, grad_wo = attn_finish(chips.sides, attn.mine, attn.got, mark)
    return (
        block_out, grad_tokens, grad_wq, grad_wk, grad_wv, grad_wo, grad_wu, grad_wd,
        gains.mine[0], gains.mine[1], grad_value_pool,
    )


def solution(mesh):
    placed = (
        P(("dp", "mp"), None),
        P(("dp", "mp"), None),
        P(None, "mp"),
        P(None, "mp"),
        P(None, "mp"),
        P("mp", None),
        P(None, "mp"),
        P("mp", None),
        P(),
        P(),
        P("dp", None, None),
        P("dp", None),
        P("dp"),
        P("dp", None),
    )
    return jax.shard_map(
        functools.partial(body, mesh.shape["dp"], mesh.shape["mp"]),
        mesh=mesh,
        in_specs=placed,
        out_specs=(
            P(("dp", "mp"), None),
            P(("dp", "mp"), None),
            P(None, "mp"),
            P(None, "mp"),
            P(None, "mp"),
            P("mp", None),
            P(None, "mp"),
            P("mp", None),
            P(),
            P(),
            P("dp", None, None),
        ),
        check_vma=False,
    )
```

time: 733 us -> 275 us (0.38)
  waiting for transfers between devices: 415 us -> 72.5 us
  Pallas kernels: 0 us -> 156 us
  matrix products: 154 us -> 0 us
  blocking collectives: 48.1 us -> 0 us
  local copies, waits for them, and re-layouts: 49.1 us -> 1.95 us
  other arithmetic: 44.5 us -> 0.09 us
  starting transfers between devices: 0.99 us -> 42.4 us
  between operations: 14.8 us -> 1.02 us
    psum x2 -> x0, waiting for transfers between devices: 349 us -> none  [the longest x1 349 us: body(): lax.psum((grad_w_query, grad_w_key, grad_w_value, grad_w_out, grad_w_up,...]
    pallas_call x0 -> x42, Pallas kernels: none -> 156 us  [the longest x4 39.4 us: ffn_part(): pl.pallas_call(functools.partial(ffn_kernel, own, 256), grid=(steps,), ou...]
    dot_general x26 -> x0, matrix products: 154 us -> none  [the longest x1 15.6 us: body(): jnp.dot(grad_rows, w_down.T, preferred_element_type=jnp.float32)]
    ppermute x0 -> x39, waiting for transfers between devices: none -> 72.5 us  [the longest x28 71.6 us: exchange(): return lax.ppermute(array, ('dp', 'mp'), self.pairs[level])]
    psum x2 -> x0, blocking collectives: 48.1 us -> none  [the longest x1 45.6 us: body(): lax.psum((grad_w_query, grad_w_key, grad_w_value, grad_w_out, grad_w_up,...]
    ppermute x0 -> x39, starting transfers between devices: none -> 42.4 us  [the longest x28 39.7 us: exchange(): return lax.ppermute(array, ('dp', 'mp'), self.pairs[level])]
    all_gather x4 -> x0, waiting for transfers between devices: 41.6 us -> none  [the longest x1 13.7 us: body(): attn_rows = lax.all_gather(normed_attn, 'mp', axis=0, tiled=True)]
    unnamed x106 -> x4, local copies, waits for them, and re-layouts: 26.8 us -> 1.34 us
  transfers between devices with their start and end apart: 10 -> 39, of which waited for: 7 -> 13; matrix products, arithmetic and copies ran while one was open for 10% -> 0% of each run, Pallas kernels for 0% -> 51%
where the time goes in v1:
time: 275 us; the launch traced here: 274 us
  Pallas kernels  156 us (57%)
  waiting for transfers between devices  72.5 us (26%)
  starting transfers between devices  42.4 us (15%)
    ppermute x28, waiting for transfers between devices, exchange(): return lax.ppermute(array, ('dp', 'mp'), self.pairs[level])  71.6 us
    ppermute x28, starting transfers between devices, exchange(): return lax.ppermute(array, ('dp', 'mp'), self.pairs[level])  39.7 us
    pallas_call x4, Pallas kernels, ffn_part(): pl.pallas_call(functools.partial(ffn_kernel, own, 256), grid=(steps,), ou...  39.4 us
    pallas_call x2, Pallas kernels, attn_back(): pl.pallas_call(attn_back_kernel, grid=(seqs,), out_shape=[o[0] for o in o...  31.4 us
    pallas_call x1, Pallas kernels, attention_forward(): pl.pallas_call(attn_second_kernel, grid=(seqs,), out_shape=[o[0] for o in...  14.8 us
    pallas_call x1, Pallas kernels, attention_forward(): pl.pallas_call(attn_first_kernel, grid_spec=pltpu.PrefetchScalarGridSpec(...  13 us
    pallas_call x1, Pallas kernels, norm_back(): pl.pallas_call(norm_back_kernel, grid=(rows // block,), out_shape=[stored...  11.8 us
    pallas_call x1, Pallas kernels, input_back(): pl.pallas_call(input_back_kernel, grid=(seqs,), out_shape=[stored((rows,...  10.4 us
  transfers between devices with their start and end apart: 39, of which 13 were waited for; matrix products, arithmetic and copies ran while one was open for 0% of the time, Pallas kernels for 51%

profile of v1, /device:TPU:0, one launch (start us, length us, event | category | flops | bytes accessed | tf_op | source)
XLA Modules:
  0.0 274.2 jit_solution(17441297590400941727)
XLA Ops:
  2.2 0.9 collective-permute-done.wq_ref.wqt
  4.8 13.0 %attn_first.1 = (bf16[1024,768]{1,0:T(8,128)(2,1)}, bf16[4,32,768]{2,1,0:T(8,128)(2,1)}, f32[4,288,1]{2,1,0:T(8,128)}, bf16[4,32,32]{2,1,0:T(8,128)(2,1)}, bf16[...) custom-call(s32[1]{0:T(128)} %bitcast.first_ref, ...), custom_call_target="tpu_custom_call" | custom-call | flops 13799999488 | tf_op jit(solution)/shard_map/attn_first/pallas_call | solution.py:179
  17.8 14.8 %attn_second.1 = (bf16[1024,384]{1,0:T(8,128)(2,1)}, bf16[4,288,384]{2,1,0:T(8,128)(2,1)}, bf16[4,288,384]{2,1,0:T(8,128)(2,1)}, bf16[4,6,288,256]{3,2,1,0:T(8,1...) custom-call(bf16[1024,768]{1,0:T(8,128)(2,1)} %x_ref.5, f32[768]{0:T(1024)} %gain_ref.6, ...), custom_call_target="tpu_custom_call" | custom-call | flops 13799999488 | tf_op jit(solution)/shard_map/attn_second/pallas_call | solution.py:203
  32.6 9.4 %ffn_part.4 = (bf16[1024,768]{1,0:T(8,128)(2,1)}, bf16[1024,768]{1,0:T(8,128)(2,1)}, bf16[2,768,768]{2,1,0:T(8,128)(2,1)}, f32[8,128]{1,0:T(8,128)S(1)}) custom-call(bf16[1024,768]{1,0:T(8,128)(2,1)} %get-tuple-element.146.nf_ref, bf16[1024,768]{1,0:T(8,128)(2,1)} %cot_ref.9, bf16[768,1536]{1,0:T(8,128)(2,1)} %collective-permute-done.5.wu_ref.wut_ref, ...), custom_call_target="tpu_custom_call" | custom-call | flops 11500000256 | tf_op jit(solution)/shard_map/ffn_part/pallas_call | solution.py:283
  42.3 9.5 %ffn_part.5 = (bf16[1024,768]{1,0:T(8,128)(2,1)}, bf16[1024,768]{1,0:T(8,128)(2,1)}, bf16[2,768,768]{2,1,0:T(8,128)(2,1)}, f32[8,128]{1,0:T(8,128)S(1)}) custom-call(bf16[1024,768]{1,0:T(8,128)(2,1)} %get-tuple-element.146.nf_ref, bf16[1024,768]{1,0:T(8,128)(2,1)} %cot_ref.9, bf16[768,1536]{1,0:T(8,128)(2,1)} %collective-permute-done.5.wu_ref.wut_ref, ...), custom_call_target="tpu_custom_call" | custom-call | flops 11500000256 | tf_op jit(solution)/shard_map/ffn_part/pallas_call | solution.py:283
  52.3 10.1 %ffn_part.6 = (bf16[1024,768]{1,0:T(8,128)(2,1)}, bf16[1024,768]{1,0:T(8,128)(2,1)}, bf16[768,768]{1,0:T(8,128)(2,1)S(1)}, bf16[768,768]{1,0:T(8,128)(2,1)S(1)}, f32[8,128]{1,0:T(8,128)S(1)}) custom-call(bf16[1024,768]{1,0:T(8,128)(2,1)} %get-tuple-element.146.nf_ref, bf16[1024,768]{1,0:T(8,128)(2,1)} %cot_ref.9, bf16[768,1536]{1,0:T(8,128)(2,1)} %wuo_ref.1, ...), custom_call_target="tpu_custom_call" | custom-call | flops 11500000256 | tf_op jit(solution)/shard_map/ffn_part/pallas_call | solution.py:283
  62.4 2.6 collective-permute-start.9
  65.0 10.4 %ffn_part.7 = (bf16[1024,768]{1,0:T(8,128)(2,1)}, bf16[1024,768]{1,0:T(8,128)(2,1)}, bf16[768,768]{1,0:T(8,128)(2,1)S(1)}, bf16[768,768]{1,0:T(8,128)(2,1)S(1)}, f32[8,128]{1,0:T(8,128)S(1)}) custom-call(bf16[1024,768]{1,0:T(8,128)(2,1)} %get-tuple-element.146.nf_ref, bf16[1024,768]{1,0:T(8,128)(2,1)} %cot_ref.9, bf16[768,1536]{1,0:T(8,128)(2,1)} %wuo_ref.1, ...), custom_call_target="tpu_custom_call" | custom-call | flops 11500000256 | tf_op jit(solution)/shard_map/ffn_part/pallas_call | solution.py:283
  75.5 11.8 %norm_back.1 = (f32[1024,768]{1,0:T(8,128)}, bf16[1024,768]{1,0:T(8,128)(2,1)}, f32[1,768]{1,0:T(1,128)S(1)}, f32[8,128]{1,0:T(8,128)S(1)}) custom-call(bf16[1024,768]{1,0:T(8,128)(2,1)} %cot_ref.9, f32[1024,768]{1,0:T(8,128)} %get-tuple-element.145.middle_ref, f32[768]{0:T(1024)} %gain_ref.6, bf16[768,1536]{1,0:T(8,128)(2,1)} %collective-permute-done.5.wu_ref.wut_ref, ...), custom_call_target="tpu_custom_call" | custom-call | flops 10350000128 | tf_op jit(solution)/shard_map/norm_back/pallas_call | solution.py:326
  87.3 1.1 halve.10
  88.4 2.1 collective-permute-start.11
  90.5 15.7 %attn_back.2 = (bf16[1024,384]{1,0:T(8,128)(2,1)}, bf16[4,288,384]{2,1,0:T(8,128)(2,1)}, bf16[4,288,384]{2,1,0:T(8,128)(2,1)}, bf16[1536,768]{1,0:T(8,128)(2,1)S(1)}, f32[8,128]{1,0:T(8,128)S(1)}) custom-call(bf16[1024,768]{1,0:T(8,128)(2,1)} %get-tuple-element.163.gm_ref, bf16[1024,768]{1,0:T(8,128)(2,1)} %get-tuple-element.141.xn_ref, ...), custom_call_target="tpu_custom_call" | custom-call | flops 1150000000 | tf_op jit(solution)/shard_map/attn_back/pallas_call | solution.py:438
  106.2 1.1 halve.11
  108.3 15.7 %attn_back.3 = (bf16[1024,384]{1,0:T(8,128)(2,1)}, bf16[4,288,384]{2,1,0:T(8,128)(2,1)}, bf16[4,288,384]{2,1,0:T(8,128)(2,1)}, bf16[1536,768]{1,0:T(8,128)(2,1)S(1)}, f32[8,128]{1,0:T(8,128)S(1)}) custom-call(bf16[1024,768]{1,0:T(8,128)(2,1)} %get-tuple-element.163.gm_ref, bf16[1024,768]{1,0:T(8,128)(2,1)} %get-tuple-element.141.xn_ref, ...), custom_call_target="tpu_custom_call" | custom-call | flops 34500001792 | tf_op jit(solution)/shard_map/attn_back/pallas_call | solution.py:438
  124.1 1.6 halve.13
  125.7 2.0 collective-permute-start.16
  127.6 1.6 collective-permute-start.12
  129.2 8.0 %collective-permute-done.12 = bf16[192,768]{1,0:T(8,128)(2,1)S(1)} collective-permute-done((bf16[192,768]{1,0:T(8,128)(2,1)S(1)}, bf16[192,768]{1,0:T(8,128)(2,1)S(1)}, u32[]{:S(2)}, u32[]{:S(2)}) %collective-permute-start.12) | collective-permute-done | bytes 294944 | tf_op jit(solution)/shard_map/ppermute | solution.py:701
  137.8 4.0 %collective-permute-start.15 = (bf16[96,768]{1,0:T(8,128)(2,1)S(1)}, bf16[96,768]{1,0:T(8,128)(2,1)S(1)}, u32[]{:S(2)}, u32[]{:S(2)}) collective-permute-start(bf16[96,768]{1,0:T(8,128)(2,1)S(1)} %get-tuple-element.194), channel_id=1, source_target_pairs={{0,24},{1,9},{2,26},{3,11},{4,28},{5,13},{6,30},{7,15},{8,16},{9,1... | collective-permute-start | bytes 442376 | tf_op jit(solution)/shard_map/ppermute | solution.py:701
  142.7 10.4 %input_back.1 = (f32[1024,768]{1,0:T(8,128)}, f32[4,32,768]{2,1,0:T(8,128)S(1)}, f32[1,768]{1,0:T(1,128)S(1)}, f32[8,128]{1,0:T(8,128)S(1)}) custom-call(bf16[1024,768]{1,0:T(8,128)(2,1)} %x_ref.5, f32[1024,768]{1,0:T(8,128)} %get-tuple-element.197.gm_ref, f32[768]{0:T(1024)} %gain_ref.7, bf16[4,32,32]{2,1,0:T(8,128)(2,1)} %get-tuple-element.198.hot_ref, ...), custom_call_target="tpu_custom_call" | custom-call | flops 9200000000 | tf_op jit(solution)/shard_map/input_back/pallas_call | solution.py:494
  153.3 1.1 halve.16
  155.1 1.5 collective-permute-start.17
  157.3 9.5 %block_out.1 = (bf16[1024,768]{1,0:T(8,128)(2,1)}, f32[8,128]{1,0:T(8,128)S(1)}) custom-call(f32[1024,768]{1,0:T(8,128)} %get-tuple-element.145.middle_ref, bf16[1536,768]{1,0:T(8,128)(2,1)S(1)} %collective-permute-done.4.wd_ref.wdt_ref, bf16[1536,768]{1,0:T(8,128)(2,1)} %wdo_ref.1, bf16[1024,768]{1,0:T(8,128)(2,1)} %get-tuple-element.147.a0t, ...), custom_call_target="tpu_custom_call" | custom-call | flops 9200000000 | tf_op jit(solution)/shard_map/block_out/pallas_call | solution.py:354
  166.8 1.0 pool_join.1
  168.3 1.6 collective-permute-start.23
  169.9 2.8 %collective-permute-start.18 = (bf16[96,768]{1,0:T(8,128)(2,1)S(1)}, bf16[96,768]{1,0:T(8,128)(2,1)S(1)}, u32[]{:S(2)}, u32[]{:S(2)}) collective-permute-start(bf16[96,768]{1,0:T(8,128)(2,1)S(1)} %get-tuple-element.215), channel_id=1, source_target_pairs={{0,24},{1,9},{2,26},{3,11},{4,28},{5,13},{6,30},{7,15},{8,16},{9,1... | collective-permute-start | bytes 442376 | tf_op jit(solution)/shard_map/ppermute | solution.py:701
  172.8 9.8 %collective-permute-done.18.b_ref = bf16[96,768]{1,0:T(8,128)(2,1)S(1)} collective-permute-done((bf16[96,768]{1,0:T(8,128)(2,1)S(1)}, bf16[96,768]{1,0:T(8,128)(2,1)S(1)}, u32[]{:S(2)}, u32[]{:S(2)}) %collective-permute-start.18) | collective-permute-done | bytes 147488 | tf_op jit(solution)/shard_map/ppermute | solution.py:701
  184.2 1.6 collective-permute-start.27
  186.2 1.1 collective-permute-start.28
  187.3 8.1 %collective-permute-done.22.got_ref = bf16[96,768]{1,0:T(8,128)(2,1)S(1)} collective-permute-done((bf16[96,768]{1,0:T(8,128)(2,1)S(1)}, bf16[96,768]{1,0:T(8,128)(2,1)S(1)}, u32[]{:S(2)}, u32[]{:S(2)}) %collective-permute-start.22) | collective-permute-done | bytes 147488 | tf_op jit(solution)/shard_map/ppermute | solution.py:701
  197.9 9.5 %collective-permute-done.26.got_ref = bf16[192,768]{1,0:T(8,128)(2,1)S(1)} collective-permute-done((bf16[192,768]{1,0:T(8,128)(2,1)S(1)}, bf16[192,768]{1,0:T(8,128)(2,1)S(1)}, u32[]{:S(2)}, u32[]{:S(2)}) %collective-permute-start.26) | collective-permute-done | bytes 294944 | tf_op jit(solution)/shard_map/ppermute | solution.py:701
  208.5 2.1 collective-permute-start.25
  210.6 1.5 collective-permute-start.32
  212.1 3.4 %collective-permute-done.25.b_ref = bf16[96,768]{1,0:T(8,128)(2,1)S(1)} collective-permute-done((bf16[96,768]{1,0:T(8,128)(2,1)S(1)}, bf16[96,768]{1,0:T(8,128)(2,1)S(1)}, u32[]{:S(2)}, u32[]{:S(2)}) %collective-permute-start.25) | collective-permute-done | bytes 147488 | tf_op jit(solution)/shard_map/ppermute | solution.py:701
  215.5 2.6 collective-permute-done.32.b_ref
  218.8 3.1 %ffn_finish.2 = (f32[1536,768]{1,0:T(8,128)}, f32[768,1536]{1,0:T(8,128)}, f32[8,128]{1,0:T(8,128)S(1)}) custom-call(s32[4]{0:T(128)S(1)} %broadcast_select_fusion.refs_1_.sides_ref, bf16[768,768]{1,0:T(8,128)(2,1)S(1)} %bitcast.71, bf16[768,768]{1,0:T(8,128)(2,1)S(1)} %collective-permute-done.31.got_ref, f32[8,128]{1,0:T(8,128)S(1)} %get-tuple-element.246.refs_0_), custom_call_target="tpu_custom_call" | custom-call | flops 2300000000 | tf_op jit(solution)/shard_map/ffn_finish/pallas_call | solution.py:630
  221.9 0.8 join.14
  223.3 4.7 %collective-permute-start.29 = (bf16[96,768]{1,0:T(8,128)(2,1)S(1)}, bf16[96,768]{1,0:T(8,128)(2,1)S(1)}, u32[]{:S(2)}, u32[]{:S(2)}) collective-permute-start(bf16[96,768]{1,0:T(8,128)(2,1)S(1)} %get-tuple-element.241.mine_ref), channel_id=1, source_target_pairs={{0,24},{1,9},{2,26},{3,11},{4,28},{5,13},{6,30},{7,15},{8,16},{9,1... | collective-permute-start | bytes 442376 | tf_op jit(solution)/shard_map/ppermute | solution.py:701
  228.0 3.6 %collective-permute-done.29.got_ref = bf16[96,768]{1,0:T(8,128)(2,1)S(1)} collective-permute-done((bf16[96,768]{1,0:T(8,128)(2,1)S(1)}, bf16[96,768]{1,0:T(8,128)(2,1)S(1)}, u32[]{:S(2)}, u32[]{:S(2)}) %collective-permute-start.29) | collective-permute-done | bytes 147488 | tf_op jit(solution)/shard_map/ppermute | solution.py:701
  232.2 2.0 collective-permute-start.35
  234.3 6.2 %collective-permute-done.35.b_ref = f32[2,768]{1,0:T(2,128)S(1)} collective-permute-done((f32[2,768]{1,0:T(2,128)S(1)}, f32[2,768]{1,0:T(2,128)S(1)}, u32[]{:S(2)}, u32[]{:S(2)}) %collective-permute-start.35) | collective-permute-done | bytes 6176 | tf_op jit(solution)/shard_map/ppermute | solution.py:701
  240.5 3.1 %ffn_finish.3 = (f32[1536,768]{1,0:T(8,128)}, f32[768,1536]{1,0:T(8,128)}, f32[8,128]{1,0:T(8,128)S(1)}) custom-call(s32[4]{0:T(128)S(1)} %broadcast_select_fusion.refs_1_.sides_ref, bf16[768,768]{1,0:T(8,128)(2,1)S(1)} %bitcast.45, bf16[768,768]{1,0:T(8,128)(2,1)S(1)} %collective-permute-done.34.got_ref, ...), custom_call_target="tpu_custom_call", output_to_operand_aliasing={{0}: (3, {}), {1}: (4, {})} | custom-call | flops 2300000000 | tf_op jit(solution)/shard_map/ffn_finish/pallas_call | solution.py:630
  244.3 1.5 collective-permute-start.36
  245.8 3.9 %collective-permute-start.37 = (f32[2,768]{1,0:T(2,128)S(1)}, f32[2,768]{1,0:T(2,128)S(1)}, u32[]{:S(2)}, u32[]{:S(2)}) collective-permute-start(f32[2,768]{1,0:T(2,128)S(1)} %get-tuple-element.258.a_ref), channel_id=1, source_target_pairs={{0,24},{1,9},{2,26},{3,11},{4,28},{5,13},{6,30},{7,15},{8,16},{9,1... | collective-permute-start | bytes 18440 | tf_op jit(solution)/shard_map/ppermute | solution.py:701
  249.7 1.6 collective-permute-done.37.b_ref
  251.3 2.9 %collective-permute-done.36.got_ref = bf16[384,768]{1,0:T(8,128)(2,1)S(1)} collective-permute-done((bf16[384,768]{1,0:T(8,128)(2,1)S(1)}, bf16[384,768]{1,0:T(8,128)(2,1)S(1)}, u32[]{:S(2)}, u32[]{:S(2)}) %collective-permute-start.36) | collective-permute-done | bytes 589856 | tf_op jit(solution)/shard_map/ppermute | solution.py:701
  256.1 15.2 %collective-permute-done.38.got_ref = bf16[768,768]{1,0:T(8,128)(2,1)S(1)} collective-permute-done((bf16[768,768]{1,0:T(8,128)(2,1)S(1)}, bf16[768,768]{1,0:T(8,128)(2,1)S(1)}, u32[]{:S(2)}, u32[]{:S(2)}) %collective-permute-start.38) | collective-permute-done | bytes 1179680 | tf_op jit(solution)/shard_map/ppermute | solution.py:701
  271.3 2.9 %attn_finish.1 = (f32[768,384]{1,0:T(8,128)}, f32[768,384]{1,0:T(8,128)}, f32[768,384]{1,0:T(8,128)}, f32[384,768]{1,0:T(8,128)}) custom-call(s32[4]{0:T(128)S(1)} %broadcast_select_fusion.refs_1_.sides_ref, bf16[768,768]{1,0:T(8,128)(2,1)S(1)} %bitcast.73, bf16[768,768]{1,0:T(8,128)(2,1)S(1)} %collective-permute-done.38.got_ref, ...), custom_call_target="tpu_custom_call" | custom-call | flops 2300000000 | tf_op jit(solution)/shard_map/attn_finish/pallas_call | solution.py:661
  (79 shorter events, 18.6 us)
Async XLA Ops:
  0.6 2.4 collective-permute-start
  1.2 16.6 %collective-permute-start.1 = (bf16[768,384]{1,0:T(8,128)(2,1)}, bf16[768,384]{1,0:T(8,128)(2,1)}, u32[]{:S(2)}, u32[]{:S(2)}) collective-permute-start(bf16[768,384]{1,0:T(8,128)(2,1)} %wko.1), channel_id=1, source_target_pairs={{0,1},{1,0},{2,3},{3,2},{4,5},{5,4},{6,7},{7,6},{8,9},{9,8},{10,11... | collective-permute-start | bytes 1769480 | tf_op jit(solution)/shard_map/ppermute | solution.py:752
  1.2 16.6 %collective-permute-start.2 = (bf16[768,384]{1,0:T(8,128)(2,1)}, bf16[768,384]{1,0:T(8,128)(2,1)}, u32[]{:S(2)}, u32[]{:S(2)}) collective-permute-start(bf16[768,384]{1,0:T(8,128)(2,1)} %wvo.1), channel_id=1, source_target_pairs={{0,1},{1,0},{2,3},{3,2},{4,5},{5,4},{6,7},{7,6},{8,9},{9,8},{10,11... | collective-permute-start | bytes 1769480 | tf_op jit(solution)/shard_map/ppermute | solution.py:752
  1.7 16.1 %collective-permute-start.3 = (bf16[384,768]{1,0:T(8,128)(2,1)}, bf16[384,768]{1,0:T(8,128)(2,1)S(1)}, u32[]{:S(2)}, u32[]{:S(2)}) collective-permute-start(bf16[384,768]{1,0:T(8,128)(2,1)} %wo_ref.1), channel_id=1, source_target_pairs={{0,1},{1,0},{2,3},{3,2},{4,5},{5,4},{6,7},{7,6},{8,9},{9,8},{10,11... | collective-permute-start | bytes 1769480 | tf_op jit(solution)/shard_map/ppermute | solution.py:752
  1.8 30.9 %collective-permute-start.5 = (bf16[768,1536]{1,0:T(8,128)(2,1)}, bf16[768,1536]{1,0:T(8,128)(2,1)}, u32[]{:S(2)}, u32[]{:S(2)}) collective-permute-start(bf16[768,1536]{1,0:T(8,128)(2,1)} %wuo_ref.1), channel_id=1, source_target_pairs={{0,1},{1,0},{2,3},{3,2},{4,5},{5,4},{6,7},{7,6},{8,9},{9,8},{10,11... | collective-permute-start | bytes 7077896 | tf_op jit(solution)/shard_map/ppermute | solution.py:752
  3.0 29.6 %collective-permute-start.4 = (bf16[1536,768]{1,0:T(8,128)(2,1)}, bf16[1536,768]{1,0:T(8,128)(2,1)S(1)}, u32[]{:S(2)}, u32[]{:S(2)}) collective-permute-start(bf16[1536,768]{1,0:T(8,128)(2,1)} %wdo_ref.1), channel_id=1, source_target_pairs={{0,1},{1,0},{2,3},{3,2},{4,5},{5,4},{6,7},{7,6},{8,9},{9,8},{10,11... | collective-permute-start | bytes 7077896 | tf_op jit(solution)/shard_map/ppermute | solution.py:752
  3.4 0.7 copy-start
  4.1 0.7 copy-start.1
  42.1 10.2 %collective-permute-start.6 = (bf16[2,768,768]{2,1,0:T(8,128)(2,1)}, bf16[2,768,768]{2,1,0:T(8,128)(2,1)}, u32[]{:S(2)}, u32[]{:S(2)}) collective-permute-start(bf16[2,768,768]{2,1,0:T(8,128)(2,1)} %get-tuple-element.148), channel_id=1, source_target_pairs={{0,1},{1,0},{2,3},{3,2},{4,5},{5,4},{6,7},{7,6},{8,9},{9,8},{10,11... | collective-permute-start | bytes 7077896 | tf_op jit(solution)/shard_map/ppermute | solution.py:752
  51.8 13.2 %collective-permute-start.7 = (bf16[2,768,768]{2,1,0:T(8,128)(2,1)}, bf16[2,768,768]{2,1,0:T(8,128)(2,1)}, u32[]{:S(2)}, u32[]{:S(2)}) collective-permute-start(bf16[2,768,768]{2,1,0:T(8,128)(2,1)} %get-tuple-element.153), channel_id=1, source_target_pairs={{0,1},{1,0},{2,3},{3,2},{4,5},{5,4},{6,7},{7,6},{8,9},{9,8},{10,11... | collective-permute-start | bytes 7077896 | tf_op jit(solution)/shard_map/ppermute | solution.py:752
  62.4 24.9 %collective-permute-start.9 = (bf16[768,768]{1,0:T(8,128)(2,1)S(1)}, bf16[768,768]{1,0:T(8,128)(2,1)S(1)}, u32[]{:S(2)}, u32[]{:S(2)}) collective-permute-start(bf16[768,768]{1,0:T(8,128)(2,1)S(1)} %get-tuple-element.170), channel_id=1, source_target_pairs={{0,2},{1,5},{2,0},{3,7},{4,6},{5,1},{6,4},{7,3},{8,10},{9,13},{10,... | collective-permute-start | bytes 3538952 | tf_op jit(solution)/shard_map/ppermute | solution.py:701
  75.5 30.7 %collective-permute-start.8 = (bf16[768,768]{1,0:T(8,128)(2,1)S(1)}, bf16[768,768]{1,0:T(8,128)(2,1)S(1)}, u32[]{:S(2)}, u32[]{:S(2)}) collective-permute-start(bf16[768,768]{1,0:T(8,128)(2,1)S(1)} %get-tuple-element.157), channel_id=1, source_target_pairs={{0,2},{1,5},{2,0},{3,7},{4,6},{5,1},{6,4},{7,3},{8,10},{9,13},{10,... | collective-permute-start | bytes 3538952 | tf_op jit(solution)/shard_map/ppermute | solution.py:701
  88.4 19.1 %collective-permute-start.11 = (bf16[384,768]{1,0:T(8,128)(2,1)S(1)}, bf16[384,768]{1,0:T(8,128)(2,1)S(1)}, u32[]{:S(2)}, u32[]{:S(2)}) collective-permute-start(bf16[384,768]{1,0:T(8,128)(2,1)S(1)} %get-tuple-element.177), channel_id=1, source_target_pairs={{0,4},{1,3},{2,6},{3,1},{4,0},{5,7},{6,2},{7,5},{8,12},{9,11},{10,... | collective-permute-start | bytes 1769480 | tf_op jit(solution)/shard_map/ppermute | solution.py:701
  107.3 34.5 %collective-permute-start.10 = (bf16[384,768]{1,0:T(8,128)(2,1)S(1)}, bf16[384,768]{1,0:T(8,128)(2,1)S(1)}, u32[]{:S(2)}, u32[]{:S(2)}) collective-permute-start(bf16[384,768]{1,0:T(8,128)(2,1)S(1)} %get-tuple-element.175), channel_id=1, source_target_pairs={{0,4},{1,3},{2,6},{3,1},{4,0},{5,7},{6,2},{7,5},{8,12},{9,11},{10,... | collective-permute-start | bytes 1769480 | tf_op jit(solution)/shard_map/ppermute | solution.py:701
  107.4 16.6 %collective-permute-start.13 = (bf16[1536,768]{1,0:T(8,128)(2,1)S(1)}, bf16[1536,768]{1,0:T(8,128)(2,1)S(1)}, u32[]{:S(2)}, u32[]{:S(2)}) collective-permute-start(bf16[1536,768]{1,0:T(8,128)(2,1)S(1)} %get-tuple-element.187), channel_id=1, source_target_pairs={{0,1},{1,0},{2,3},{3,2},{4,5},{5,4},{6,7},{7,6},{8,9},{9,8},{10,11... | collective-permute-start | bytes 7077896 | tf_op jit(solution)/shard_map/ppermute | solution.py:752
  125.7 27.6 %collective-permute-start.16 = (bf16[768,768]{1,0:T(8,128)(2,1)S(1)}, bf16[768,768]{1,0:T(8,128)(2,1)S(1)}, u32[]{:S(2)}, u32[]{:S(2)}) collective-permute-start(bf16[768,768]{1,0:T(8,128)(2,1)S(1)} %get-tuple-element.196), channel_id=1, source_target_pairs={{0,2},{1,5},{2,0},{3,7},{4,6},{5,1},{6,4},{7,3},{8,10},{9,13},{10,... | collective-permute-start | bytes 3538952 | tf_op jit(solution)/shard_map/ppermute | solution.py:701
  127.6 9.6 %collective-permute-start.12 = (bf16[192,768]{1,0:T(8,128)(2,1)S(1)}, bf16[192,768]{1,0:T(8,128)(2,1)S(1)}, u32[]{:S(2)}, u32[]{:S(2)}) collective-permute-start(bf16[192,768]{1,0:T(8,128)(2,1)S(1)} %get-tuple-element.180), channel_id=1, source_target_pairs={{0,8},{1,25},{2,10},{3,27},{4,12},{5,29},{6,14},{7,31},{8,0},{9,17... | collective-permute-start | bytes 884744 | tf_op jit(solution)/shard_map/ppermute | solution.py:701
  137.8 16.6 %collective-permute-start.15 = (bf16[96,768]{1,0:T(8,128)(2,1)S(1)}, bf16[96,768]{1,0:T(8,128)(2,1)S(1)}, u32[]{:S(2)}, u32[]{:S(2)}) collective-permute-start(bf16[96,768]{1,0:T(8,128)(2,1)S(1)} %get-tuple-element.194), channel_id=1, source_target_pairs={{0,24},{1,9},{2,26},{3,11},{4,28},{5,13},{6,30},{7,15},{8,16},{9,1... | collective-permute-start | bytes 442376 | tf_op jit(solution)/shard_map/ppermute | solution.py:701
  142.7 14.0 %collective-permute-start.14 = (bf16[192,768]{1,0:T(8,128)(2,1)S(1)}, bf16[192,768]{1,0:T(8,128)(2,1)S(1)}, u32[]{:S(2)}, u32[]{:S(2)}) collective-permute-start(bf16[192,768]{1,0:T(8,128)(2,1)S(1)} %get-tuple-element.192), channel_id=1, source_target_pairs={{0,8},{1,25},{2,10},{3,27},{4,12},{5,29},{6,14},{7,31},{8,0},{9,17... | collective-permute-start | bytes 884744 | tf_op jit(solution)/shard_map/ppermute | solution.py:701
  153.2 13.6 %collective-permute-start.20 = (f32[4,32,768]{2,1,0:T(8,128)S(1)}, f32[4,32,768]{2,1,0:T(8,128)S(1)}, u32[]{:S(2)}, u32[]{:S(2)}) collective-permute-start(f32[4,32,768]{2,1,0:T(8,128)S(1)} %get-tuple-element.217.mine_ref), channel_id=1, source_target_pairs={{0,1},{1,0},{2,3},{3,2},{4,5},{5,4},{6,7},{7,6},{8,9},{9,8},{10,11... | collective-permute-start | bytes 1179656 | tf_op jit(solution)/shard_map/ppermute | solution.py:752
  154.5 13.2 %collective-permute-start.19 = (bf16[96,768]{1,0:T(8,128)(2,1)S(1)}, bf16[96,768]{1,0:T(8,128)(2,1)S(1)}, u32[]{:S(2)}, u32[]{:S(2)}) collective-permute-start(bf16[96,768]{1,0:T(8,128)(2,1)S(1)} %get-tuple-element.216.mine_ref), channel_id=1, source_target_pairs={{0,24},{1,9},{2,26},{3,11},{4,28},{5,13},{6,30},{7,15},{8,16},{9,1... | collective-permute-start | bytes 442376 | tf_op jit(solution)/shard_map/ppermute | solution.py:701
  155.1 27.5 %collective-permute-start.17 = (bf16[384,768]{1,0:T(8,128)(2,1)S(1)}, bf16[384,768]{1,0:T(8,128)(2,1)S(1)}, u32[]{:S(2)}, u32[]{:S(2)}) collective-permute-start(bf16[384,768]{1,0:T(8,128)(2,1)S(1)} %get-tuple-element.213), channel_id=1, source_target_pairs={{0,4},{1,3},{2,6},{3,1},{4,0},{5,7},{6,2},{7,5},{8,12},{9,11},{10,... | collective-permute-start | bytes 1769480 | tf_op jit(solution)/shard_map/ppermute | solution.py:701
  168.3 15.2 %collective-permute-start.23 = (bf16[192,768]{1,0:T(8,128)(2,1)S(1)}, bf16[192,768]{1,0:T(8,128)(2,1)S(1)}, u32[]{:S(2)}, u32[]{:S(2)}) collective-permute-start(bf16[192,768]{1,0:T(8,128)(2,1)S(1)} %bitcast.60), channel_id=1, source_target_pairs={{0,8},{1,25},{2,10},{3,27},{4,12},{5,29},{6,14},{7,31},{8,0},{9,17... | collective-permute-start | bytes 884744 | tf_op jit(solution)/shard_map/ppermute | solution.py:701
  169.9 12.7 %collective-permute-start.18 = (bf16[96,768]{1,0:T(8,128)(2,1)S(1)}, bf16[96,768]{1,0:T(8,128)(2,1)S(1)}, u32[]{:S(2)}, u32[]{:S(2)}) collective-permute-start(bf16[96,768]{1,0:T(8,128)(2,1)S(1)} %get-tuple-element.215), channel_id=1, source_target_pairs={{0,24},{1,9},{2,26},{3,11},{4,28},{5,13},{6,30},{7,15},{8,16},{9,1... | collective-permute-start | bytes 442376 | tf_op jit(solution)/shard_map/ppermute | solution.py:701
  172.7 10.8 %collective-permute-start.24 = (f32[2,768]{1,0:T(2,128)S(1)}, f32[2,768]{1,0:T(2,128)S(1)}, u32[]{:S(2)}, u32[]{:S(2)}) collective-permute-start(f32[2,768]{1,0:T(2,128)S(1)} %pad_maximum_fusion.a_ref), channel_id=1, source_target_pairs={{0,1},{1,0},{2,3},{3,2},{4,5},{5,4},{6,7},{7,6},{8,9},{9,8},{10,11... | collective-permute-start | bytes 18440 | tf_op jit(solution)/shard_map/ppermute | solution.py:752
  184.2 12.4 %collective-permute-start.27 = (bf16[384,768]{1,0:T(8,128)(2,1)S(1)}, bf16[384,768]{1,0:T(8,128)(2,1)S(1)}, u32[]{:S(2)}, u32[]{:S(2)}) collective-permute-start(bf16[384,768]{1,0:T(8,128)(2,1)S(1)} %bitcast.50), channel_id=1, source_target_pairs={{0,4},{1,3},{2,6},{3,1},{4,0},{5,7},{6,2},{7,5},{8,12},{9,11},{10,... | collective-permute-start | bytes 1769480 | tf_op jit(solution)/shard_map/ppermute | solution.py:701
  185.8 10.2 %collective-permute-start.21 = (bf16[192,768]{1,0:T(8,128)(2,1)S(1)}, bf16[192,768]{1,0:T(8,128)(2,1)S(1)}, u32[]{:S(2)}, u32[]{:S(2)}) collective-permute-start(bf16[192,768]{1,0:T(8,128)(2,1)S(1)} %get-tuple-element.223), channel_id=1, source_target_pairs={{0,8},{1,25},{2,10},{3,27},{4,12},{5,29},{6,14},{7,31},{8,0},{9,17... | collective-permute-start | bytes 884744 | tf_op jit(solution)/shard_map/ppermute | solution.py:701
  185.8 9.6 %collective-permute-start.22 = (bf16[96,768]{1,0:T(8,128)(2,1)S(1)}, bf16[96,768]{1,0:T(8,128)(2,1)S(1)}, u32[]{:S(2)}, u32[]{:S(2)}) collective-permute-start(bf16[96,768]{1,0:T(8,128)(2,1)S(1)} %get-tuple-element.224.mine_ref), channel_id=1, source_target_pairs={{0,24},{1,9},{2,26},{3,11},{4,28},{5,13},{6,30},{7,15},{8,16},{9,1... | collective-permute-start | bytes 442376 | tf_op jit(solution)/shard_map/ppermute | solution.py:701
  186.2 10.4 %collective-permute-start.28 = (f32[2,768]{1,0:T(2,128)S(1)}, f32[2,768]{1,0:T(2,128)S(1)}, u32[]{:S(2)}, u32[]{:S(2)}) collective-permute-start(f32[2,768]{1,0:T(2,128)S(1)} %get-tuple-element.236.a_ref), channel_id=1, source_target_pairs={{0,2},{1,5},{2,0},{3,7},{4,6},{5,1},{6,4},{7,3},{8,10},{9,13},{10,... | collective-permute-start | bytes 18440 | tf_op jit(solution)/shard_map/ppermute | solution.py:701
  197.5 21.4 %collective-permute-start.31 = (bf16[768,768]{1,0:T(8,128)(2,1)S(1)}, bf16[768,768]{1,0:T(8,128)(2,1)S(1)}, u32[]{:S(2)}, u32[]{:S(2)}) collective-permute-start(bf16[768,768]{1,0:T(8,128)(2,1)S(1)} %bitcast.70), channel_id=1, source_target_pairs={{0,2},{1,5},{2,0},{3,7},{4,6},{5,1},{6,4},{7,3},{8,10},{9,13},{10,... | collective-permute-start | bytes 3538952 | tf_op jit(solution)/shard_map/ppermute | solution.py:701
  197.9 9.5 %collective-permute-start.26 = (bf16[192,768]{1,0:T(8,128)(2,1)S(1)}, bf16[192,768]{1,0:T(8,128)(2,1)S(1)}, u32[]{:S(2)}, u32[]{:S(2)}) collective-permute-start(bf16[192,768]{1,0:T(8,128)(2,1)S(1)} %bitcast.63), channel_id=1, source_target_pairs={{0,8},{1,25},{2,10},{3,27},{4,12},{5,29},{6,14},{7,31},{8,0},{9,17... | collective-permute-start | bytes 884744 | tf_op jit(solution)/shard_map/ppermute | solution.py:701
  208.1 13.8 %collective-permute-start.30 = (bf16[384,768]{1,0:T(8,128)(2,1)S(1)}, bf16[384,768]{1,0:T(8,128)(2,1)S(1)}, u32[]{:S(2)}, u32[]{:S(2)}) collective-permute-start(bf16[384,768]{1,0:T(8,128)(2,1)S(1)} %bitcast.52), channel_id=1, source_target_pairs={{0,4},{1,3},{2,6},{3,1},{4,0},{5,7},{6,2},{7,5},{8,12},{9,11},{10,... | collective-permute-start | bytes 1769480 | tf_op jit(solution)/shard_map/ppermute | solution.py:701
  208.5 6.9 %collective-permute-start.25 = (bf16[96,768]{1,0:T(8,128)(2,1)S(1)}, bf16[96,768]{1,0:T(8,128)(2,1)S(1)}, u32[]{:S(2)}, u32[]{:S(2)}) collective-permute-start(bf16[96,768]{1,0:T(8,128)(2,1)S(1)} %get-tuple-element.233), channel_id=1, source_target_pairs={{0,24},{1,9},{2,26},{3,11},{4,28},{5,13},{6,30},{7,15},{8,16},{9,1... | collective-permute-start | bytes 442376 | tf_op jit(solution)/shard_map/ppermute | solution.py:701
  210.6 7.5 %collective-permute-start.32 = (f32[2,768]{1,0:T(2,128)S(1)}, f32[2,768]{1,0:T(2,128)S(1)}, u32[]{:S(2)}, u32[]{:S(2)}) collective-permute-start(f32[2,768]{1,0:T(2,128)S(1)} %get-tuple-element.244.a_ref), channel_id=1, source_target_pairs={{0,4},{1,3},{2,6},{3,1},{4,0},{5,7},{6,2},{7,5},{8,12},{9,11},{10,... | collective-permute-start | bytes 18440 | tf_op jit(solution)/shard_map/ppermute | solution.py:701
  222.8 17.7 %collective-permute-start.34 = (bf16[768,768]{1,0:T(8,128)(2,1)S(1)}, bf16[768,768]{1,0:T(8,128)(2,1)S(1)}, u32[]{:S(2)}, u32[]{:S(2)}) collective-permute-start(bf16[768,768]{1,0:T(8,128)(2,1)S(1)} %bitcast.44), channel_id=1, source_target_pairs={{0,2},{1,5},{2,0},{3,7},{4,6},{5,1},{6,4},{7,3},{8,10},{9,13},{10,... | collective-permute-start | bytes 3538952 | tf_op jit(solution)/shard_map/ppermute | solution.py:701
  223.3 8.3 %collective-permute-start.29 = (bf16[96,768]{1,0:T(8,128)(2,1)S(1)}, bf16[96,768]{1,0:T(8,128)(2,1)S(1)}, u32[]{:S(2)}, u32[]{:S(2)}) collective-permute-start(bf16[96,768]{1,0:T(8,128)(2,1)S(1)} %get-tuple-element.241.mine_ref), channel_id=1, source_target_pairs={{0,24},{1,9},{2,26},{3,11},{4,28},{5,13},{6,30},{7,15},{8,16},{9,1... | collective-permute-start | bytes 442376 | tf_op jit(solution)/shard_map/ppermute | solution.py:701
  232.2 11.4 %collective-permute-start.33 = (bf16[192,768]{1,0:T(8,128)(2,1)S(1)}, bf16[192,768]{1,0:T(8,128)(2,1)S(1)}, u32[]{:S(2)}, u32[]{:S(2)}) collective-permute-start(bf16[192,768]{1,0:T(8,128)(2,1)S(1)} %bitcast.66), channel_id=1, source_target_pairs={{0,8},{1,25},{2,10},{3,27},{4,12},{5,29},{6,14},{7,31},{8,0},{9,17... | collective-permute-start | bytes 884744 | tf_op jit(solution)/shard_map/ppermute | solution.py:701
  232.2 8.2 %collective-permute-start.35 = (f32[2,768]{1,0:T(2,128)S(1)}, f32[2,768]{1,0:T(2,128)S(1)}, u32[]{:S(2)}, u32[]{:S(2)}) collective-permute-start(f32[2,768]{1,0:T(2,128)S(1)} %get-tuple-element.253.a_ref), channel_id=1, source_target_pairs={{0,8},{1,25},{2,10},{3,27},{4,12},{5,29},{6,14},{7,31},{8,0},{9,17... | collective-permute-start | bytes 18440 | tf_op jit(solution)/shard_map/ppermute | solution.py:701
  244.3 9.9 %collective-permute-start.36 = (bf16[384,768]{1,0:T(8,128)(2,1)S(1)}, bf16[384,768]{1,0:T(8,128)(2,1)S(1)}, u32[]{:S(2)}, u32[]{:S(2)}) collective-permute-start(bf16[384,768]{1,0:T(8,128)(2,1)S(1)} %bitcast.56), channel_id=1, source_target_pairs={{0,4},{1,3},{2,6},{3,1},{4,0},{5,7},{6,2},{7,5},{8,12},{9,11},{10,... | collective-permute-start | bytes 1769480 | tf_op jit(solution)/shard_map/ppermute | solution.py:701
  245.8 5.5 %collective-permute-start.37 = (f32[2,768]{1,0:T(2,128)S(1)}, f32[2,768]{1,0:T(2,128)S(1)}, u32[]{:S(2)}, u32[]{:S(2)}) collective-permute-start(f32[2,768]{1,0:T(2,128)S(1)} %get-tuple-element.258.a_ref), channel_id=1, source_target_pairs={{0,24},{1,9},{2,26},{3,11},{4,28},{5,13},{6,30},{7,15},{8,16},{9,1... | collective-permute-start | bytes 18440 | tf_op jit(solution)/shard_map/ppermute | solution.py:701
  255.0 16.3 %collective-permute-start.38 = (bf16[768,768]{1,0:T(8,128)(2,1)S(1)}, bf16[768,768]{1,0:T(8,128)(2,1)S(1)}, u32[]{:S(2)}, u32[]{:S(2)}) collective-permute-start(bf16[768,768]{1,0:T(8,128)(2,1)S(1)} %bitcast.72), channel_id=1, source_target_pairs={{0,2},{1,5},{2,0},{3,7},{4,6},{5,1},{6,4},{7,3},{8,10},{9,13},{10,... | collective-permute-start | bytes 3538952 | tf_op jit(solution)/shard_map/ppermute | solution.py:701

commit v2 on v1

--- a/solution.py
+++ b/solution.py
@@ -333,7 +333,7 @@
         ],
         out_specs=[row, row, whole((1, width)), MARK_SPEC],
         compiler_params=params(22),
-        cost_estimate=cost(9),
+        cost_estimate=cost(0.1),
         name="norm_back",
     )(*streamed(cot, middle, gain_ffn), wu_oth, *streamed(wu_own, *dis), *after)
 
@@ -360,14 +360,21 @@
         ],
         out_specs=[row, MARK_SPEC],
         compiler_params=params(18),
-        cost_estimate=cost(8),
+        cost_estimate=cost(0.1),
         name="block_out",
     )(*streamed(middle), wd_oth, *streamed(wd_own, *acts), *after)
 
 
-def stack_halves(grad):
-    half = grad.shape[0] // 2
-    return jnp.concatenate([grad[:half], grad[half:]], axis=1)
+def stack(grad):
+    part = grad.shape[1]
+    return jnp.concatenate([grad[at : at + part] for at in range(0, grad.shape[0], part)], axis=1)
+
+
+def unstack_to(ref, at, stacked):
+    part = stacked.shape[0]
+    for block in range(stacked.shape[1] // part):
+        rows = slice(block * part, (block + 1) * part)
+        ref[rows, at : at + part] = stacked[:, rows].astype(F32)
 
 
 def attn_back_kernel(
@@ -416,22 +423,25 @@
     def _():
         inner = awo.shape[0]
         grad_ref[:inner] = awo[...].astype(BF)
-        grad_ref[inner : 2 * inner] = stack_halves(aw[:, :inner].astype(BF))
+        grad_ref[inner : 2 * inner] = stack(aw[:, :inner].astype(BF))
         rest = (aw[:, inner:] + mm(selall_ref[...], slots[...], TN)).astype(BF)
-        grad_ref[2 * inner : 3 * inner] = stack_halves(rest[:, :inner])
-        grad_ref[3 * inner :] = stack_halves(rest[:, inner:])
-
-
-def attn_back(gmb, xn, sel, wo, kept, us, after=()):
+        grad_ref[2 * inner : 3 * inner] = stack(rest[:, :inner])
+        grad_ref[3 * inner :] = stack(rest[:, inner:])
+
+
+def attn_back(gmb, xn, sel, wo, kept, at, inner, us, after=()):
     rows, width = gmb.shape
-    seqs, heads, keys, length = kept[3].shape
-    inner = wo.shape[0]
-    row, head, key = rows_of(length, width), rows_of(length, inner), seq_of(keys, inner)
+    seqs, _, keys, length = kept[3].shape
+    heads = inner // HDIM
+    block = at // inner
+    row = rows_of(length, width)
+    head_in = pl.BlockSpec((length, inner), lambda s: (s, block))
+    key_in = pl.BlockSpec((1, keys, inner), lambda s: (s, 0, block))
     grads = sds((4 * inner, width), BF)
     outs = [
-        (stored((rows, inner), BF), head),
-        (stored((seqs, keys, inner), BF), key),
-        (stored((seqs, keys, inner), BF), key),
+        (stored((rows, inner), BF), rows_of(length, inner)),
+        (stored((seqs, keys, inner), BF), seq_of(keys, inner)),
+        (stored((seqs, keys, inner), BF), seq_of(keys, inner)),
         (grads, whole(grads.shape)),
         (MARK, MARK_SPEC),
     ]
@@ -440,8 +450,11 @@
         grid=(seqs,),
         out_shape=[o[0] for o in outs],
         in_specs=[
-            row, row, whole((seqs * SLOT_ROWS, width)), whole((inner, width)),
-            head, key, key, seq_of(heads, keys, length), head, *[ANYWHERE] * len(after),
+            row, row, whole((seqs * SLOT_ROWS, width)),
+            pl.BlockSpec((inner, width), lambda s: (block, 0)),
+            head_in, key_in, key_in,
+            pl.BlockSpec((1, heads, keys, length), lambda s: (s, block, 0, 0)),
+            head_in, *[ANYWHERE] * len(after),
         ],
         out_specs=[o[1] for o in outs],
         scratch_shapes=[
@@ -456,9 +469,13 @@
 
 
 def input_back_kernel(
-    x_ref, gm_ref, gain_ref, hot_ref, wqo, wqt, wko, wkt, wvo, wvt,
-    dqo, dqt, dko, dkt, dvo, dvt, *refs,
+    parts, x_ref, gm_ref, gain_ref, hot_ref, wqo, wqt, wko, wkt, wvo, wvt,
+    *refs,
 ):
+    grads, refs = refs[: 3 * parts], refs[3 * parts :]
+    dq = jnp.concatenate([g[...] for g in grads[:parts]], axis=1)
+    dk = jnp.concatenate([g[0] for g in grads[parts : 2 * parts]], axis=1)
+    dv = jnp.concatenate([g[0] for g in grads[2 * parts :]], axis=1)
     wq, wk, wv = refs[-3:]
     gx_ref, gp_ref, gg_ref = marked(refs[:-3])[-3:]
     first = pl.program_id(0) == 0
@@ -471,9 +488,8 @@
             cat[:, :inner] = own[...]
             cat[:, inner:] = oth[...]
 
-    dkeys = mm(jnp.concatenate([dko[0], dkt[0]], axis=1), wk[...], NT)
-    dkeys += mm(jnp.concatenate([dvo[0], dvt[0]], axis=1), wv[...], NT)
-    dxn = dkeys[:length] + mm(jnp.concatenate([dqo[...], dqt[...]], axis=1), wq[...], NT)
+    dkeys = mm(dk, wk[...], NT) + mm(dv, wv[...], NT)
+    dxn = dkeys[:length] + mm(dq, wq[...], NT)
     x = x_ref[...].astype(F32)
     factor = lax.rsqrt(jnp.mean(x * x, axis=-1, keepdims=True) + EPS)
     scaled = x * factor
@@ -485,14 +501,15 @@
     gp_ref[0] = mm(hot_ref[0], dkeys[length:].astype(BF))
 
 
-def input_back(tokens, gm, gain_attn, hot, own, oth, d_own, d_oth, after=()):
+def input_back(tokens, gm, gain_attn, hot, own, oth, grads, after=()):
     rows, width = tokens.shape
-    seqs, keys, inner = d_own[1].shape
+    seqs, keys = grads[0][1].shape[:2]
     length = rows // seqs
-    pool_rows = hot.shape[1]
-    row, head, key = rows_of(length, width), rows_of(length, inner), seq_of(keys, inner)
-    return pl.pallas_call(
-        input_back_kernel,
+    pool_rows, inner = hot.shape[1], own[0].shape[1]
+    row = rows_of(length, width)
+    flat = [g[kind] for kind in range(3) for g in grads]
+    return pl.pallas_call(
+        functools.partial(input_back_kernel, len(grads)),
         grid=(seqs,),
         out_shape=[
             stored((rows, width), F32),
@@ -502,17 +519,20 @@
         ],
         in_specs=[
             row, row, whole((width,)), seq_of(pool_rows, SLOT_ROWS),
-            *[whole((width, inner))] * 6, head, head, key, key, key, key, *[ANYWHERE] * len(after),
+            *[whole((width, inner))] * 6,
+            *[rows_of(length, g[0].shape[1]) for g in grads],
+            *[seq_of(keys, g[0].shape[1]) for g in [*grads, *grads]],
+            *[ANYWHERE] * len(after),
         ],
         out_specs=[row, seq_of(pool_rows, width), whole((1, width)), MARK_SPEC],
         scratch_shapes=[pltpu.VMEM((width, 2 * inner), BF)] * 3,
         compiler_params=params(22),
-        cost_estimate=cost(8),
+        cost_estimate=cost(0.1),
         name="input_back",
     )(
-        *streamed(tokens, gm, gain_attn), *streamed(hot),
+        *streamed(tokens, gm, gain_attn, hot),
         *[w for pair in zip(streamed(*own[:3]), oth[:3]) for w in pair],
-        *streamed(d_own[0], d_oth[0], d_own[1], d_oth[1], d_own[2], d_oth[2]), *after,
+        *streamed(*flat), *after,
     )
 
 
@@ -547,6 +567,35 @@
         cost_estimate=cost(0.05),
         name="halve",
     )(sides, a.reshape(2, rows, width), b.reshape(2, rows, width), *after)
+
+
+def open_kernel(sides_ref, *refs):
+    keep_ref, send_ref = marked(refs)[-2:]
+    upper = sides_ref[0] == 1
+    at = 0
+    for own_ref, got_ref in zip(refs[::2], refs[1::2]):
+        if len(own_ref.shape) != 3 or at == keep_ref.shape[0]:
+            break
+        rows = own_ref.shape[1]
+        low, high = bf_sum(own_ref[0], got_ref[0]), bf_sum(own_ref[1], got_ref[1])
+        keep_ref[at : at + rows] = jnp.where(upper, high, low)
+        send_ref[at : at + rows] = jnp.where(upper, low, high)
+        at += rows
+
+
+def open_sums(sides, owns, gots, after=()):
+    width = owns[0].shape[1]
+    arrays = [a.reshape(2, -1, width) for pair in zip(owns, gots) for a in pair]
+    rows = sum(o.shape[0] for o in owns) // 2
+    return pl.pallas_call(
+        open_kernel,
+        out_shape=[sds((rows, width), BF)] * 2 + [MARK],
+        in_specs=[IN_SMEM, *[whole(a.shape) for a in arrays], *[ANYWHERE] * len(after)],
+        out_specs=[whole((rows, width))] * 2 + [MARK_SPEC],
+        compiler_params=params(14),
+        cost_estimate=cost(0.05),
+        name="open_sums",
+    )(sides, *arrays, *after)
 
 
 def add_kernel(a_ref, b_ref, *refs):
@@ -639,27 +688,29 @@
         ],
         input_output_aliases={3 + at: at for at in range(len(before))},
         compiler_params=params(10),
-        cost_estimate=cost(2),
+        cost_estimate=cost(0.05),
         name="ffn_finish",
     )(sides, mine, got, *before, *after)
 
 
-def attn_finish_kernel(sides_ref, mine_ref, got_ref, *refs):
+def attn_finish_kernel(parts, sides_ref, mine_ref, got_ref, *refs):
     wq_ref, wk_ref, wv_ref, wo_ref = refs[-4:]
-    inner = wo_ref.shape[0]
     low, high = joined(0, sides_ref, mine_ref[...], got_ref[...])
-    wo_ref[...] = low[:inner].astype(F32)
-    for ref, stacked in ((wq_ref, low[inner:]), (wk_ref, high[:inner]), (wv_ref, high[inner:])):
-        ref[:inner] = stacked[:, :inner].astype(F32)
-        ref[inner:] = stacked[:, inner:].astype(F32)
-
-
-def attn_finish(sides, mine, got, after=()):
+    at = column = 0
+    for part in parts:
+        wo_ref[column : column + part] = low[at : at + part].astype(F32)
+        unstack_to(wq_ref, column, low[at + part : at + 2 * part])
+        unstack_to(wk_ref, column, high[at : at + part])
+        unstack_to(wv_ref, column, high[at + part : at + 2 * part])
+        at, column = at + 2 * part, column + part
+
+
+def attn_finish(parts, sides, mine, got, after=()):
     rows, width = mine.shape
     inner = rows // 2
     full = whole(mine.shape)
     return pl.pallas_call(
-        attn_finish_kernel,
+        functools.partial(attn_finish_kernel, parts),
         out_shape=[stored((width, inner), F32)] * 3 + [stored((inner, width), F32)],
         in_specs=[IN_SMEM, full, full, *[ANYWHERE] * len(after)],
         out_specs=[whole((width, inner))] * 3 + [whole((inner, width))],
@@ -739,6 +790,10 @@
         if not self.done:
             self.got = self.chips.exchange(self.at, self.mine)
         return [mark]
+
+
+def arrived(groups):
+    return [g.got for g in groups]
 
 
 def body(
@@ -779,37 +834,57 @@
     acts, dis = sum(acts, []), sum(dis, [])
     gm, gmb, gg_ffn, mark = norm_back(cotangent, middle, gain_ffn, wu_oth, w_up, dis, mark)
     mark = ffn[0].step([mark])
-    *d_oth, a_oth, mark = attn_back(gmb, xn, sel, oth[3], second, 1, mark)
-    a_got = core_swap(a_oth)
-    mark = ffn[0].step(ffn[1].step([mark]))
-    *d_own, a_own, mark = attn_back(gmb, xn, sel, *streamed(w_out), first, 30, mark)
-    attn = Group(chips, a_own, a_got)
-    mark = ffn[1].step(ffn[0].step(attn.step([mark])))
+    parts, starts = (256, 128), (0, 256)
+    assert sum(parts) == w_out.shape[0]
+    d_own, d_oth, a_own, a_got = [], [], [], []
+    for at, part in zip(starts, parts):
+        *d, grad, mark = attn_back(gmb, xn, sel, oth[3], second, at, part, 0.1, mark)
+        d_oth.append(d)
+        a_got.append(core_swap(grad))
+        mark = ffn[1].step(ffn[0].step([mark, *arrived(ffn)]))
+    for at, part in zip(starts, parts):
+        *d, grad, mark = attn_back(
+            gmb, xn, sel, *streamed(w_out), first, at, part, 22, mark
+        )
+        d_own.append(d)
+        a_own.append(grad)
+        if len(a_own) < len(parts):
+            mark = ffn[1].step(ffn[0].step([mark, *arrived(ffn)]))
+    keep, send, mark = open_sums(chips.sides, a_own, a_got, [mark, *arrived(ffn)])
+    attn = Group(chips, keep, chips.exchange(0, send), 1)
+    mark = ffn[1].step(ffn[0].step([mark]))
     grad_tokens, grad_pool, gg_attn, mark = input_back(
-        tokens, gm, gain_attn, hot, own, oth, d_own, d_oth, mark
+        tokens, gm, gain_attn, hot, own, oth, [*d_own, *d_oth], mark
     )
     pool_got = core_swap(grad_pool)
     gains = jnp.concatenate([gg_attn, gg_ffn], axis=0)
     gains = Small(chips, gains, core_swap(gains))
-    mark = ffn[1].step(ffn[0].step(attn.step([mark])))
+    mark = gains.step(ffn[1].step(ffn[0].step(attn.step([mark, *arrived(ffn)]))))
     block_out, mark = block_output(middle, wd_oth, w_down, acts, mark)
     grad_value_pool, mark = pool_join(grad_pool, pool_got, [mark])
     mark = [mark]
+    last = 2 * chips.levels
     ready = []
-    while not attn.done or len(ready) < count or not gains.done:
-        for at in range(count):
-            if not ffn[at].done:
-                mark = ffn[at].step(mark)
-            elif len(ready) == at:
-                out = ffn_finish(at, count, chips.sides, ffn[at].mine, ffn[at].got, ready[-1] if ready else (), mark)
-                ready.append(out[:2])
-                mark = [out[2]]
-        if not attn.done:
-            mark = attn.step(mark)
+    late = [0] * count
+    while attn.at < last or not gains.done:
+        waited = [g for g, l in zip(ffn, late) if g.at < last or l == 1]
+        late = [l + (g.at == last) for g, l in zip(ffn, late)]
+        if attn.at < last:
+            mark = attn.step([*mark, *arrived([*waited, *([] if gains.done else [gains])])])
+        for group in ffn:
+            if group.at < last:
+                mark = group.step(mark)
         if not gains.done:
             mark = gains.step(mark)
+    while len(ready) < count:
+        at = len(ready)
+        *out, mark = ffn_finish(
+            at, count, chips.sides, ffn[at].mine, ffn[at].got, ready[-1] if ready else (), mark
+        )
+        ready.append(out)
+        mark = [mark]
     grad_wd, grad_wu = ready[-1]
-    grad_wq, grad_wk, grad_wv, grad_wo = attn_finish(chips.sides, attn.mine, attn.got, mark)
+    grad_wq, grad_wk, grad_wv, grad_wo = attn_finish(parts, chips.sides, attn.mine, attn.got, mark)
     return (
         block_out, grad_tokens, grad_wq, grad_wk, grad_wv, grad_wo, grad_wu, grad_wd,
         gains.mine[0], gains.mine[1], grad_value_pool,

time: 275 us -> 261 us (0.949)
  waiting for transfers between devices: 72.5 us -> 49.7 us
  Pallas kernels: 156 us -> 166 us
    ppermute x28, waiting for transfers between devices: 71.6 us -> 48 us  [exchange(): return lax.ppermute(array, ('dp', 'mp'), self.pairs[level])]
    pallas_call x2 -> x4, Pallas kernels: 31.4 us -> 42.4 us  [attn_back(): pl.pallas_call(attn_back_kernel, grid=(seqs,), out_shape=[o[0] for o in o...]
    ppermute x28, starting transfers between devices: 39.7 us -> 35.7 us  [exchange(): return lax.ppermute(array, ('dp', 'mp'), self.pairs[level])]
    pallas_call x10 -> x9, Pallas kernels: 9.42 us -> 7.8 us  [halve(): pl.pallas_call(functools.partial(halve_kernel, level), grid=(steps,), out...]
    pallas_call x2 -> x3, Pallas kernels: 13.4 us -> 14.4 us  [the longest x1 10.2 us: input_back(): pl.pallas_call(functools.partial(input_back_kernel, len(grads)), grid=(se...]
  transfers between devices with their start and end apart: 39 -> 40, of which waited for: 13 -> 10; matrix products, arithmetic and copies ran while one was open for 0% -> 0% of each run, Pallas kernels for 51% -> 55%
where the time goes in v2:
time: 261 us; the launch traced here: 260 us
  Pallas kernels  166 us (64%)
  waiting for transfers between devices  49.7 us (19%)
  starting transfers between devices  40.7 us (16%)
    ppermute x28, waiting for transfers between devices, exchange(): return lax.ppermute(array, ('dp', 'mp'), self.pairs[level])  48 us
    pallas_call x4, Pallas kernels, attn_back(): pl.pallas_call(attn_back_kernel, grid=(seqs,), out_shape=[o[0] for o in o...  42.4 us
    pallas_call x4, Pallas kernels, ffn_part(): pl.pallas_call(functools.partial(ffn_kernel, own, 256), grid=(steps,), ou...  40 us
    ppermute x28, starting transfers between devices, exchange(): return lax.ppermute(array, ('dp', 'mp'), self.pairs[level])  35.7 us
    pallas_call x1, Pallas kernels, attention_forward(): pl.pallas_call(attn_second_kernel, grid=(seqs,), out_shape=[o[0] for o in...  14.8 us
    pallas_call x1, Pallas kernels, attention_forward(): pl.pallas_call(attn_first_kernel, grid_spec=pltpu.PrefetchScalarGridSpec(...  13 us
    pallas_call x1, Pallas kernels, norm_back(): pl.pallas_call(norm_back_kernel, grid=(rows // block,), out_shape=[stored...  11.1 us
    pallas_call x1, Pallas kernels, input_back(): pl.pallas_call(functools.partial(input_back_kernel, len(grads)), grid=(se...  10.2 us
  transfers between devices with their start and end apart: 40, of which 10 were waited for; matrix products, arithmetic and copies ran while one was open for 0% of the time, Pallas kernels for 55%

profile of v2, /device:TPU:0, one launch (start us, length us, event | category | flops | bytes accessed | tf_op | source)
XLA Modules:
  0.0 260.0 jit_solution(2747557607401132788)
XLA Ops:
  2.2 0.9 collective-permute-done.wq_ref.wqt
  4.8 13.0 %attn_first.1 = (bf16[1024,768]{1,0:T(8,128)(2,1)}, bf16[4,32,768]{2,1,0:T(8,128)(2,1)}, f32[4,288,1]{2,1,0:T(8,128)}, bf16[4,32,32]{2,1,0:T(8,128)(2,1)}, bf16[...) custom-call(s32[1]{0:T(128)} %bitcast.first_ref, ...), custom_call_target="tpu_custom_call" | custom-call | flops 13799999488 | tf_op jit(solution)/shard_map/attn_first/pallas_call | solution.py:179
  17.8 14.8 %attn_second.1 = (bf16[1024,384]{1,0:T(8,128)(2,1)}, bf16[4,288,384]{2,1,0:T(8,128)(2,1)}, bf16[4,288,384]{2,1,0:T(8,128)(2,1)}, bf16[4,6,288,256]{3,2,1,0:T(8,1...) custom-call(bf16[1024,768]{1,0:T(8,128)(2,1)} %x_ref.5, f32[768]{0:T(1024)} %gain_ref.6, ...), custom_call_target="tpu_custom_call" | custom-call | flops 13799999488 | tf_op jit(solution)/shard_map/attn_second/pallas_call | solution.py:203
  32.6 10.2 %ffn_part.4 = (bf16[1024,768]{1,0:T(8,128)(2,1)}, bf16[1024,768]{1,0:T(8,128)(2,1)}, bf16[2,768,768]{2,1,0:T(8,128)(2,1)}, f32[8,128]{1,0:T(8,128)S(1)}) custom-call(bf16[1024,768]{1,0:T(8,128)(2,1)} %get-tuple-element.156.nf_ref, bf16[1024,768]{1,0:T(8,128)(2,1)} %cot_ref.9, bf16[768,1536]{1,0:T(8,128)(2,1)S(1)} %collective-permute-done.5.wu_ref.wut_ref, ...), custom_call_target="tpu_custom_call" | custom-call | flops 11500000256 | tf_op jit(solution)/shard_map/ffn_part/pallas_call | solution.py:283
  43.0 9.4 %ffn_part.5 = (bf16[1024,768]{1,0:T(8,128)(2,1)}, bf16[1024,768]{1,0:T(8,128)(2,1)}, bf16[2,768,768]{2,1,0:T(8,128)(2,1)}, f32[8,128]{1,0:T(8,128)S(1)}) custom-call(bf16[1024,768]{1,0:T(8,128)(2,1)} %get-tuple-element.156.nf_ref, bf16[1024,768]{1,0:T(8,128)(2,1)} %cot_ref.9, bf16[768,1536]{1,0:T(8,128)(2,1)S(1)} %collective-permute-done.5.wu_ref.wut_ref, ...), custom_call_target="tpu_custom_call" | custom-call | flops 11500000256 | tf_op jit(solution)/shard_map/ffn_part/pallas_call | solution.py:283
  52.9 10.1 %ffn_part.6 = (bf16[1024,768]{1,0:T(8,128)(2,1)}, bf16[1024,768]{1,0:T(8,128)(2,1)}, bf16[768,768]{1,0:T(8,128)(2,1)S(1)}, bf16[768,768]{1,0:T(8,128)(2,1)S(1)}, f32[8,128]{1,0:T(8,128)S(1)}) custom-call(bf16[1024,768]{1,0:T(8,128)(2,1)} %get-tuple-element.156.nf_ref, bf16[1024,768]{1,0:T(8,128)(2,1)} %cot_ref.9, bf16[768,1536]{1,0:T(8,128)(2,1)} %wuo_ref.1, ...), custom_call_target="tpu_custom_call" | custom-call | flops 11500000256 | tf_op jit(solution)/shard_map/ffn_part/pallas_call | solution.py:283
  62.9 2.6 %collective-permute-start.9 = (bf16[768,768]{1,0:T(8,128)(2,1)S(1)}, bf16[768,768]{1,0:T(8,128)(2,1)S(1)}, u32[]{:S(2)}, u32[]{:S(2)}) collective-permute-start(bf16[768,768]{1,0:T(8,128)(2,1)S(1)} %get-tuple-element.181), channel_id=1, source_target_pairs={{0,2},{1,5},{2,0},{3,7},{4,6},{5,1},{6,4},{7,3},{8,10},{9,13},{10,... | collective-permute-start | bytes 3538952 | tf_op jit(solution)/shard_map/ppermute | solution.py:752
  65.6 10.3 %ffn_part.7 = (bf16[1024,768]{1,0:T(8,128)(2,1)}, bf16[1024,768]{1,0:T(8,128)(2,1)}, bf16[768,768]{1,0:T(8,128)(2,1)S(1)}, bf16[768,768]{1,0:T(8,128)(2,1)S(1)}, f32[8,128]{1,0:T(8,128)S(1)}) custom-call(bf16[1024,768]{1,0:T(8,128)(2,1)} %get-tuple-element.156.nf_ref, bf16[1024,768]{1,0:T(8,128)(2,1)} %cot_ref.9, bf16[768,1536]{1,0:T(8,128)(2,1)} %wuo_ref.1, ...), custom_call_target="tpu_custom_call" | custom-call | flops 11500000256 | tf_op jit(solution)/shard_map/ffn_part/pallas_call | solution.py:283
  75.9 11.1 %norm_back.1 = (f32[1024,768]{1,0:T(8,128)}, bf16[1024,768]{1,0:T(8,128)(2,1)}, f32[1,768]{1,0:T(1,128)S(1)}, f32[8,128]{1,0:T(8,128)S(1)}) custom-call(bf16[1024,768]{1,0:T(8,128)(2,1)} %cot_ref.9, f32[1024,768]{1,0:T(8,128)} %get-tuple-element.155.middle_ref, f32[768]{0:T(1024)} %gain_ref.6, bf16[768,1536]{1,0:T(8,128)(2,1)S(1)} %collective-permute-done.5.wu_ref.wut_ref, ...), custom_call_target="tpu_custom_call" | custom-call | flops 115000000 | tf_op jit(solution)/shard_map/norm_back/pallas_call | solution.py:326
  87.0 1.1 halve.9
  88.2 2.1 collective-permute-start.10
  90.3 12.3 %attn_back.4 = (bf16[1024,256]{1,0:T(8,128)(2,1)}, bf16[4,288,256]{2,1,0:T(8,128)(2,1)}, bf16[4,288,256]{2,1,0:T(8,128)(2,1)}, bf16[1024,768]{1,0:T(8,128)(2,1)S(1)}, f32[8,128]{1,0:T(8,128)S(1)}) custom-call(bf16[1024,768]{1,0:T(8,128)(2,1)} %get-tuple-element.173.gm_ref, bf16[1024,768]{1,0:T(8,128)(2,1)} %get-tuple-element.151.xn_ref, ...), custom_call_target="tpu_custom_call" | custom-call | flops 115000000 | tf_op jit(solution)/shard_map/attn_back/pallas_call | solution.py:448
  103.5 1.1 halve.11
  104.7 2.1 collective-permute-start.12
  106.8 1.0 collective-permute-start.17
  107.8 8.8 %attn_back.5 = (bf16[1024,128]{1,0:T(8,128)(2,1)}, bf16[4,288,128]{2,1,0:T(8,128)(2,1)}, bf16[4,288,128]{2,1,0:T(8,128)(2,1)}, bf16[512,768]{1,0:T(8,128)(2,1)S(1)}, f32[8,128]{1,0:T(8,128)S(1)}) custom-call(bf16[1024,768]{1,0:T(8,128)(2,1)} %get-tuple-element.173.gm_ref, bf16[1024,768]{1,0:T(8,128)(2,1)} %get-tuple-element.151.xn_ref, ...), custom_call_target="tpu_custom_call" | custom-call | flops 115000000 | tf_op jit(solution)/shard_map/attn_back/pallas_call | solution.py:448
  117.3 2.0 collective-permute-start.14
  120.9 12.4 %attn_back.6 = (bf16[1024,256]{1,0:T(8,128)(2,1)}, bf16[4,288,256]{2,1,0:T(8,128)(2,1)}, bf16[4,288,256]{2,1,0:T(8,128)(2,1)}, bf16[1024,768]{1,0:T(8,128)(2,1)S(1)}, f32[8,128]{1,0:T(8,128)S(1)}) custom-call(bf16[1024,768]{1,0:T(8,128)(2,1)} %get-tuple-element.173.gm_ref, bf16[1024,768]{1,0:T(8,128)(2,1)} %get-tuple-element.151.xn_ref, ...), custom_call_target="tpu_custom_call" | custom-call | flops 25300000768 | tf_op jit(solution)/shard_map/attn_back/pallas_call | solution.py:448
  134.0 1.3 collective-permute-start.15
  135.3 2.6 collective-permute-start.16
  137.9 8.8 %attn_back.7 = (bf16[1024,128]{1,0:T(8,128)(2,1)}, bf16[4,288,128]{2,1,0:T(8,128)(2,1)}, bf16[4,288,128]{2,1,0:T(8,128)(2,1)}, bf16[512,768]{1,0:T(8,128)(2,1)S(1)}, f32[8,128]{1,0:T(8,128)S(1)}) custom-call(bf16[1024,768]{1,0:T(8,128)(2,1)} %get-tuple-element.173.gm_ref, bf16[1024,768]{1,0:T(8,128)(2,1)} %get-tuple-element.151.xn_ref, ...), custom_call_target="tpu_custom_call" | custom-call | flops 25300000768 | tf_op jit(solution)/shard_map/attn_back/pallas_call | solution.py:448
  146.7 1.3 open_sums.1
  148.0 1.6 collective-permute-start.22
  150.3 1.5 collective-permute-start.20
  151.7 10.2 %input_back.1 = (f32[1024,768]{1,0:T(8,128)}, f32[4,32,768]{2,1,0:T(8,128)S(1)}, f32[1,768]{1,0:T(1,128)S(1)}, f32[8,128]{1,0:T(8,128)S(1)}) custom-call(bf16[1024,768]{1,0:T(8,128)(2,1)} %x_ref.5, f32[1024,768]{1,0:T(8,128)} %get-tuple-element.171.gm_ref, f32[768]{0:T(1024)} %gain_ref.7, bf16[4,32,32]{2,1,0:T(8,128)(2,1)} %get-tuple-element.172.hot_ref, ...), custom_call_target="tpu_custom_call" | custom-call | flops 115000000 | tf_op jit(solution)/shard_map/input_back/pallas_call | solution.py:511
  162.0 2.3 collective-permute-done.22
  164.3 1.1 halve.15
  166.1 1.6 collective-permute-start.25
  168.9 1.5 collective-permute-start.19
  171.2 1.5 collective-permute-start.27
  172.7 9.5 %block_out.1 = (bf16[1024,768]{1,0:T(8,128)(2,1)}, f32[8,128]{1,0:T(8,128)S(1)}) custom-call(f32[1024,768]{1,0:T(8,128)} %get-tuple-element.155.middle_ref, bf16[1536,768]{1,0:T(8,128)(2,1)S(1)} %copy-done.1, bf16[1536,768]{1,0:T(8,128)(2,1)} %wdo_ref.1, bf16[1024,768]{1,0:T(8,128)(2,1)} %get-tuple-element.157.a0t, ...), custom_call_target="tpu_custom_call" | custom-call | flops 115000000 | tf_op jit(solution)/shard_map/block_out/pallas_call | solution.py:354
  182.2 1.0 pool_join.1
  185.5 1.6 collective-permute-start.29
  187.1 0.9 collective-permute-start.28
  189.0 10.3 %collective-permute-done.30.refs_2_.b_ref = f32[2,768]{1,0:T(2,128)S(1)} collective-permute-done((f32[2,768]{1,0:T(2,128)S(1)}, f32[2,768]{1,0:T(2,128)S(1)}, u32[]{:S(2)}, u32[]{:S(2)}) %collective-permute-start.30) | collective-permute-done | bytes 6176 | tf_op jit(solution)/shard_map/ppermute | solution.py:752
  200.8 1.1 collective-permute-start.35
  201.9 3.5 %collective-permute-start.31 = (bf16[96,768]{1,0:T(8,128)(2,1)S(1)}, bf16[96,768]{1,0:T(8,128)(2,1)S(1)}, u32[]{:S(2)}, u32[]{:S(2)}) collective-permute-start(bf16[96,768]{1,0:T(8,128)(2,1)S(1)} %get-tuple-element.261), channel_id=1, source_target_pairs={{0,24},{1,9},{2,26},{3,11},{4,28},{5,13},{6,30},{7,15},{8,16},{9,1... | collective-permute-start | bytes 442376 | tf_op jit(solution)/shard_map/ppermute | solution.py:752
  205.4 3.6 %collective-permute-done.33.refs_2_.b_ref = f32[2,768]{1,0:T(2,128)S(1)} collective-permute-done((f32[2,768]{1,0:T(2,128)S(1)}, f32[2,768]{1,0:T(2,128)S(1)}, u32[]{:S(2)}, u32[]{:S(2)}) %collective-permute-start.33) | collective-permute-done | bytes 6176 | tf_op jit(solution)/shard_map/ppermute | solution.py:752
  209.1 3.4 %collective-permute-start.34 = (bf16[96,768]{1,0:T(8,128)(2,1)S(1)}, bf16[96,768]{1,0:T(8,128)(2,1)S(1)}, u32[]{:S(2)}, u32[]{:S(2)}) collective-permute-start(bf16[96,768]{1,0:T(8,128)(2,1)S(1)} %get-tuple-element.267.mine_ref), channel_id=1, source_target_pairs={{0,24},{1,9},{2,26},{3,11},{4,28},{5,13},{6,30},{7,15},{8,16},{9,1... | collective-permute-start | bytes 442376 | tf_op jit(solution)/shard_map/ppermute | solution.py:752
  213.0 4.9 %collective-permute-done.36.refs_2_.b_ref = f32[2,768]{1,0:T(2,128)S(1)} collective-permute-done((f32[2,768]{1,0:T(2,128)S(1)}, f32[2,768]{1,0:T(2,128)S(1)}, u32[]{:S(2)}, u32[]{:S(2)}) %collective-permute-start.36) | collective-permute-done | bytes 6176 | tf_op jit(solution)/shard_map/ppermute | solution.py:752
  217.9 2.0 collective-permute-done.35.refs_1_.got_ref
  221.3 7.6 %collective-permute-done.37.got_ref = bf16[192,768]{1,0:T(8,128)(2,1)S(1)} collective-permute-done((bf16[192,768]{1,0:T(8,128)(2,1)S(1)}, bf16[192,768]{1,0:T(8,128)(2,1)S(1)}, u32[]{:S(2)}, u32[]{:S(2)}) %collective-permute-start.37) | collective-permute-done | bytes 294944 | tf_op jit(solution)/shard_map/ppermute | solution.py:752
  229.7 9.9 %collective-permute-done.38.got_ref = bf16[384,768]{1,0:T(8,128)(2,1)S(1)} collective-permute-done((bf16[384,768]{1,0:T(8,128)(2,1)S(1)}, bf16[384,768]{1,0:T(8,128)(2,1)S(1)}, u32[]{:S(2)}, u32[]{:S(2)}) %collective-permute-start.38) | collective-permute-done | bytes 589856 | tf_op jit(solution)/shard_map/ppermute | solution.py:752
  240.3 2.5 collective-permute-start.39
  243.4 3.1 %ffn_finish.2 = (f32[1536,768]{1,0:T(8,128)}, f32[768,1536]{1,0:T(8,128)}, f32[8,128]{1,0:T(8,128)S(1)}) custom-call(s32[4]{0:T(128)S(1)} %broadcast_select_fusion.refs_1_.sides_ref, bf16[768,768]{1,0:T(8,128)(2,1)S(1)} %bitcast.46, bf16[768,768]{1,0:T(8,128)(2,1)S(1)} %collective-permute-done.32.refs_1_.got_ref, f32[8,128]{1,0:T(8,128)S(1)} %get-tuple-element.278.refs_0_), custom_call_target="tpu_custom_call" | custom-call | flops 57500000 | tf_op jit(solution)/shard_map/ffn_finish/pallas_call | solution.py:679
  246.5 3.1 %ffn_finish.3 = (f32[1536,768]{1,0:T(8,128)}, f32[768,1536]{1,0:T(8,128)}, f32[8,128]{1,0:T(8,128)S(1)}) custom-call(s32[4]{0:T(128)S(1)} %broadcast_select_fusion.refs_1_.sides_ref, bf16[768,768]{1,0:T(8,128)(2,1)S(1)} %bitcast.52, bf16[768,768]{1,0:T(8,128)(2,1)S(1)} %collective-permute-done.35.refs_1_.got_ref, ...), custom_call_target="tpu_custom_call", output_to_operand_aliasing={{0}: (3, {}), {1}: (4, {})} | custom-call | flops 57500000 | tf_op jit(solution)/shard_map/ffn_finish/pallas_call | solution.py:679
  249.6 7.4 %collective-permute-done.39.got_ref = bf16[768,768]{1,0:T(8,128)(2,1)S(1)} collective-permute-done((bf16[768,768]{1,0:T(8,128)(2,1)S(1)}, bf16[768,768]{1,0:T(8,128)(2,1)S(1)}, u32[]{:S(2)}, u32[]{:S(2)}) %collective-permute-start.39) | collective-permute-done | bytes 1179680 | tf_op jit(solution)/shard_map/ppermute | solution.py:752
  257.0 2.9 %attn_finish.1 = (f32[768,384]{1,0:T(8,128)}, f32[768,384]{1,0:T(8,128)}, f32[768,384]{1,0:T(8,128)}, f32[384,768]{1,0:T(8,128)}) custom-call(s32[4]{0:T(128)S(1)} %broadcast_select_fusion.refs_1_.sides_ref, bf16[768,768]{1,0:T(8,128)(2,1)S(1)} %bitcast.77, bf16[768,768]{1,0:T(8,128)(2,1)S(1)} %collective-permute-done.39.got_ref, ...), custom_call_target="tpu_custom_call" | custom-call | flops 2300000000 | tf_op jit(solution)/shard_map/attn_finish/pallas_call | solution.py:712
  (87 shorter events, 20.0 us)
Async XLA Ops:
  0.6 2.4 collective-permute-start
  1.2 16.6 %collective-permute-start.1 = (bf16[768,384]{1,0:T(8,128)(2,1)}, bf16[768,384]{1,0:T(8,128)(2,1)}, u32[]{:S(2)}, u32[]{:S(2)}) collective-permute-start(bf16[768,384]{1,0:T(8,128)(2,1)} %wko.1), channel_id=1, source_target_pairs={{0,1},{1,0},{2,3},{3,2},{4,5},{5,4},{6,7},{7,6},{8,9},{9,8},{10,11... | collective-permute-start | bytes 1769480 | tf_op jit(solution)/shard_map/ppermute | solution.py:807
  1.2 16.6 %collective-permute-start.2 = (bf16[768,384]{1,0:T(8,128)(2,1)}, bf16[768,384]{1,0:T(8,128)(2,1)}, u32[]{:S(2)}, u32[]{:S(2)}) collective-permute-start(bf16[768,384]{1,0:T(8,128)(2,1)} %wvo.1), channel_id=1, source_target_pairs={{0,1},{1,0},{2,3},{3,2},{4,5},{5,4},{6,7},{7,6},{8,9},{9,8},{10,11... | collective-permute-start | bytes 1769480 | tf_op jit(solution)/shard_map/ppermute | solution.py:807
  1.7 16.1 %collective-permute-start.3 = (bf16[384,768]{1,0:T(8,128)(2,1)}, bf16[384,768]{1,0:T(8,128)(2,1)S(1)}, u32[]{:S(2)}, u32[]{:S(2)}) collective-permute-start(bf16[384,768]{1,0:T(8,128)(2,1)} %wo_ref.3), channel_id=1, source_target_pairs={{0,1},{1,0},{2,3},{3,2},{4,5},{5,4},{6,7},{7,6},{8,9},{9,8},{10,11... | collective-permute-start | bytes 1769480 | tf_op jit(solution)/shard_map/ppermute | solution.py:807
  1.8 30.8 %collective-permute-start.5 = (bf16[768,1536]{1,0:T(8,128)(2,1)}, bf16[768,1536]{1,0:T(8,128)(2,1)S(1)}, u32[]{:S(2)}, u32[]{:S(2)}) collective-permute-start(bf16[768,1536]{1,0:T(8,128)(2,1)} %wuo_ref.1), channel_id=1, source_target_pairs={{0,1},{1,0},{2,3},{3,2},{4,5},{5,4},{6,7},{7,6},{8,9},{9,8},{10,11... | collective-permute-start | bytes 7077896 | tf_op jit(solution)/shard_map/ppermute | solution.py:807
  3.0 29.6 %collective-permute-start.4 = (bf16[1536,768]{1,0:T(8,128)(2,1)}, bf16[1536,768]{1,0:T(8,128)(2,1)S(1)}, u32[]{:S(2)}, u32[]{:S(2)}) collective-permute-start(bf16[1536,768]{1,0:T(8,128)(2,1)} %wdo_ref.1), channel_id=1, source_target_pairs={{0,1},{1,0},{2,3},{3,2},{4,5},{5,4},{6,7},{7,6},{8,9},{9,8},{10,11... | collective-permute-start | bytes 7077896 | tf_op jit(solution)/shard_map/ppermute | solution.py:807
  3.4 0.7 copy-start.2
  4.1 0.7 copy-start.3
  32.6 10.4 %copy-start = (bf16[1536,768]{1,0:T(8,128)(2,1)}, bf16[1536,768]{1,0:T(8,128)(2,1)S(1)}, u32[]{:S(2)}) copy-start(bf16[1536,768]{1,0:T(8,128)(2,1)S(1)} %collective-permute-done.4.wd_ref.wdt_ref) | copy-start | bytes 7077892
  42.9 10.0 %collective-permute-start.6 = (bf16[2,768,768]{2,1,0:T(8,128)(2,1)}, bf16[2,768,768]{2,1,0:T(8,128)(2,1)}, u32[]{:S(2)}, u32[]{:S(2)}) collective-permute-start(bf16[2,768,768]{2,1,0:T(8,128)(2,1)} %get-tuple-element.158), channel_id=1, source_target_pairs={{0,1},{1,0},{2,3},{3,2},{4,5},{5,4},{6,7},{7,6},{8,9},{9,8},{10,11... | collective-permute-start | bytes 7077896 | tf_op jit(solution)/shard_map/ppermute | solution.py:807
  52.4 13.2 %collective-permute-start.7 = (bf16[2,768,768]{2,1,0:T(8,128)(2,1)}, bf16[2,768,768]{2,1,0:T(8,128)(2,1)}, u32[]{:S(2)}, u32[]{:S(2)}) collective-permute-start(bf16[2,768,768]{2,1,0:T(8,128)(2,1)} %get-tuple-element.163), channel_id=1, source_target_pairs={{0,1},{1,0},{2,3},{3,2},{4,5},{5,4},{6,7},{7,6},{8,9},{9,8},{10,11... | collective-permute-start | bytes 7077896 | tf_op jit(solution)/shard_map/ppermute | solution.py:807
  62.9 24.1 %collective-permute-start.9 = (bf16[768,768]{1,0:T(8,128)(2,1)S(1)}, bf16[768,768]{1,0:T(8,128)(2,1)S(1)}, u32[]{:S(2)}, u32[]{:S(2)}) collective-permute-start(bf16[768,768]{1,0:T(8,128)(2,1)S(1)} %get-tuple-element.181), channel_id=1, source_target_pairs={{0,2},{1,5},{2,0},{3,7},{4,6},{5,1},{6,4},{7,3},{8,10},{9,13},{10,... | collective-permute-start | bytes 3538952 | tf_op jit(solution)/shard_map/ppermute | solution.py:752
  75.9 26.7 %collective-permute-start.8 = (bf16[768,768]{1,0:T(8,128)(2,1)S(1)}, bf16[768,768]{1,0:T(8,128)(2,1)S(1)}, u32[]{:S(2)}, u32[]{:S(2)}) collective-permute-start(bf16[768,768]{1,0:T(8,128)(2,1)S(1)} %get-tuple-element.179), channel_id=1, source_target_pairs={{0,2},{1,5},{2,0},{3,7},{4,6},{5,1},{6,4},{7,3},{8,10},{9,13},{10,... | collective-permute-start | bytes 3538952 | tf_op jit(solution)/shard_map/ppermute | solution.py:752
  88.2 14.4 %collective-permute-start.10 = (bf16[384,768]{1,0:T(8,128)(2,1)S(1)}, bf16[384,768]{1,0:T(8,128)(2,1)S(1)}, u32[]{:S(2)}, u32[]{:S(2)}) collective-permute-start(bf16[384,768]{1,0:T(8,128)(2,1)S(1)} %get-tuple-element.184), channel_id=1, source_target_pairs={{0,4},{1,3},{2,6},{3,1},{4,0},{5,7},{6,2},{7,5},{8,12},{9,11},{10,... | collective-permute-start | bytes 1769480 | tf_op jit(solution)/shard_map/ppermute | solution.py:752
  104.6 12.1 %collective-permute-start.11 = (bf16[384,768]{1,0:T(8,128)(2,1)S(1)}, bf16[384,768]{1,0:T(8,128)(2,1)S(1)}, u32[]{:S(2)}, u32[]{:S(2)}) collective-permute-start(bf16[384,768]{1,0:T(8,128)(2,1)S(1)} %get-tuple-element.194), channel_id=1, source_target_pairs={{0,4},{1,3},{2,6},{3,1},{4,0},{5,7},{6,2},{7,5},{8,12},{9,11},{10,... | collective-permute-start | bytes 1769480 | tf_op jit(solution)/shard_map/ppermute | solution.py:752
  104.7 12.0 %collective-permute-start.12 = (bf16[192,768]{1,0:T(8,128)(2,1)S(1)}, bf16[192,768]{1,0:T(8,128)(2,1)S(1)}, u32[]{:S(2)}, u32[]{:S(2)}) collective-permute-start(bf16[192,768]{1,0:T(8,128)(2,1)S(1)} %get-tuple-element.196), channel_id=1, source_target_pairs={{0,8},{1,25},{2,10},{3,27},{4,12},{5,29},{6,14},{7,31},{8,0},{9,17... | collective-permute-start | bytes 884744 | tf_op jit(solution)/shard_map/ppermute | solution.py:752
  106.8 39.9 %collective-permute-start.17 = (bf16[1024,768]{1,0:T(8,128)(2,1)S(1)}, bf16[1024,768]{1,0:T(8,128)(2,1)S(1)}, u32[]{:S(2)}, u32[]{:S(2)}) collective-permute-start(bf16[1024,768]{1,0:T(8,128)(2,1)S(1)} %get-tuple-element.224), channel_id=1, source_target_pairs={{0,1},{1,0},{2,3},{3,2},{4,5},{5,4},{6,7},{7,6},{8,9},{9,8},{10,11... | collective-permute-start | bytes 4718600 | tf_op jit(solution)/shard_map/ppermute | solution.py:807
  116.6 30.1 %collective-permute-start.18 = (bf16[512,768]{1,0:T(8,128)(2,1)S(1)}, bf16[512,768]{1,0:T(8,128)(2,1)S(1)}, u32[]{:S(2)}, u32[]{:S(2)}) collective-permute-start(bf16[512,768]{1,0:T(8,128)(2,1)S(1)} %get-tuple-element.226), channel_id=1, source_target_pairs={{0,1},{1,0},{2,3},{3,2},{4,5},{5,4},{6,7},{7,6},{8,9},{9,8},{10,11... | collective-permute-start | bytes 2359304 | tf_op jit(solution)/shard_map/ppermute | solution.py:807
  117.3 16.0 %collective-permute-start.14 = (bf16[96,768]{1,0:T(8,128)(2,1)S(1)}, bf16[96,768]{1,0:T(8,128)(2,1)S(1)}, u32[]{:S(2)}, u32[]{:S(2)}) collective-permute-start(bf16[96,768]{1,0:T(8,128)(2,1)S(1)} %get-tuple-element.205), channel_id=1, source_target_pairs={{0,24},{1,9},{2,26},{3,11},{4,28},{5,13},{6,30},{7,15},{8,16},{9,1... | collective-permute-start | bytes 442376 | tf_op jit(solution)/shard_map/ppermute | solution.py:752
  120.2 13.1 %collective-permute-start.13 = (bf16[192,768]{1,0:T(8,128)(2,1)S(1)}, bf16[192,768]{1,0:T(8,128)(2,1)S(1)}, u32[]{:S(2)}, u32[]{:S(2)}) collective-permute-start(bf16[192,768]{1,0:T(8,128)(2,1)S(1)} %get-tuple-element.203), channel_id=1, source_target_pairs={{0,8},{1,25},{2,10},{3,27},{4,12},{5,29},{6,14},{7,31},{8,0},{9,17... | collective-permute-start | bytes 884744 | tf_op jit(solution)/shard_map/ppermute | solution.py:752
  134.0 12.7 %collective-permute-start.15 = (bf16[96,768]{1,0:T(8,128)(2,1)S(1)}, bf16[96,768]{1,0:T(8,128)(2,1)S(1)}, u32[]{:S(2)}, u32[]{:S(2)}) collective-permute-start(bf16[96,768]{1,0:T(8,128)(2,1)S(1)} %get-tuple-element.221), channel_id=1, source_target_pairs={{0,24},{1,9},{2,26},{3,11},{4,28},{5,13},{6,30},{7,15},{8,16},{9,1... | collective-permute-start | bytes 442376 | tf_op jit(solution)/shard_map/ppermute | solution.py:752
  135.3 11.4 %collective-permute-start.16 = (bf16[96,768]{1,0:T(8,128)(2,1)S(1)}, bf16[96,768]{1,0:T(8,128)(2,1)S(1)}, u32[]{:S(2)}, u32[]{:S(2)}) collective-permute-start(bf16[96,768]{1,0:T(8,128)(2,1)S(1)} %get-tuple-element.222.mine_ref), channel_id=1, source_target_pairs={{0,24},{1,9},{2,26},{3,11},{4,28},{5,13},{6,30},{7,15},{8,16},{9,1... | collective-permute-start | bytes 442376 | tf_op jit(solution)/shard_map/ppermute | solution.py:752
  148.0 16.3 %collective-permute-start.22 = (bf16[768,768]{1,0:T(8,128)(2,1)S(1)}, bf16[768,768]{1,0:T(8,128)(2,1)S(1)}, u32[]{:S(2)}, u32[]{:S(2)}) collective-permute-start(bf16[768,768]{1,0:T(8,128)(2,1)S(1)} %get-tuple-element.236), channel_id=1, source_target_pairs={{0,2},{1,5},{2,0},{3,7},{4,6},{5,1},{6,4},{7,3},{8,10},{9,13},{10,... | collective-permute-start | bytes 3538952 | tf_op jit(solution)/shard_map/ppermute | solution.py:752
  150.1 11.8 %collective-permute-start.21 = (bf16[192,768]{1,0:T(8,128)(2,1)S(1)}, bf16[192,768]{1,0:T(8,128)(2,1)S(1)}, u32[]{:S(2)}, u32[]{:S(2)}) collective-permute-start(bf16[192,768]{1,0:T(8,128)(2,1)S(1)} %bitcast.68), channel_id=1, source_target_pairs={{0,8},{1,25},{2,10},{3,27},{4,12},{5,29},{6,14},{7,31},{8,0},{9,17... | collective-permute-start | bytes 884744 | tf_op jit(solution)/shard_map/ppermute | solution.py:752
  150.3 11.7 %collective-permute-start.20 = (bf16[96,768]{1,0:T(8,128)(2,1)S(1)}, bf16[96,768]{1,0:T(8,128)(2,1)S(1)}, u32[]{:S(2)}, u32[]{:S(2)}) collective-permute-start(bf16[96,768]{1,0:T(8,128)(2,1)S(1)} %get-tuple-element.233.mine_ref), channel_id=1, source_target_pairs={{0,24},{1,9},{2,26},{3,11},{4,28},{5,13},{6,30},{7,15},{8,16},{9,1... | collective-permute-start | bytes 442376 | tf_op jit(solution)/shard_map/ppermute | solution.py:752
  164.3 8.4 %copy-start.1 = (bf16[1536,768]{1,0:T(8,128)(2,1)S(1)}, bf16[1536,768]{1,0:T(8,128)(2,1)}, u32[]{:S(2)}) copy-start(bf16[1536,768]{1,0:T(8,128)(2,1)} %copy-done) | copy-start | bytes 7077892
  166.1 17.0 %collective-permute-start.25 = (bf16[384,768]{1,0:T(8,128)(2,1)S(1)}, bf16[384,768]{1,0:T(8,128)(2,1)S(1)}, u32[]{:S(2)}, u32[]{:S(2)}) collective-permute-start(bf16[384,768]{1,0:T(8,128)(2,1)S(1)} %bitcast.57), channel_id=1, source_target_pairs={{0,4},{1,3},{2,6},{3,1},{4,0},{5,7},{6,2},{7,5},{8,12},{9,11},{10,... | collective-permute-start | bytes 1769480 | tf_op jit(solution)/shard_map/ppermute | solution.py:752
  167.7 15.4 %collective-permute-start.23 = (bf16[384,768]{1,0:T(8,128)(2,1)S(1)}, bf16[384,768]{1,0:T(8,128)(2,1)S(1)}, u32[]{:S(2)}, u32[]{:S(2)}) collective-permute-start(bf16[384,768]{1,0:T(8,128)(2,1)S(1)} %get-tuple-element.245), channel_id=1, source_target_pairs={{0,4},{1,3},{2,6},{3,1},{4,0},{5,7},{6,2},{7,5},{8,12},{9,11},{10,... | collective-permute-start | bytes 1769480 | tf_op jit(solution)/shard_map/ppermute | solution.py:752
  168.2 14.0 %collective-permute-start.24 = (f32[4,32,768]{2,1,0:T(8,128)S(1)}, f32[4,32,768]{2,1,0:T(8,128)S(1)}, u32[]{:S(2)}, u32[]{:S(2)}) collective-permute-start(f32[4,32,768]{2,1,0:T(8,128)S(1)} %get-tuple-element.246.mine_ref), channel_id=1, source_target_pairs={{0,1},{1,0},{2,3},{3,2},{4,5},{5,4},{6,7},{7,6},{8,9},{9,8},{10,11... | collective-permute-start | bytes 1179656 | tf_op jit(solution)/shard_map/ppermute | solution.py:807
  168.8 14.4 %collective-permute-start.26 = (bf16[192,768]{1,0:T(8,128)(2,1)S(1)}, bf16[192,768]{1,0:T(8,128)(2,1)S(1)}, u32[]{:S(2)}, u32[]{:S(2)}) collective-permute-start(bf16[192,768]{1,0:T(8,128)(2,1)S(1)} %bitcast.66), channel_id=1, source_target_pairs={{0,8},{1,25},{2,10},{3,27},{4,12},{5,29},{6,14},{7,31},{8,0},{9,17... | collective-permute-start | bytes 884744 | tf_op jit(solution)/shard_map/ppermute | solution.py:752
  168.9 2.4 collective-permute-start.19
  171.2 11.9 %collective-permute-start.27 = (f32[2,768]{1,0:T(2,128)S(1)}, f32[2,768]{1,0:T(2,128)S(1)}, u32[]{:S(2)}, u32[]{:S(2)}) collective-permute-start(f32[2,768]{1,0:T(2,128)S(1)} %get-tuple-element.251.a_ref), channel_id=1, source_target_pairs={{0,2},{1,5},{2,0},{3,7},{4,6},{5,1},{6,4},{7,3},{8,10},{9,13},{10,... | collective-permute-start | bytes 18440 | tf_op jit(solution)/shard_map/ppermute | solution.py:752
  185.5 13.8 %collective-permute-start.29 = (bf16[384,768]{1,0:T(8,128)(2,1)S(1)}, bf16[384,768]{1,0:T(8,128)(2,1)S(1)}, u32[]{:S(2)}, u32[]{:S(2)}) collective-permute-start(bf16[384,768]{1,0:T(8,128)(2,1)S(1)} %bitcast.60), channel_id=1, source_target_pairs={{0,4},{1,3},{2,6},{3,1},{4,0},{5,7},{6,2},{7,5},{8,12},{9,11},{10,... | collective-permute-start | bytes 1769480 | tf_op jit(solution)/shard_map/ppermute | solution.py:752
  187.1 12.2 %collective-permute-start.28 = (bf16[192,768]{1,0:T(8,128)(2,1)S(1)}, bf16[192,768]{1,0:T(8,128)(2,1)S(1)}, u32[]{:S(2)}, u32[]{:S(2)}) collective-permute-start(bf16[192,768]{1,0:T(8,128)(2,1)S(1)} %get-tuple-element.253), channel_id=1, source_target_pairs={{0,8},{1,25},{2,10},{3,27},{4,12},{5,29},{6,14},{7,31},{8,0},{9,17... | collective-permute-start | bytes 884744 | tf_op jit(solution)/shard_map/ppermute | solution.py:752
  188.0 21.0 %collective-permute-start.32 = (bf16[768,768]{1,0:T(8,128)(2,1)S(1)}, bf16[768,768]{1,0:T(8,128)(2,1)S(1)}, u32[]{:S(2)}, u32[]{:S(2)}) collective-permute-start(bf16[768,768]{1,0:T(8,128)(2,1)S(1)} %bitcast.45), channel_id=1, source_target_pairs={{0,2},{1,5},{2,0},{3,7},{4,6},{5,1},{6,4},{7,3},{8,10},{9,13},{10,... | collective-permute-start | bytes 3538952 | tf_op jit(solution)/shard_map/ppermute | solution.py:752
  188.6 10.7 %collective-permute-start.30 = (f32[2,768]{1,0:T(2,128)S(1)}, f32[2,768]{1,0:T(2,128)S(1)}, u32[]{:S(2)}, u32[]{:S(2)}) collective-permute-start(f32[2,768]{1,0:T(2,128)S(1)} %get-tuple-element.259.a_ref), channel_id=1, source_target_pairs={{0,4},{1,3},{2,6},{3,1},{4,0},{5,7},{6,2},{7,5},{8,12},{9,11},{10,... | collective-permute-start | bytes 18440 | tf_op jit(solution)/shard_map/ppermute | solution.py:752
  200.8 19.2 %collective-permute-start.35 = (bf16[768,768]{1,0:T(8,128)(2,1)S(1)}, bf16[768,768]{1,0:T(8,128)(2,1)S(1)}, u32[]{:S(2)}, u32[]{:S(2)}) collective-permute-start(bf16[768,768]{1,0:T(8,128)(2,1)S(1)} %bitcast.51), channel_id=1, source_target_pairs={{0,2},{1,5},{2,0},{3,7},{4,6},{5,1},{6,4},{7,3},{8,10},{9,13},{10,... | collective-permute-start | bytes 3538952 | tf_op jit(solution)/shard_map/ppermute | solution.py:752
  201.9 7.1 %collective-permute-start.31 = (bf16[96,768]{1,0:T(8,128)(2,1)S(1)}, bf16[96,768]{1,0:T(8,128)(2,1)S(1)}, u32[]{:S(2)}, u32[]{:S(2)}) collective-permute-start(bf16[96,768]{1,0:T(8,128)(2,1)S(1)} %get-tuple-element.261), channel_id=1, source_target_pairs={{0,24},{1,9},{2,26},{3,11},{4,28},{5,13},{6,30},{7,15},{8,16},{9,1... | collective-permute-start | bytes 442376 | tf_op jit(solution)/shard_map/ppermute | solution.py:752
  205.4 3.6 %collective-permute-start.33 = (f32[2,768]{1,0:T(2,128)S(1)}, f32[2,768]{1,0:T(2,128)S(1)}, u32[]{:S(2)}, u32[]{:S(2)}) collective-permute-start(f32[2,768]{1,0:T(2,128)S(1)} %get-tuple-element.266.a_ref), channel_id=1, source_target_pairs={{0,8},{1,25},{2,10},{3,27},{4,12},{5,29},{6,14},{7,31},{8,0},{9,17... | collective-permute-start | bytes 18440 | tf_op jit(solution)/shard_map/ppermute | solution.py:752
  209.1 8.8 %collective-permute-start.34 = (bf16[96,768]{1,0:T(8,128)(2,1)S(1)}, bf16[96,768]{1,0:T(8,128)(2,1)S(1)}, u32[]{:S(2)}, u32[]{:S(2)}) collective-permute-start(bf16[96,768]{1,0:T(8,128)(2,1)S(1)} %get-tuple-element.267.mine_ref), channel_id=1, source_target_pairs={{0,24},{1,9},{2,26},{3,11},{4,28},{5,13},{6,30},{7,15},{8,16},{9,1... | collective-permute-start | bytes 442376 | tf_op jit(solution)/shard_map/ppermute | solution.py:752
  212.4 5.4 %collective-permute-start.36 = (f32[2,768]{1,0:T(2,128)S(1)}, f32[2,768]{1,0:T(2,128)S(1)}, u32[]{:S(2)}, u32[]{:S(2)}) collective-permute-start(f32[2,768]{1,0:T(2,128)S(1)} %get-tuple-element.271.a_ref), channel_id=1, source_target_pairs={{0,24},{1,9},{2,26},{3,11},{4,28},{5,13},{6,30},{7,15},{8,16},{9,1... | collective-permute-start | bytes 18440 | tf_op jit(solution)/shard_map/ppermute | solution.py:752
  220.5 8.4 %collective-permute-start.37 = (bf16[192,768]{1,0:T(8,128)(2,1)S(1)}, bf16[192,768]{1,0:T(8,128)(2,1)S(1)}, u32[]{:S(2)}, u32[]{:S(2)}) collective-permute-start(bf16[192,768]{1,0:T(8,128)(2,1)S(1)} %bitcast.71), channel_id=1, source_target_pairs={{0,8},{1,25},{2,10},{3,27},{4,12},{5,29},{6,14},{7,31},{8,0},{9,17... | collective-permute-start | bytes 884744 | tf_op jit(solution)/shard_map/ppermute | solution.py:752
  229.6 9.9 %collective-permute-start.38 = (bf16[384,768]{1,0:T(8,128)(2,1)S(1)}, bf16[384,768]{1,0:T(8,128)(2,1)S(1)}, u32[]{:S(2)}, u32[]{:S(2)}) collective-permute-start(bf16[384,768]{1,0:T(8,128)(2,1)S(1)} %bitcast.62), channel_id=1, source_target_pairs={{0,4},{1,3},{2,6},{3,1},{4,0},{5,7},{6,2},{7,5},{8,12},{9,11},{10,... | collective-permute-start | bytes 1769480 | tf_op jit(solution)/shard_map/ppermute | solution.py:752
  240.3 16.7 %collective-permute-start.39 = (bf16[768,768]{1,0:T(8,128)(2,1)S(1)}, bf16[768,768]{1,0:T(8,128)(2,1)S(1)}, u32[]{:S(2)}, u32[]{:S(2)}) collective-permute-start(bf16[768,768]{1,0:T(8,128)(2,1)S(1)} %bitcast.76), channel_id=1, source_target_pairs={{0,2},{1,5},{2,0},{3,7},{4,6},{5,1},{6,4},{7,3},{8,10},{9,13},{10,... | collective-permute-start | bytes 3538952 | tf_op jit(solution)/shard_map/ppermute | solution.py:752

commit v3 on v2

--- a/solution.py
+++ b/solution.py
@@ -748,6 +748,15 @@
             for b in range(bits)
         ]
 
+        masks = [1 << b for b in range(bits)]
+        self.turns = [
+            [(d * mp + m, (d ^ mask) * mp + m) for d in range(dp) for m in range(mp)]
+            for mask in masks[:1] + masks[2:] + masks[1:2]
+        ]
+
+    def turn(self, at, array):
+        return lax.ppermute(array, ("dp", "mp"), self.turns[at])
+
     def exchange(self, level, array):
         return lax.ppermute(array, ("dp", "mp"), self.pairs[level])
 
@@ -788,7 +797,7 @@
         self.mine, mark = add(self.mine, self.got, after)
         self.at += 1
         if not self.done:
-            self.got = self.chips.exchange(self.at, self.mine)
+            self.got = self.chips.turn(self.at, self.mine)
         return [mark]
 
 

time: 261 us -> 260 us (level)
    ppermute x28 -> x24, waiting for transfers between devices: 48 us -> 33.7 us  [exchange(): return lax.ppermute(array, ('dp', 'mp'), self.pairs[level])]
    ppermute x0 -> x4, waiting for transfers between devices: none -> 13.9 us  [turn(): return lax.ppermute(array, ('dp', 'mp'), self.turns[at])]
    ppermute x28 -> x24, starting transfers between devices: 35.7 us -> 30.8 us  [exchange(): return lax.ppermute(array, ('dp', 'mp'), self.pairs[level])]
    ppermute x0 -> x4, starting transfers between devices: none -> 4.69 us  [turn(): return lax.ppermute(array, ('dp', 'mp'), self.turns[at])]
  transfers between devices with their start and end apart: 40 -> 40, of which waited for: 10 -> 12; matrix products, arithmetic and copies ran while one was open for 0% -> 0% of each run, Pallas kernels for 55% -> 55%
where the time goes in v3:
time: 260 us; the launch traced here: 259 us
  Pallas kernels  166 us (64%)
  waiting for transfers between devices  49.2 us (19%)
  starting transfers between devices  40.5 us (16%)
    pallas_call x4, Pallas kernels, attn_back(): pl.pallas_call(attn_back_kernel, grid=(seqs,), out_shape=[o[0] for o in o...  42.4 us
    pallas_call x4, Pallas kernels, ffn_part(): pl.pallas_call(functools.partial(ffn_kernel, own, 256), grid=(steps,), ou...  40 us
    ppermute x24, waiting for transfers between devices, exchange(): return lax.ppermute(array, ('dp', 'mp'), self.pairs[level])  33.7 us
    ppermute x24, starting transfers between devices, exchange(): return lax.ppermute(array, ('dp', 'mp'), self.pairs[level])  30.8 us
    pallas_call x1, Pallas kernels, attention_forward(): pl.pallas_call(attn_second_kernel, grid=(seqs,), out_shape=[o[0] for o in...  14.8 us
    ppermute x4, waiting for transfers between devices, turn(): return lax.ppermute(array, ('dp', 'mp'), self.turns[at])  13.9 us
    pallas_call x1, Pallas kernels, attention_forward(): pl.pallas_call(attn_first_kernel, grid_spec=pltpu.PrefetchScalarGridSpec(...  13 us
    pallas_call x1, Pallas kernels, norm_back(): pl.pallas_call(norm_back_kernel, grid=(rows // block,), out_shape=[stored...  11.1 us
  transfers between devices with their start and end apart: 40, of which 12 were waited for; matrix products, arithmetic and copies ran while one was open for 0% of the time, Pallas kernels for 55%

profile of v3, /device:TPU:0, one launch (start us, length us, event | category | flops | bytes accessed | tf_op | source)
XLA Modules:
  0.0 259.3 jit_solution(559806108939985042)
XLA Ops:
  4.8 13.0 %attn_first.1 = (bf16[1024,768]{1,0:T(8,128)(2,1)}, bf16[4,32,768]{2,1,0:T(8,128)(2,1)}, f32[4,288,1]{2,1,0:T(8,128)}, bf16[4,32,32]{2,1,0:T(8,128)(2,1)}, bf16[...) custom-call(s32[1]{0:T(128)} %bitcast.first_ref, ...), custom_call_target="tpu_custom_call" | custom-call | flops 13799999488 | tf_op jit(solution)/shard_map/attn_first/pallas_call | solution.py:179
  17.8 14.8 %attn_second.1 = (bf16[1024,384]{1,0:T(8,128)(2,1)}, bf16[4,288,384]{2,1,0:T(8,128)(2,1)}, bf16[4,288,384]{2,1,0:T(8,128)(2,1)}, bf16[4,6,288,256]{3,2,1,0:T(8,1...) custom-call(bf16[1024,768]{1,0:T(8,128)(2,1)} %x_ref.5, f32[768]{0:T(1024)} %gain_ref.6, ...), custom_call_target="tpu_custom_call" | custom-call | flops 13799999488 | tf_op jit(solution)/shard_map/attn_second/pallas_call | solution.py:203
  32.6 10.2 %ffn_part.4 = (bf16[1024,768]{1,0:T(8,128)(2,1)}, bf16[1024,768]{1,0:T(8,128)(2,1)}, bf16[2,768,768]{2,1,0:T(8,128)(2,1)}, f32[8,128]{1,0:T(8,128)S(1)}) custom-call(bf16[1024,768]{1,0:T(8,128)(2,1)} %get-tuple-element.156.nf_ref, bf16[1024,768]{1,0:T(8,128)(2,1)} %cot_ref.9, bf16[768,1536]{1,0:T(8,128)(2,1)S(1)} %collective-permute-done.5.wu_ref.wut_ref, ...), custom_call_target="tpu_custom_call" | custom-call | flops 11500000256 | tf_op jit(solution)/shard_map/ffn_part/pallas_call | solution.py:283
  43.0 9.4 %ffn_part.5 = (bf16[1024,768]{1,0:T(8,128)(2,1)}, bf16[1024,768]{1,0:T(8,128)(2,1)}, bf16[2,768,768]{2,1,0:T(8,128)(2,1)}, f32[8,128]{1,0:T(8,128)S(1)}) custom-call(bf16[1024,768]{1,0:T(8,128)(2,1)} %get-tuple-element.156.nf_ref, bf16[1024,768]{1,0:T(8,128)(2,1)} %cot_ref.9, bf16[768,1536]{1,0:T(8,128)(2,1)S(1)} %collective-permute-done.5.wu_ref.wut_ref, ...), custom_call_target="tpu_custom_call" | custom-call | flops 11500000256 | tf_op jit(solution)/shard_map/ffn_part/pallas_call | solution.py:283
  52.9 10.1 %ffn_part.6 = (bf16[1024,768]{1,0:T(8,128)(2,1)}, bf16[1024,768]{1,0:T(8,128)(2,1)}, bf16[768,768]{1,0:T(8,128)(2,1)S(1)}, bf16[768,768]{1,0:T(8,128)(2,1)S(1)}, f32[8,128]{1,0:T(8,128)S(1)}) custom-call(bf16[1024,768]{1,0:T(8,128)(2,1)} %get-tuple-element.156.nf_ref, bf16[1024,768]{1,0:T(8,128)(2,1)} %cot_ref.9, bf16[768,1536]{1,0:T(8,128)(2,1)} %wuo_ref.1, ...), custom_call_target="tpu_custom_call" | custom-call | flops 11500000256 | tf_op jit(solution)/shard_map/ffn_part/pallas_call | solution.py:283
  62.9 2.6 %collective-permute-start.9 = (bf16[768,768]{1,0:T(8,128)(2,1)S(1)}, bf16[768,768]{1,0:T(8,128)(2,1)S(1)}, u32[]{:S(2)}, u32[]{:S(2)}) collective-permute-start(bf16[768,768]{1,0:T(8,128)(2,1)S(1)} %get-tuple-element.181), channel_id=1, source_target_pairs={{0,2},{1,5},{2,0},{3,7},{4,6},{5,1},{6,4},{7,3},{8,10},{9,13},{10,... | collective-permute-start | bytes 3538952 | tf_op jit(solution)/shard_map/ppermute | solution.py:761
  65.6 10.3 %ffn_part.7 = (bf16[1024,768]{1,0:T(8,128)(2,1)}, bf16[1024,768]{1,0:T(8,128)(2,1)}, bf16[768,768]{1,0:T(8,128)(2,1)S(1)}, bf16[768,768]{1,0:T(8,128)(2,1)S(1)}, f32[8,128]{1,0:T(8,128)S(1)}) custom-call(bf16[1024,768]{1,0:T(8,128)(2,1)} %get-tuple-element.156.nf_ref, bf16[1024,768]{1,0:T(8,128)(2,1)} %cot_ref.9, bf16[768,1536]{1,0:T(8,128)(2,1)} %wuo_ref.1, ...), custom_call_target="tpu_custom_call" | custom-call | flops 11500000256 | tf_op jit(solution)/shard_map/ffn_part/pallas_call | solution.py:283
  75.9 11.1 %norm_back.1 = (f32[1024,768]{1,0:T(8,128)}, bf16[1024,768]{1,0:T(8,128)(2,1)}, f32[1,768]{1,0:T(1,128)S(1)}, f32[8,128]{1,0:T(8,128)S(1)}) custom-call(bf16[1024,768]{1,0:T(8,128)(2,1)} %cot_ref.9, f32[1024,768]{1,0:T(8,128)} %get-tuple-element.155.middle_ref, f32[768]{0:T(1024)} %gain_ref.6, bf16[768,1536]{1,0:T(8,128)(2,1)S(1)} %collective-permute-done.5.wu_ref.wut_ref, ...), custom_call_target="tpu_custom_call" | custom-call | flops 115000000 | tf_op jit(solution)/shard_map/norm_back/pallas_call | solution.py:326
  87.0 1.1 halve.9
  88.2 2.1 collective-permute-start.10
  90.3 12.3 %attn_back.4 = (bf16[1024,256]{1,0:T(8,128)(2,1)}, bf16[4,288,256]{2,1,0:T(8,128)(2,1)}, bf16[4,288,256]{2,1,0:T(8,128)(2,1)}, bf16[1024,768]{1,0:T(8,128)(2,1)S(1)}, f32[8,128]{1,0:T(8,128)S(1)}) custom-call(bf16[1024,768]{1,0:T(8,128)(2,1)} %get-tuple-element.173.gm_ref, bf16[1024,768]{1,0:T(8,128)(2,1)} %get-tuple-element.151.xn_ref, ...), custom_call_target="tpu_custom_call" | custom-call | flops 115000000 | tf_op jit(solution)/shard_map/attn_back/pallas_call | solution.py:448
  103.5 1.1 halve.11
  104.7 2.1 collective-permute-start.12
  106.8 1.0 collective-permute-start.17
  107.8 8.8 %attn_back.5 = (bf16[1024,128]{1,0:T(8,128)(2,1)}, bf16[4,288,128]{2,1,0:T(8,128)(2,1)}, bf16[4,288,128]{2,1,0:T(8,128)(2,1)}, bf16[512,768]{1,0:T(8,128)(2,1)S(1)}, f32[8,128]{1,0:T(8,128)S(1)}) custom-call(bf16[1024,768]{1,0:T(8,128)(2,1)} %get-tuple-element.173.gm_ref, bf16[1024,768]{1,0:T(8,128)(2,1)} %get-tuple-element.151.xn_ref, ...), custom_call_target="tpu_custom_call" | custom-call | flops 115000000 | tf_op jit(solution)/shard_map/attn_back/pallas_call | solution.py:448
  117.3 2.0 collective-permute-start.14
  120.9 12.4 %attn_back.6 = (bf16[1024,256]{1,0:T(8,128)(2,1)}, bf16[4,288,256]{2,1,0:T(8,128)(2,1)}, bf16[4,288,256]{2,1,0:T(8,128)(2,1)}, bf16[1024,768]{1,0:T(8,128)(2,1)S(1)}, f32[8,128]{1,0:T(8,128)S(1)}) custom-call(bf16[1024,768]{1,0:T(8,128)(2,1)} %get-tuple-element.173.gm_ref, bf16[1024,768]{1,0:T(8,128)(2,1)} %get-tuple-element.151.xn_ref, ...), custom_call_target="tpu_custom_call" | custom-call | flops 25300000768 | tf_op jit(solution)/shard_map/attn_back/pallas_call | solution.py:448
  134.0 1.3 collective-permute-start.15
  135.3 2.6 collective-permute-start.16
  137.9 8.8 %attn_back.7 = (bf16[1024,128]{1,0:T(8,128)(2,1)}, bf16[4,288,128]{2,1,0:T(8,128)(2,1)}, bf16[4,288,128]{2,1,0:T(8,128)(2,1)}, bf16[512,768]{1,0:T(8,128)(2,1)S(1)}, f32[8,128]{1,0:T(8,128)S(1)}) custom-call(bf16[1024,768]{1,0:T(8,128)(2,1)} %get-tuple-element.173.gm_ref, bf16[1024,768]{1,0:T(8,128)(2,1)} %get-tuple-element.151.xn_ref, ...), custom_call_target="tpu_custom_call" | custom-call | flops 25300000768 | tf_op jit(solution)/shard_map/attn_back/pallas_call | solution.py:448
  146.7 1.3 open_sums.1
  148.0 1.6 collective-permute-start.22
  150.3 1.5 collective-permute-start.20
  151.7 10.2 %input_back.1 = (f32[1024,768]{1,0:T(8,128)}, f32[4,32,768]{2,1,0:T(8,128)S(1)}, f32[1,768]{1,0:T(1,128)S(1)}, f32[8,128]{1,0:T(8,128)S(1)}) custom-call(bf16[1024,768]{1,0:T(8,128)(2,1)} %x_ref.5, f32[1024,768]{1,0:T(8,128)} %get-tuple-element.171.gm_ref, f32[768]{0:T(1024)} %gain_ref.7, bf16[4,32,32]{2,1,0:T(8,128)(2,1)} %get-tuple-element.172.hot_ref, ...), custom_call_target="tpu_custom_call" | custom-call | flops 115000000 | tf_op jit(solution)/shard_map/input_back/pallas_call | solution.py:511
  162.0 2.3 collective-permute-done.22
  164.3 1.1 halve.15
  166.1 1.6 collective-permute-start.25
  168.9 1.5 collective-permute-start.19
  171.2 1.5 collective-permute-start.27
  172.7 9.5 %block_out.1 = (bf16[1024,768]{1,0:T(8,128)(2,1)}, f32[8,128]{1,0:T(8,128)S(1)}) custom-call(f32[1024,768]{1,0:T(8,128)} %get-tuple-element.155.middle_ref, bf16[1536,768]{1,0:T(8,128)(2,1)S(1)} %copy-done.1, bf16[1536,768]{1,0:T(8,128)(2,1)} %wdo_ref.1, bf16[1024,768]{1,0:T(8,128)(2,1)} %get-tuple-element.157.a0t, ...), custom_call_target="tpu_custom_call" | custom-call | flops 115000000 | tf_op jit(solution)/shard_map/block_out/pallas_call | solution.py:354
  185.5 1.6 collective-permute-start.29
  188.6 1.3 collective-permute-start.30
  189.9 7.0 %collective-permute-done.30.refs_2_.b_ref = f32[2,768]{1,0:T(2,128)S(1)} collective-permute-done((f32[2,768]{1,0:T(2,128)S(1)}, f32[2,768]{1,0:T(2,128)S(1)}, u32[]{:S(2)}, u32[]{:S(2)}) %collective-permute-start.30) | collective-permute-done | bytes 6176 | tf_op jit(solution)/shard_map/ppermute | solution.py:758
  196.9 3.2 %collective-permute-done.29.refs_1_.got_ref = bf16[384,768]{1,0:T(8,128)(2,1)S(1)} collective-permute-done((bf16[384,768]{1,0:T(8,128)(2,1)S(1)}, bf16[384,768]{1,0:T(8,128)(2,1)S(1)}, u32[]{:S(2)}, u32[]{:S(2)}) %collective-permute-start.29) | collective-permute-done | bytes 589856 | tf_op jit(solution)/shard_map/ppermute | solution.py:761
  201.6 4.1 %collective-permute-start.31 = (bf16[96,768]{1,0:T(8,128)(2,1)S(1)}, bf16[96,768]{1,0:T(8,128)(2,1)S(1)}, u32[]{:S(2)}, u32[]{:S(2)}) collective-permute-start(bf16[96,768]{1,0:T(8,128)(2,1)S(1)} %get-tuple-element.261), channel_id=1, source_target_pairs={{0,24},{1,9},{2,26},{3,11},{4,28},{5,13},{6,30},{7,15},{8,16},{9,1... | collective-permute-start | bytes 442376 | tf_op jit(solution)/shard_map/ppermute | solution.py:761
  206.0 4.7 %collective-permute-done.33.refs_2_.b_ref = f32[2,768]{1,0:T(2,128)S(1)} collective-permute-done((f32[2,768]{1,0:T(2,128)S(1)}, f32[2,768]{1,0:T(2,128)S(1)}, u32[]{:S(2)}, u32[]{:S(2)}) %collective-permute-start.33) | collective-permute-done | bytes 6176 | tf_op jit(solution)/shard_map/ppermute | solution.py:758
  210.7 2.0 collective-permute-start.34
  212.7 1.6 collective-permute-start.36
  214.3 2.2 collective-permute-done.36.refs_2_.b_ref
  216.5 1.3 collective-permute-done.34.got_ref
  217.8 2.1 collective-permute-done.35.refs_1_.got_ref
  221.2 7.4 %collective-permute-done.37.got_ref = bf16[192,768]{1,0:T(8,128)(2,1)S(1)} collective-permute-done((bf16[192,768]{1,0:T(8,128)(2,1)S(1)}, bf16[192,768]{1,0:T(8,128)(2,1)S(1)}, u32[]{:S(2)}, u32[]{:S(2)}) %collective-permute-start.37) | collective-permute-done | bytes 294944 | tf_op jit(solution)/shard_map/ppermute | solution.py:761
  229.3 1.6 collective-permute-start.38
  230.9 8.3 %collective-permute-done.38.got_ref = bf16[384,768]{1,0:T(8,128)(2,1)S(1)} collective-permute-done((bf16[384,768]{1,0:T(8,128)(2,1)S(1)}, bf16[384,768]{1,0:T(8,128)(2,1)S(1)}, u32[]{:S(2)}, u32[]{:S(2)}) %collective-permute-start.38) | collective-permute-done | bytes 589856 | tf_op jit(solution)/shard_map/ppermute | solution.py:761
  241.1 3.1 %ffn_finish.2 = (f32[1536,768]{1,0:T(8,128)}, f32[768,1536]{1,0:T(8,128)}, f32[8,128]{1,0:T(8,128)S(1)}) custom-call(s32[4]{0:T(128)S(1)} %broadcast_select_fusion.refs_1_.sides_ref, bf16[768,768]{1,0:T(8,128)(2,1)S(1)} %bitcast.46, bf16[768,768]{1,0:T(8,128)(2,1)S(1)} %collective-permute-done.32.refs_1_.got_ref, f32[8,128]{1,0:T(8,128)S(1)} %get-tuple-element.278.refs_0_), custom_call_target="tpu_custom_call" | custom-call | flops 57500000 | tf_op jit(solution)/shard_map/ffn_finish/pallas_call | solution.py:679
  244.2 3.1 %ffn_finish.3 = (f32[1536,768]{1,0:T(8,128)}, f32[768,1536]{1,0:T(8,128)}, f32[8,128]{1,0:T(8,128)S(1)}) custom-call(s32[4]{0:T(128)S(1)} %broadcast_select_fusion.refs_1_.sides_ref, bf16[768,768]{1,0:T(8,128)(2,1)S(1)} %bitcast.52, bf16[768,768]{1,0:T(8,128)(2,1)S(1)} %collective-permute-done.35.refs_1_.got_ref, ...), custom_call_target="tpu_custom_call", output_to_operand_aliasing={{0}: (3, {}), {1}: (4, {})} | custom-call | flops 57500000 | tf_op jit(solution)/shard_map/ffn_finish/pallas_call | solution.py:679
  247.3 9.1 %collective-permute-done.39.got_ref = bf16[768,768]{1,0:T(8,128)(2,1)S(1)} collective-permute-done((bf16[768,768]{1,0:T(8,128)(2,1)S(1)}, bf16[768,768]{1,0:T(8,128)(2,1)S(1)}, u32[]{:S(2)}, u32[]{:S(2)}) %collective-permute-start.39) | collective-permute-done | bytes 1179680 | tf_op jit(solution)/shard_map/ppermute | solution.py:761
  256.3 2.9 %attn_finish.1 = (f32[768,384]{1,0:T(8,128)}, f32[768,384]{1,0:T(8,128)}, f32[768,384]{1,0:T(8,128)}, f32[384,768]{1,0:T(8,128)}) custom-call(s32[4]{0:T(128)S(1)} %broadcast_select_fusion.refs_1_.sides_ref, bf16[768,768]{1,0:T(8,128)(2,1)S(1)} %bitcast.77, bf16[768,768]{1,0:T(8,128)(2,1)S(1)} %collective-permute-done.39.got_ref, ...), custom_call_target="tpu_custom_call" | custom-call | flops 2300000000 | tf_op jit(solution)/shard_map/attn_finish/pallas_call | solution.py:712
  (87 shorter events, 22.5 us)
Async XLA Ops:
  0.6 2.4 collective-permute-start
  1.2 16.6 %collective-permute-start.1 = (bf16[768,384]{1,0:T(8,128)(2,1)}, bf16[768,384]{1,0:T(8,128)(2,1)}, u32[]{:S(2)}, u32[]{:S(2)}) collective-permute-start(bf16[768,384]{1,0:T(8,128)(2,1)} %wko.1), channel_id=1, source_target_pairs={{0,1},{1,0},{2,3},{3,2},{4,5},{5,4},{6,7},{7,6},{8,9},{9,8},{10,11... | collective-permute-start | bytes 1769480 | tf_op jit(solution)/shard_map/ppermute | solution.py:816
  1.2 16.6 %collective-permute-start.2 = (bf16[768,384]{1,0:T(8,128)(2,1)}, bf16[768,384]{1,0:T(8,128)(2,1)}, u32[]{:S(2)}, u32[]{:S(2)}) collective-permute-start(bf16[768,384]{1,0:T(8,128)(2,1)} %wvo.1), channel_id=1, source_target_pairs={{0,1},{1,0},{2,3},{3,2},{4,5},{5,4},{6,7},{7,6},{8,9},{9,8},{10,11... | collective-permute-start | bytes 1769480 | tf_op jit(solution)/shard_map/ppermute | solution.py:816
  1.7 16.1 %collective-permute-start.3 = (bf16[384,768]{1,0:T(8,128)(2,1)}, bf16[384,768]{1,0:T(8,128)(2,1)S(1)}, u32[]{:S(2)}, u32[]{:S(2)}) collective-permute-start(bf16[384,768]{1,0:T(8,128)(2,1)} %wo_ref.3), channel_id=1, source_target_pairs={{0,1},{1,0},{2,3},{3,2},{4,5},{5,4},{6,7},{7,6},{8,9},{9,8},{10,11... | collective-permute-start | bytes 1769480 | tf_op jit(solution)/shard_map/ppermute | solution.py:816
  1.8 30.8 %collective-permute-start.5 = (bf16[768,1536]{1,0:T(8,128)(2,1)}, bf16[768,1536]{1,0:T(8,128)(2,1)S(1)}, u32[]{:S(2)}, u32[]{:S(2)}) collective-permute-start(bf16[768,1536]{1,0:T(8,128)(2,1)} %wuo_ref.1), channel_id=1, source_target_pairs={{0,1},{1,0},{2,3},{3,2},{4,5},{5,4},{6,7},{7,6},{8,9},{9,8},{10,11... | collective-permute-start | bytes 7077896 | tf_op jit(solution)/shard_map/ppermute | solution.py:816
  3.0 29.6 %collective-permute-start.4 = (bf16[1536,768]{1,0:T(8,128)(2,1)}, bf16[1536,768]{1,0:T(8,128)(2,1)S(1)}, u32[]{:S(2)}, u32[]{:S(2)}) collective-permute-start(bf16[1536,768]{1,0:T(8,128)(2,1)} %wdo_ref.1), channel_id=1, source_target_pairs={{0,1},{1,0},{2,3},{3,2},{4,5},{5,4},{6,7},{7,6},{8,9},{9,8},{10,11... | collective-permute-start | bytes 7077896 | tf_op jit(solution)/shard_map/ppermute | solution.py:816
  3.4 0.7 copy-start.2
  4.1 0.7 copy-start.3
  32.6 10.4 %copy-start = (bf16[1536,768]{1,0:T(8,128)(2,1)}, bf16[1536,768]{1,0:T(8,128)(2,1)S(1)}, u32[]{:S(2)}) copy-start(bf16[1536,768]{1,0:T(8,128)(2,1)S(1)} %collective-permute-done.4.wd_ref.wdt_ref) | copy-start | bytes 7077892
  42.9 10.0 %collective-permute-start.6 = (bf16[2,768,768]{2,1,0:T(8,128)(2,1)}, bf16[2,768,768]{2,1,0:T(8,128)(2,1)}, u32[]{:S(2)}, u32[]{:S(2)}) collective-permute-start(bf16[2,768,768]{2,1,0:T(8,128)(2,1)} %get-tuple-element.158), channel_id=1, source_target_pairs={{0,1},{1,0},{2,3},{3,2},{4,5},{5,4},{6,7},{7,6},{8,9},{9,8},{10,11... | collective-permute-start | bytes 7077896 | tf_op jit(solution)/shard_map/ppermute | solution.py:816
  52.4 13.2 %collective-permute-start.7 = (bf16[2,768,768]{2,1,0:T(8,128)(2,1)}, bf16[2,768,768]{2,1,0:T(8,128)(2,1)}, u32[]{:S(2)}, u32[]{:S(2)}) collective-permute-start(bf16[2,768,768]{2,1,0:T(8,128)(2,1)} %get-tuple-element.163), channel_id=1, source_target_pairs={{0,1},{1,0},{2,3},{3,2},{4,5},{5,4},{6,7},{7,6},{8,9},{9,8},{10,11... | collective-permute-start | bytes 7077896 | tf_op jit(solution)/shard_map/ppermute | solution.py:816
  62.9 24.1 %collective-permute-start.9 = (bf16[768,768]{1,0:T(8,128)(2,1)S(1)}, bf16[768,768]{1,0:T(8,128)(2,1)S(1)}, u32[]{:S(2)}, u32[]{:S(2)}) collective-permute-start(bf16[768,768]{1,0:T(8,128)(2,1)S(1)} %get-tuple-element.181), channel_id=1, source_target_pairs={{0,2},{1,5},{2,0},{3,7},{4,6},{5,1},{6,4},{7,3},{8,10},{9,13},{10,... | collective-permute-start | bytes 3538952 | tf_op jit(solution)/shard_map/ppermute | solution.py:761
  75.9 26.7 %collective-permute-start.8 = (bf16[768,768]{1,0:T(8,128)(2,1)S(1)}, bf16[768,768]{1,0:T(8,128)(2,1)S(1)}, u32[]{:S(2)}, u32[]{:S(2)}) collective-permute-start(bf16[768,768]{1,0:T(8,128)(2,1)S(1)} %get-tuple-element.179), channel_id=1, source_target_pairs={{0,2},{1,5},{2,0},{3,7},{4,6},{5,1},{6,4},{7,3},{8,10},{9,13},{10,... | collective-permute-start | bytes 3538952 | tf_op jit(solution)/shard_map/ppermute | solution.py:761
  88.2 14.4 %collective-permute-start.10 = (bf16[384,768]{1,0:T(8,128)(2,1)S(1)}, bf16[384,768]{1,0:T(8,128)(2,1)S(1)}, u32[]{:S(2)}, u32[]{:S(2)}) collective-permute-start(bf16[384,768]{1,0:T(8,128)(2,1)S(1)} %get-tuple-element.184), channel_id=1, source_target_pairs={{0,4},{1,3},{2,6},{3,1},{4,0},{5,7},{6,2},{7,5},{8,12},{9,11},{10,... | collective-permute-start | bytes 1769480 | tf_op jit(solution)/shard_map/ppermute | solution.py:761
  104.6 12.1 %collective-permute-start.11 = (bf16[384,768]{1,0:T(8,128)(2,1)S(1)}, bf16[384,768]{1,0:T(8,128)(2,1)S(1)}, u32[]{:S(2)}, u32[]{:S(2)}) collective-permute-start(bf16[384,768]{1,0:T(8,128)(2,1)S(1)} %get-tuple-element.194), channel_id=1, source_target_pairs={{0,4},{1,3},{2,6},{3,1},{4,0},{5,7},{6,2},{7,5},{8,12},{9,11},{10,... | collective-permute-start | bytes 1769480 | tf_op jit(solution)/shard_map/ppermute | solution.py:761
  104.7 12.0 %collective-permute-start.12 = (bf16[192,768]{1,0:T(8,128)(2,1)S(1)}, bf16[192,768]{1,0:T(8,128)(2,1)S(1)}, u32[]{:S(2)}, u32[]{:S(2)}) collective-permute-start(bf16[192,768]{1,0:T(8,128)(2,1)S(1)} %get-tuple-element.196), channel_id=1, source_target_pairs={{0,8},{1,25},{2,10},{3,27},{4,12},{5,29},{6,14},{7,31},{8,0},{9,17... | collective-permute-start | bytes 884744 | tf_op jit(solution)/shard_map/ppermute | solution.py:761
  106.8 39.9 %collective-permute-start.17 = (bf16[1024,768]{1,0:T(8,128)(2,1)S(1)}, bf16[1024,768]{1,0:T(8,128)(2,1)S(1)}, u32[]{:S(2)}, u32[]{:S(2)}) collective-permute-start(bf16[1024,768]{1,0:T(8,128)(2,1)S(1)} %get-tuple-element.224), channel_id=1, source_target_pairs={{0,1},{1,0},{2,3},{3,2},{4,5},{5,4},{6,7},{7,6},{8,9},{9,8},{10,11... | collective-permute-start | bytes 4718600 | tf_op jit(solution)/shard_map/ppermute | solution.py:816
  116.6 30.1 %collective-permute-start.18 = (bf16[512,768]{1,0:T(8,128)(2,1)S(1)}, bf16[512,768]{1,0:T(8,128)(2,1)S(1)}, u32[]{:S(2)}, u32[]{:S(2)}) collective-permute-start(bf16[512,768]{1,0:T(8,128)(2,1)S(1)} %get-tuple-element.226), channel_id=1, source_target_pairs={{0,1},{1,0},{2,3},{3,2},{4,5},{5,4},{6,7},{7,6},{8,9},{9,8},{10,11... | collective-permute-start | bytes 2359304 | tf_op jit(solution)/shard_map/ppermute | solution.py:816
  117.3 16.0 %collective-permute-start.14 = (bf16[96,768]{1,0:T(8,128)(2,1)S(1)}, bf16[96,768]{1,0:T(8,128)(2,1)S(1)}, u32[]{:S(2)}, u32[]{:S(2)}) collective-permute-start(bf16[96,768]{1,0:T(8,128)(2,1)S(1)} %get-tuple-element.205), channel_id=1, source_target_pairs={{0,24},{1,9},{2,26},{3,11},{4,28},{5,13},{6,30},{7,15},{8,16},{9,1... | collective-permute-start | bytes 442376 | tf_op jit(solution)/shard_map/ppermute | solution.py:761
  120.2 13.1 %collective-permute-start.13 = (bf16[192,768]{1,0:T(8,128)(2,1)S(1)}, bf16[192,768]{1,0:T(8,128)(2,1)S(1)}, u32[]{:S(2)}, u32[]{:S(2)}) collective-permute-start(bf16[192,768]{1,0:T(8,128)(2,1)S(1)} %get-tuple-element.203), channel_id=1, source_target_pairs={{0,8},{1,25},{2,10},{3,27},{4,12},{5,29},{6,14},{7,31},{8,0},{9,17... | collective-permute-start | bytes 884744 | tf_op jit(solution)/shard_map/ppermute | solution.py:761
  134.0 12.7 %collective-permute-start.15 = (bf16[96,768]{1,0:T(8,128)(2,1)S(1)}, bf16[96,768]{1,0:T(8,128)(2,1)S(1)}, u32[]{:S(2)}, u32[]{:S(2)}) collective-permute-start(bf16[96,768]{1,0:T(8,128)(2,1)S(1)} %get-tuple-element.221), channel_id=1, source_target_pairs={{0,24},{1,9},{2,26},{3,11},{4,28},{5,13},{6,30},{7,15},{8,16},{9,1... | collective-permute-start | bytes 442376 | tf_op jit(solution)/shard_map/ppermute | solution.py:761
  135.3 11.4 %collective-permute-start.16 = (bf16[96,768]{1,0:T(8,128)(2,1)S(1)}, bf16[96,768]{1,0:T(8,128)(2,1)S(1)}, u32[]{:S(2)}, u32[]{:S(2)}) collective-permute-start(bf16[96,768]{1,0:T(8,128)(2,1)S(1)} %get-tuple-element.222.mine_ref), channel_id=1, source_target_pairs={{0,24},{1,9},{2,26},{3,11},{4,28},{5,13},{6,30},{7,15},{8,16},{9,1... | collective-permute-start | bytes 442376 | tf_op jit(solution)/shard_map/ppermute | solution.py:761
  148.0 16.3 %collective-permute-start.22 = (bf16[768,768]{1,0:T(8,128)(2,1)S(1)}, bf16[768,768]{1,0:T(8,128)(2,1)S(1)}, u32[]{:S(2)}, u32[]{:S(2)}) collective-permute-start(bf16[768,768]{1,0:T(8,128)(2,1)S(1)} %get-tuple-element.236), channel_id=1, source_target_pairs={{0,2},{1,5},{2,0},{3,7},{4,6},{5,1},{6,4},{7,3},{8,10},{9,13},{10,... | collective-permute-start | bytes 3538952 | tf_op jit(solution)/shard_map/ppermute | solution.py:761
  150.1 11.8 %collective-permute-start.21 = (bf16[192,768]{1,0:T(8,128)(2,1)S(1)}, bf16[192,768]{1,0:T(8,128)(2,1)S(1)}, u32[]{:S(2)}, u32[]{:S(2)}) collective-permute-start(bf16[192,768]{1,0:T(8,128)(2,1)S(1)} %bitcast.68), channel_id=1, source_target_pairs={{0,8},{1,25},{2,10},{3,27},{4,12},{5,29},{6,14},{7,31},{8,0},{9,17... | collective-permute-start | bytes 884744 | tf_op jit(solution)/shard_map/ppermute | solution.py:761
  150.3 11.7 %collective-permute-start.20 = (bf16[96,768]{1,0:T(8,128)(2,1)S(1)}, bf16[96,768]{1,0:T(8,128)(2,1)S(1)}, u32[]{:S(2)}, u32[]{:S(2)}) collective-permute-start(bf16[96,768]{1,0:T(8,128)(2,1)S(1)} %get-tuple-element.233.mine_ref), channel_id=1, source_target_pairs={{0,24},{1,9},{2,26},{3,11},{4,28},{5,13},{6,30},{7,15},{8,16},{9,1... | collective-permute-start | bytes 442376 | tf_op jit(solution)/shard_map/ppermute | solution.py:761
  164.3 8.4 %copy-start.1 = (bf16[1536,768]{1,0:T(8,128)(2,1)S(1)}, bf16[1536,768]{1,0:T(8,128)(2,1)}, u32[]{:S(2)}) copy-start(bf16[1536,768]{1,0:T(8,128)(2,1)} %copy-done) | copy-start | bytes 7077892
  166.1 17.0 %collective-permute-start.25 = (bf16[384,768]{1,0:T(8,128)(2,1)S(1)}, bf16[384,768]{1,0:T(8,128)(2,1)S(1)}, u32[]{:S(2)}, u32[]{:S(2)}) collective-permute-start(bf16[384,768]{1,0:T(8,128)(2,1)S(1)} %bitcast.57), channel_id=1, source_target_pairs={{0,4},{1,3},{2,6},{3,1},{4,0},{5,7},{6,2},{7,5},{8,12},{9,11},{10,... | collective-permute-start | bytes 1769480 | tf_op jit(solution)/shard_map/ppermute | solution.py:761
  167.7 15.4 %collective-permute-start.23 = (bf16[384,768]{1,0:T(8,128)(2,1)S(1)}, bf16[384,768]{1,0:T(8,128)(2,1)S(1)}, u32[]{:S(2)}, u32[]{:S(2)}) collective-permute-start(bf16[384,768]{1,0:T(8,128)(2,1)S(1)} %get-tuple-element.245), channel_id=1, source_target_pairs={{0,4},{1,3},{2,6},{3,1},{4,0},{5,7},{6,2},{7,5},{8,12},{9,11},{10,... | collective-permute-start | bytes 1769480 | tf_op jit(solution)/shard_map/ppermute | solution.py:761
  168.2 14.0 %collective-permute-start.24 = (f32[4,32,768]{2,1,0:T(8,128)S(1)}, f32[4,32,768]{2,1,0:T(8,128)S(1)}, u32[]{:S(2)}, u32[]{:S(2)}) collective-permute-start(f32[4,32,768]{2,1,0:T(8,128)S(1)} %get-tuple-element.246.mine_ref), channel_id=1, source_target_pairs={{0,1},{1,0},{2,3},{3,2},{4,5},{5,4},{6,7},{7,6},{8,9},{9,8},{10,11... | collective-permute-start | bytes 1179656 | tf_op jit(solution)/shard_map/ppermute | solution.py:816
  168.8 14.4 %collective-permute-start.26 = (bf16[192,768]{1,0:T(8,128)(2,1)S(1)}, bf16[192,768]{1,0:T(8,128)(2,1)S(1)}, u32[]{:S(2)}, u32[]{:S(2)}) collective-permute-start(bf16[192,768]{1,0:T(8,128)(2,1)S(1)} %bitcast.66), channel_id=1, source_target_pairs={{0,8},{1,25},{2,10},{3,27},{4,12},{5,29},{6,14},{7,31},{8,0},{9,17... | collective-permute-start | bytes 884744 | tf_op jit(solution)/shard_map/ppermute | solution.py:761
  168.9 2.4 collective-permute-start.19
  171.2 11.9 %collective-permute-start.27 = (f32[2,768]{1,0:T(2,128)S(1)}, f32[2,768]{1,0:T(2,128)S(1)}, u32[]{:S(2)}, u32[]{:S(2)}) collective-permute-start(f32[2,768]{1,0:T(2,128)S(1)} %get-tuple-element.251.a_ref), channel_id=1, source_target_pairs={{0,2},{1,3},{2,0},{3,1},{4,6},{5,7},{6,4},{7,5},{8,10},{9,11},{10,... | collective-permute-start | bytes 18440 | tf_op jit(solution)/shard_map/ppermute | solution.py:758
  185.5 14.6 %collective-permute-start.29 = (bf16[384,768]{1,0:T(8,128)(2,1)S(1)}, bf16[384,768]{1,0:T(8,128)(2,1)S(1)}, u32[]{:S(2)}, u32[]{:S(2)}) collective-permute-start(bf16[384,768]{1,0:T(8,128)(2,1)S(1)} %bitcast.60), channel_id=1, source_target_pairs={{0,4},{1,3},{2,6},{3,1},{4,0},{5,7},{6,2},{7,5},{8,12},{9,11},{10,... | collective-permute-start | bytes 1769480 | tf_op jit(solution)/shard_map/ppermute | solution.py:761
  187.1 9.7 %collective-permute-start.28 = (bf16[192,768]{1,0:T(8,128)(2,1)S(1)}, bf16[192,768]{1,0:T(8,128)(2,1)S(1)}, u32[]{:S(2)}, u32[]{:S(2)}) collective-permute-start(bf16[192,768]{1,0:T(8,128)(2,1)S(1)} %get-tuple-element.253), channel_id=1, source_target_pairs={{0,8},{1,25},{2,10},{3,27},{4,12},{5,29},{6,14},{7,31},{8,0},{9,17... | collective-permute-start | bytes 884744 | tf_op jit(solution)/shard_map/ppermute | solution.py:761
  188.0 22.7 %collective-permute-start.32 = (bf16[768,768]{1,0:T(8,128)(2,1)S(1)}, bf16[768,768]{1,0:T(8,128)(2,1)S(1)}, u32[]{:S(2)}, u32[]{:S(2)}) collective-permute-start(bf16[768,768]{1,0:T(8,128)(2,1)S(1)} %bitcast.45), channel_id=1, source_target_pairs={{0,2},{1,5},{2,0},{3,7},{4,6},{5,1},{6,4},{7,3},{8,10},{9,13},{10,... | collective-permute-start | bytes 3538952 | tf_op jit(solution)/shard_map/ppermute | solution.py:761
  188.6 8.3 %collective-permute-start.30 = (f32[2,768]{1,0:T(2,128)S(1)}, f32[2,768]{1,0:T(2,128)S(1)}, u32[]{:S(2)}, u32[]{:S(2)}) collective-permute-start(f32[2,768]{1,0:T(2,128)S(1)} %get-tuple-element.259.a_ref), channel_id=1, source_target_pairs={{0,8},{1,9},{2,10},{3,11},{4,12},{5,13},{6,14},{7,15},{8,0},{9,1},... | collective-permute-start | bytes 18440 | tf_op jit(solution)/shard_map/ppermute | solution.py:758
  201.5 18.3 %collective-permute-start.35 = (bf16[768,768]{1,0:T(8,128)(2,1)S(1)}, bf16[768,768]{1,0:T(8,128)(2,1)S(1)}, u32[]{:S(2)}, u32[]{:S(2)}) collective-permute-start(bf16[768,768]{1,0:T(8,128)(2,1)S(1)} %bitcast.51), channel_id=1, source_target_pairs={{0,2},{1,5},{2,0},{3,7},{4,6},{5,1},{6,4},{7,3},{8,10},{9,13},{10,... | collective-permute-start | bytes 3538952 | tf_op jit(solution)/shard_map/ppermute | solution.py:761
  201.6 9.1 %collective-permute-start.31 = (bf16[96,768]{1,0:T(8,128)(2,1)S(1)}, bf16[96,768]{1,0:T(8,128)(2,1)S(1)}, u32[]{:S(2)}, u32[]{:S(2)}) collective-permute-start(bf16[96,768]{1,0:T(8,128)(2,1)S(1)} %get-tuple-element.261), channel_id=1, source_target_pairs={{0,24},{1,9},{2,26},{3,11},{4,28},{5,13},{6,30},{7,15},{8,16},{9,1... | collective-permute-start | bytes 442376 | tf_op jit(solution)/shard_map/ppermute | solution.py:761
  205.7 5.0 %collective-permute-start.33 = (f32[2,768]{1,0:T(2,128)S(1)}, f32[2,768]{1,0:T(2,128)S(1)}, u32[]{:S(2)}, u32[]{:S(2)}) collective-permute-start(f32[2,768]{1,0:T(2,128)S(1)} %get-tuple-element.266.a_ref), channel_id=1, source_target_pairs={{0,16},{1,17},{2,18},{3,19},{4,20},{5,21},{6,22},{7,23},{8,24},{9,... | collective-permute-start | bytes 18440 | tf_op jit(solution)/shard_map/ppermute | solution.py:758
  210.7 7.0 %collective-permute-start.34 = (bf16[96,768]{1,0:T(8,128)(2,1)S(1)}, bf16[96,768]{1,0:T(8,128)(2,1)S(1)}, u32[]{:S(2)}, u32[]{:S(2)}) collective-permute-start(bf16[96,768]{1,0:T(8,128)(2,1)S(1)} %get-tuple-element.267.mine_ref), channel_id=1, source_target_pairs={{0,24},{1,9},{2,26},{3,11},{4,28},{5,13},{6,30},{7,15},{8,16},{9,1... | collective-permute-start | bytes 442376 | tf_op jit(solution)/shard_map/ppermute | solution.py:761
  212.7 3.8 %collective-permute-start.36 = (f32[2,768]{1,0:T(2,128)S(1)}, f32[2,768]{1,0:T(2,128)S(1)}, u32[]{:S(2)}, u32[]{:S(2)}) collective-permute-start(f32[2,768]{1,0:T(2,128)S(1)} %get-tuple-element.271.a_ref), channel_id=1, source_target_pairs={{0,4},{1,5},{2,6},{3,7},{4,0},{5,1},{6,2},{7,3},{8,12},{9,13},{10,... | collective-permute-start | bytes 18440 | tf_op jit(solution)/shard_map/ppermute | solution.py:758
  220.4 8.2 %collective-permute-start.37 = (bf16[192,768]{1,0:T(8,128)(2,1)S(1)}, bf16[192,768]{1,0:T(8,128)(2,1)S(1)}, u32[]{:S(2)}, u32[]{:S(2)}) collective-permute-start(bf16[192,768]{1,0:T(8,128)(2,1)S(1)} %bitcast.71), channel_id=1, source_target_pairs={{0,8},{1,25},{2,10},{3,27},{4,12},{5,29},{6,14},{7,31},{8,0},{9,17... | collective-permute-start | bytes 884744 | tf_op jit(solution)/shard_map/ppermute | solution.py:761
  229.3 9.9 %collective-permute-start.38 = (bf16[384,768]{1,0:T(8,128)(2,1)S(1)}, bf16[384,768]{1,0:T(8,128)(2,1)S(1)}, u32[]{:S(2)}, u32[]{:S(2)}) collective-permute-start(bf16[384,768]{1,0:T(8,128)(2,1)S(1)} %bitcast.62), channel_id=1, source_target_pairs={{0,4},{1,3},{2,6},{3,1},{4,0},{5,7},{6,2},{7,5},{8,12},{9,11},{10,... | collective-permute-start | bytes 1769480 | tf_op jit(solution)/shard_map/ppermute | solution.py:761
  240.1 16.3 %collective-permute-start.39 = (bf16[768,768]{1,0:T(8,128)(2,1)S(1)}, bf16[768,768]{1,0:T(8,128)(2,1)S(1)}, u32[]{:S(2)}, u32[]{:S(2)}) collective-permute-start(bf16[768,768]{1,0:T(8,128)(2,1)S(1)} %bitcast.76), channel_id=1, source_target_pairs={{0,2},{1,5},{2,0},{3,7},{4,6},{5,1},{6,4},{7,3},{8,10},{9,13},{10,... | collective-permute-start | bytes 3538952 | tf_op jit(solution)/shard_map/ppermute | solution.py:761

commit v4 on v3

--- a/solution.py
+++ b/solution.py
@@ -869,9 +869,7 @@
     gains = jnp.concatenate([gg_attn, gg_ffn], axis=0)
     gains = Small(chips, gains, core_swap(gains))
     mark = gains.step(ffn[1].step(ffn[0].step(attn.step([mark, *arrived(ffn)]))))
-    block_out, mark = block_output(middle, wd_oth, w_down, acts, mark)
-    grad_value_pool, mark = pool_join(grad_pool, pool_got, [mark])
-    mark = [mark]
+    block_out = None
     last = 2 * chips.levels
     ready = []
     late = [0] * count
@@ -885,6 +883,10 @@
                 mark = group.step(mark)
         if not gains.done:
             mark = gains.step(mark)
+        if block_out is None:
+            block_out, mark = block_output(middle, wd_oth, w_down, acts, mark)
+            grad_value_pool, mark = pool_join(grad_pool, pool_got, [mark])
+            mark = [mark]
     while len(ready) < count:
         at = len(ready)
         *out, mark = ffn_finish(

time: 260 us -> 260 us (level)
  starting transfers between devices: 40.5 us -> 37 us
  waiting for transfers between devices: 49.2 us -> 52.7 us
    ppermute x24, waiting for transfers between devices: 33.7 us -> 41.8 us  [exchange(): return lax.ppermute(array, ('dp', 'mp'), self.pairs[level])]
    ppermute x4, waiting for transfers between devices: 13.9 us -> 8.84 us  [turn(): return lax.ppermute(array, ('dp', 'mp'), self.turns[at])]
    ppermute x24, starting transfers between devices: 30.8 us -> 27.3 us  [exchange(): return lax.ppermute(array, ('dp', 'mp'), self.pairs[level])]
  transfers between devices with their start and end apart: 40 -> 40, of which waited for: 12 -> 14; matrix products, arithmetic and copies ran while one was open for 0% -> 0% of each run, Pallas kernels for 55% -> 55%
where the time goes in v4:
time: 260 us; the launch traced here: 259 us
  Pallas kernels  166 us (64%)
  waiting for transfers between devices  52.7 us (20%)
  starting transfers between devices  37 us (14%)
    pallas_call x4, Pallas kernels, attn_back(): pl.pallas_call(attn_back_kernel, grid=(seqs,), out_shape=[o[0] for o in o...  42.4 us
    ppermute x24, waiting for transfers between devices, exchange(): return lax.ppermute(array, ('dp', 'mp'), self.pairs[level])  41.8 us
    pallas_call x4, Pallas kernels, ffn_part(): pl.pallas_call(functools.partial(ffn_kernel, own, 256), grid=(steps,), ou...  40 us
    ppermute x24, starting transfers between devices, exchange(): return lax.ppermute(array, ('dp', 'mp'), self.pairs[level])  27.3 us
    pallas_call x1, Pallas kernels, attention_forward(): pl.pallas_call(attn_second_kernel, grid=(seqs,), out_shape=[o[0] for o in...  14.8 us
    pallas_call x1, Pallas kernels, attention_forward(): pl.pallas_call(attn_first_kernel, grid_spec=pltpu.PrefetchScalarGridSpec(...  13 us
    pallas_call x1, Pallas kernels, norm_back(): pl.pallas_call(norm_back_kernel, grid=(rows // block,), out_shape=[stored...  11.1 us
    pallas_call x1, Pallas kernels, input_back(): pl.pallas_call(functools.partial(input_back_kernel, len(grads)), grid=(se...  10.2 us
  transfers between devices with their start and end apart: 40, of which 14 were waited for; matrix products, arithmetic and copies ran while one was open for 0% of the time, Pallas kernels for 55%

profile of v4, /device:TPU:0, one launch (start us, length us, event | category | flops | bytes accessed | tf_op | source)
XLA Modules:
  0.0 259.2 jit_solution(17991194515356383326)
XLA Ops:
  4.8 13.0 %attn_first.1 = (bf16[1024,768]{1,0:T(8,128)(2,1)}, bf16[4,32,768]{2,1,0:T(8,128)(2,1)}, f32[4,288,1]{2,1,0:T(8,128)}, bf16[4,32,32]{2,1,0:T(8,128)(2,1)}, bf16[...) custom-call(s32[1]{0:T(128)} %bitcast.first_ref, ...), custom_call_target="tpu_custom_call" | custom-call | flops 13799999488 | tf_op jit(solution)/shard_map/attn_first/pallas_call | solution.py:179
  17.8 14.8 %attn_second.1 = (bf16[1024,384]{1,0:T(8,128)(2,1)}, bf16[4,288,384]{2,1,0:T(8,128)(2,1)}, bf16[4,288,384]{2,1,0:T(8,128)(2,1)}, bf16[4,6,288,256]{3,2,1,0:T(8,1...) custom-call(bf16[1024,768]{1,0:T(8,128)(2,1)} %x_ref.5, f32[768]{0:T(1024)} %gain_ref.6, ...), custom_call_target="tpu_custom_call" | custom-call | flops 13799999488 | tf_op jit(solution)/shard_map/attn_second/pallas_call | solution.py:203
  32.6 10.2 %ffn_part.4 = (bf16[1024,768]{1,0:T(8,128)(2,1)}, bf16[1024,768]{1,0:T(8,128)(2,1)}, bf16[2,768,768]{2,1,0:T(8,128)(2,1)}, f32[8,128]{1,0:T(8,128)S(1)}) custom-call(bf16[1024,768]{1,0:T(8,128)(2,1)} %get-tuple-element.156.nf_ref, bf16[1024,768]{1,0:T(8,128)(2,1)} %cot_ref.9, bf16[768,1536]{1,0:T(8,128)(2,1)S(1)} %collective-permute-done.5.wu_ref.wut_ref, ...), custom_call_target="tpu_custom_call" | custom-call | flops 11500000256 | tf_op jit(solution)/shard_map/ffn_part/pallas_call | solution.py:283
  43.0 9.4 %ffn_part.5 = (bf16[1024,768]{1,0:T(8,128)(2,1)}, bf16[1024,768]{1,0:T(8,128)(2,1)}, bf16[2,768,768]{2,1,0:T(8,128)(2,1)}, f32[8,128]{1,0:T(8,128)S(1)}) custom-call(bf16[1024,768]{1,0:T(8,128)(2,1)} %get-tuple-element.156.nf_ref, bf16[1024,768]{1,0:T(8,128)(2,1)} %cot_ref.9, bf16[768,1536]{1,0:T(8,128)(2,1)S(1)} %collective-permute-done.5.wu_ref.wut_ref, ...), custom_call_target="tpu_custom_call" | custom-call | flops 11500000256 | tf_op jit(solution)/shard_map/ffn_part/pallas_call | solution.py:283
  52.9 10.1 %ffn_part.6 = (bf16[1024,768]{1,0:T(8,128)(2,1)}, bf16[1024,768]{1,0:T(8,128)(2,1)}, bf16[768,768]{1,0:T(8,128)(2,1)S(1)}, bf16[768,768]{1,0:T(8,128)(2,1)S(1)}, f32[8,128]{1,0:T(8,128)S(1)}) custom-call(bf16[1024,768]{1,0:T(8,128)(2,1)} %get-tuple-element.156.nf_ref, bf16[1024,768]{1,0:T(8,128)(2,1)} %cot_ref.9, bf16[768,1536]{1,0:T(8,128)(2,1)} %wuo_ref.1, ...), custom_call_target="tpu_custom_call" | custom-call | flops 11500000256 | tf_op jit(solution)/shard_map/ffn_part/pallas_call | solution.py:283
  62.9 2.6 %collective-permute-start.9 = (bf16[768,768]{1,0:T(8,128)(2,1)S(1)}, bf16[768,768]{1,0:T(8,128)(2,1)S(1)}, u32[]{:S(2)}, u32[]{:S(2)}) collective-permute-start(bf16[768,768]{1,0:T(8,128)(2,1)S(1)} %get-tuple-element.181), channel_id=1, source_target_pairs={{0,2},{1,5},{2,0},{3,7},{4,6},{5,1},{6,4},{7,3},{8,10},{9,13},{10,... | collective-permute-start | bytes 3538952 | tf_op jit(solution)/shard_map/ppermute | solution.py:761
  65.6 10.3 %ffn_part.7 = (bf16[1024,768]{1,0:T(8,128)(2,1)}, bf16[1024,768]{1,0:T(8,128)(2,1)}, bf16[768,768]{1,0:T(8,128)(2,1)S(1)}, bf16[768,768]{1,0:T(8,128)(2,1)S(1)}, f32[8,128]{1,0:T(8,128)S(1)}) custom-call(bf16[1024,768]{1,0:T(8,128)(2,1)} %get-tuple-element.156.nf_ref, bf16[1024,768]{1,0:T(8,128)(2,1)} %cot_ref.9, bf16[768,1536]{1,0:T(8,128)(2,1)} %wuo_ref.1, ...), custom_call_target="tpu_custom_call" | custom-call | flops 11500000256 | tf_op jit(solution)/shard_map/ffn_part/pallas_call | solution.py:283
  75.9 11.1 %norm_back.1 = (f32[1024,768]{1,0:T(8,128)}, bf16[1024,768]{1,0:T(8,128)(2,1)}, f32[1,768]{1,0:T(1,128)S(1)}, f32[8,128]{1,0:T(8,128)S(1)}) custom-call(bf16[1024,768]{1,0:T(8,128)(2,1)} %cot_ref.9, f32[1024,768]{1,0:T(8,128)} %get-tuple-element.155.middle_ref, f32[768]{0:T(1024)} %gain_ref.6, bf16[768,1536]{1,0:T(8,128)(2,1)S(1)} %collective-permute-done.5.wu_ref.wut_ref, ...), custom_call_target="tpu_custom_call" | custom-call | flops 115000000 | tf_op jit(solution)/shard_map/norm_back/pallas_call | solution.py:326
  87.0 1.1 halve.9
  88.2 2.1 collective-permute-start.10
  90.3 12.3 %attn_back.4 = (bf16[1024,256]{1,0:T(8,128)(2,1)}, bf16[4,288,256]{2,1,0:T(8,128)(2,1)}, bf16[4,288,256]{2,1,0:T(8,128)(2,1)}, bf16[1024,768]{1,0:T(8,128)(2,1)S(1)}, f32[8,128]{1,0:T(8,128)S(1)}) custom-call(bf16[1024,768]{1,0:T(8,128)(2,1)} %get-tuple-element.173.gm_ref, bf16[1024,768]{1,0:T(8,128)(2,1)} %get-tuple-element.151.xn_ref, ...), custom_call_target="tpu_custom_call" | custom-call | flops 115000000 | tf_op jit(solution)/shard_map/attn_back/pallas_call | solution.py:448
  103.5 1.1 halve.11
  104.7 2.1 collective-permute-start.12
  107.8 8.8 %attn_back.5 = (bf16[1024,128]{1,0:T(8,128)(2,1)}, bf16[4,288,128]{2,1,0:T(8,128)(2,1)}, bf16[4,288,128]{2,1,0:T(8,128)(2,1)}, bf16[512,768]{1,0:T(8,128)(2,1)S(1)}, f32[8,128]{1,0:T(8,128)S(1)}) custom-call(bf16[1024,768]{1,0:T(8,128)(2,1)} %get-tuple-element.173.gm_ref, bf16[1024,768]{1,0:T(8,128)(2,1)} %get-tuple-element.151.xn_ref, ...), custom_call_target="tpu_custom_call" | custom-call | flops 115000000 | tf_op jit(solution)/shard_map/attn_back/pallas_call | solution.py:448
  117.3 2.0 collective-permute-start.14
  120.9 12.4 %attn_back.6 = (bf16[1024,256]{1,0:T(8,128)(2,1)}, bf16[4,288,256]{2,1,0:T(8,128)(2,1)}, bf16[4,288,256]{2,1,0:T(8,128)(2,1)}, bf16[1024,768]{1,0:T(8,128)(2,1)S(1)}, f32[8,128]{1,0:T(8,128)S(1)}) custom-call(bf16[1024,768]{1,0:T(8,128)(2,1)} %get-tuple-element.173.gm_ref, bf16[1024,768]{1,0:T(8,128)(2,1)} %get-tuple-element.151.xn_ref, ...), custom_call_target="tpu_custom_call" | custom-call | flops 25300000768 | tf_op jit(solution)/shard_map/attn_back/pallas_call | solution.py:448
  134.0 1.3 collective-permute-start.15
  135.3 2.6 collective-permute-start.16
  137.9 8.8 %attn_back.7 = (bf16[1024,128]{1,0:T(8,128)(2,1)}, bf16[4,288,128]{2,1,0:T(8,128)(2,1)}, bf16[4,288,128]{2,1,0:T(8,128)(2,1)}, bf16[512,768]{1,0:T(8,128)(2,1)S(1)}, f32[8,128]{1,0:T(8,128)S(1)}) custom-call(bf16[1024,768]{1,0:T(8,128)(2,1)} %get-tuple-element.173.gm_ref, bf16[1024,768]{1,0:T(8,128)(2,1)} %get-tuple-element.151.xn_ref, ...), custom_call_target="tpu_custom_call" | custom-call | flops 25300000768 | tf_op jit(solution)/shard_map/attn_back/pallas_call | solution.py:448
  146.7 1.3 open_sums.1
  148.0 1.6 collective-permute-start.22
  150.3 1.5 collective-permute-start.20
  151.7 10.2 %input_back.1 = (f32[1024,768]{1,0:T(8,128)}, f32[4,32,768]{2,1,0:T(8,128)S(1)}, f32[1,768]{1,0:T(1,128)S(1)}, f32[8,128]{1,0:T(8,128)S(1)}) custom-call(bf16[1024,768]{1,0:T(8,128)(2,1)} %x_ref.5, f32[1024,768]{1,0:T(8,128)} %get-tuple-element.171.gm_ref, f32[768]{0:T(1024)} %gain_ref.7, bf16[4,32,32]{2,1,0:T(8,128)(2,1)} %get-tuple-element.172.hot_ref, ...), custom_call_target="tpu_custom_call" | custom-call | flops 115000000 | tf_op jit(solution)/shard_map/input_back/pallas_call | solution.py:511
  162.0 2.3 collective-permute-done.22
  166.1 1.6 collective-permute-start.25
  168.9 1.2 collective-permute-done.19.b_ref
  170.1 1.5 collective-permute-start.23
  171.6 2.3 collective-permute-done.23.refs_3_.b_ref
  173.9 2.6 collective-permute-done.24.refs_2_.got_ref
  176.4 5.9 %collective-permute-done.26 = bf16[384,768]{1,0:T(8,128)(2,1)S(1)} collective-permute-done((bf16[384,768]{1,0:T(8,128)(2,1)S(1)}, bf16[384,768]{1,0:T(8,128)(2,1)S(1)}, u32[]{:S(2)}, u32[]{:S(2)}) %collective-permute-start.26) | collective-permute-done | bytes 589856 | tf_op jit(solution)/shard_map/ppermute | solution.py:761
  184.7 1.6 collective-permute-start.29
  186.3 1.5 collective-permute-start.32
  187.8 2.0 collective-permute-start.30
  189.9 9.4 %block_out.1 = (bf16[1024,768]{1,0:T(8,128)(2,1)}, f32[8,128]{1,0:T(8,128)S(1)}) custom-call(f32[1024,768]{1,0:T(8,128)} %get-tuple-element.155.middle_ref, bf16[1536,768]{1,0:T(8,128)(2,1)S(1)} %copy-done.1, bf16[1536,768]{1,0:T(8,128)(2,1)} %wdo_ref.1, bf16[1024,768]{1,0:T(8,128)(2,1)} %get-tuple-element.157.a0t, ...), custom_call_target="tpu_custom_call" | custom-call | flops 115000000 | tf_op jit(solution)/shard_map/block_out/pallas_call | solution.py:354
  202.4 1.2 collective-permute-start.31
  203.8 4.9 %collective-permute-done.33.refs_2_.b_ref = f32[2,768]{1,0:T(2,128)S(1)} collective-permute-done((f32[2,768]{1,0:T(2,128)S(1)}, f32[2,768]{1,0:T(2,128)S(1)}, u32[]{:S(2)}, u32[]{:S(2)}) %collective-permute-start.33) | collective-permute-done | bytes 6176 | tf_op jit(solution)/shard_map/ppermute | solution.py:758
  209.5 1.4 collective-permute-start.34
  210.8 2.3 collective-permute-start.36
  213.2 1.7 collective-permute-done.36.refs_2_.b_ref
  214.9 1.6 collective-permute-done.34.got_ref
  216.5 1.5 collective-permute-done.35.refs_1_.got_ref
  218.7 9.9 %collective-permute-done.37.got_ref = bf16[192,768]{1,0:T(8,128)(2,1)S(1)} collective-permute-done((bf16[192,768]{1,0:T(8,128)(2,1)S(1)}, bf16[192,768]{1,0:T(8,128)(2,1)S(1)}, u32[]{:S(2)}, u32[]{:S(2)}) %collective-permute-start.37) | collective-permute-done | bytes 294944 | tf_op jit(solution)/shard_map/ppermute | solution.py:761
  229.2 1.3 collective-permute-start.38
  230.5 8.6 %collective-permute-done.38.got_ref = bf16[384,768]{1,0:T(8,128)(2,1)S(1)} collective-permute-done((bf16[384,768]{1,0:T(8,128)(2,1)S(1)}, bf16[384,768]{1,0:T(8,128)(2,1)S(1)}, u32[]{:S(2)}, u32[]{:S(2)}) %collective-permute-start.38) | collective-permute-done | bytes 589856 | tf_op jit(solution)/shard_map/ppermute | solution.py:761
  241.4 3.1 %ffn_finish.2 = (f32[1536,768]{1,0:T(8,128)}, f32[768,1536]{1,0:T(8,128)}, f32[8,128]{1,0:T(8,128)S(1)}) custom-call(s32[4]{0:T(128)S(1)} %broadcast_select_fusion.refs_1_.sides_ref, bf16[768,768]{1,0:T(8,128)(2,1)S(1)} %bitcast.46, bf16[768,768]{1,0:T(8,128)(2,1)S(1)} %collective-permute-done.32.refs_1_.got_ref, f32[8,128]{1,0:T(8,128)S(1)} %get-tuple-element.278.refs_0_), custom_call_target="tpu_custom_call" | custom-call | flops 57500000 | tf_op jit(solution)/shard_map/ffn_finish/pallas_call | solution.py:679
  244.5 3.1 %ffn_finish.3 = (f32[1536,768]{1,0:T(8,128)}, f32[768,1536]{1,0:T(8,128)}, f32[8,128]{1,0:T(8,128)S(1)}) custom-call(s32[4]{0:T(128)S(1)} %broadcast_select_fusion.refs_1_.sides_ref, bf16[768,768]{1,0:T(8,128)(2,1)S(1)} %bitcast.52, bf16[768,768]{1,0:T(8,128)(2,1)S(1)} %collective-permute-done.35.refs_1_.got_ref, ...), custom_call_target="tpu_custom_call", output_to_operand_aliasing={{0}: (3, {}), {1}: (4, {})} | custom-call | flops 57500000 | tf_op jit(solution)/shard_map/ffn_finish/pallas_call | solution.py:679
  247.6 8.7 %collective-permute-done.39.got_ref = bf16[768,768]{1,0:T(8,128)(2,1)S(1)} collective-permute-done((bf16[768,768]{1,0:T(8,128)(2,1)S(1)}, bf16[768,768]{1,0:T(8,128)(2,1)S(1)}, u32[]{:S(2)}, u32[]{:S(2)}) %collective-permute-start.39) | collective-permute-done | bytes 1179680 | tf_op jit(solution)/shard_map/ppermute | solution.py:761
  256.2 2.9 %attn_finish.1 = (f32[768,384]{1,0:T(8,128)}, f32[768,384]{1,0:T(8,128)}, f32[768,384]{1,0:T(8,128)}, f32[384,768]{1,0:T(8,128)}) custom-call(s32[4]{0:T(128)S(1)} %broadcast_select_fusion.refs_1_.sides_ref, bf16[768,768]{1,0:T(8,128)(2,1)S(1)} %bitcast.77, bf16[768,768]{1,0:T(8,128)(2,1)S(1)} %collective-permute-done.39.got_ref, ...), custom_call_target="tpu_custom_call" | custom-call | flops 2300000000 | tf_op jit(solution)/shard_map/attn_finish/pallas_call | solution.py:712
  (87 shorter events, 23.2 us)
Async XLA Ops:
  0.6 2.4 collective-permute-start
  1.2 16.6 %collective-permute-start.1 = (bf16[768,384]{1,0:T(8,128)(2,1)}, bf16[768,384]{1,0:T(8,128)(2,1)}, u32[]{:S(2)}, u32[]{:S(2)}) collective-permute-start(bf16[768,384]{1,0:T(8,128)(2,1)} %wko.1), channel_id=1, source_target_pairs={{0,1},{1,0},{2,3},{3,2},{4,5},{5,4},{6,7},{7,6},{8,9},{9,8},{10,11... | collective-permute-start | bytes 1769480 | tf_op jit(solution)/shard_map/ppermute | solution.py:816
  1.2 16.6 %collective-permute-start.2 = (bf16[768,384]{1,0:T(8,128)(2,1)}, bf16[768,384]{1,0:T(8,128)(2,1)}, u32[]{:S(2)}, u32[]{:S(2)}) collective-permute-start(bf16[768,384]{1,0:T(8,128)(2,1)} %wvo.1), channel_id=1, source_target_pairs={{0,1},{1,0},{2,3},{3,2},{4,5},{5,4},{6,7},{7,6},{8,9},{9,8},{10,11... | collective-permute-start | bytes 1769480 | tf_op jit(solution)/shard_map/ppermute | solution.py:816
  1.7 16.1 %collective-permute-start.3 = (bf16[384,768]{1,0:T(8,128)(2,1)}, bf16[384,768]{1,0:T(8,128)(2,1)S(1)}, u32[]{:S(2)}, u32[]{:S(2)}) collective-permute-start(bf16[384,768]{1,0:T(8,128)(2,1)} %wo_ref.3), channel_id=1, source_target_pairs={{0,1},{1,0},{2,3},{3,2},{4,5},{5,4},{6,7},{7,6},{8,9},{9,8},{10,11... | collective-permute-start | bytes 1769480 | tf_op jit(solution)/shard_map/ppermute | solution.py:816
  1.8 30.8 %collective-permute-start.5 = (bf16[768,1536]{1,0:T(8,128)(2,1)}, bf16[768,1536]{1,0:T(8,128)(2,1)S(1)}, u32[]{:S(2)}, u32[]{:S(2)}) collective-permute-start(bf16[768,1536]{1,0:T(8,128)(2,1)} %wuo_ref.1), channel_id=1, source_target_pairs={{0,1},{1,0},{2,3},{3,2},{4,5},{5,4},{6,7},{7,6},{8,9},{9,8},{10,11... | collective-permute-start | bytes 7077896 | tf_op jit(solution)/shard_map/ppermute | solution.py:816
  3.0 29.6 %collective-permute-start.4 = (bf16[1536,768]{1,0:T(8,128)(2,1)}, bf16[1536,768]{1,0:T(8,128)(2,1)S(1)}, u32[]{:S(2)}, u32[]{:S(2)}) collective-permute-start(bf16[1536,768]{1,0:T(8,128)(2,1)} %wdo_ref.1), channel_id=1, source_target_pairs={{0,1},{1,0},{2,3},{3,2},{4,5},{5,4},{6,7},{7,6},{8,9},{9,8},{10,11... | collective-permute-start | bytes 7077896 | tf_op jit(solution)/shard_map/ppermute | solution.py:816
  3.4 0.7 copy-start.2
  4.1 0.7 copy-start.3
  32.6 10.4 %copy-start = (bf16[1536,768]{1,0:T(8,128)(2,1)}, bf16[1536,768]{1,0:T(8,128)(2,1)S(1)}, u32[]{:S(2)}) copy-start(bf16[1536,768]{1,0:T(8,128)(2,1)S(1)} %collective-permute-done.4.wd_ref.wdt_ref) | copy-start | bytes 7077892
  42.9 10.0 %collective-permute-start.6 = (bf16[2,768,768]{2,1,0:T(8,128)(2,1)}, bf16[2,768,768]{2,1,0:T(8,128)(2,1)}, u32[]{:S(2)}, u32[]{:S(2)}) collective-permute-start(bf16[2,768,768]{2,1,0:T(8,128)(2,1)} %get-tuple-element.158), channel_id=1, source_target_pairs={{0,1},{1,0},{2,3},{3,2},{4,5},{5,4},{6,7},{7,6},{8,9},{9,8},{10,11... | collective-permute-start | bytes 7077896 | tf_op jit(solution)/shard_map/ppermute | solution.py:816
  52.4 13.2 %collective-permute-start.7 = (bf16[2,768,768]{2,1,0:T(8,128)(2,1)}, bf16[2,768,768]{2,1,0:T(8,128)(2,1)}, u32[]{:S(2)}, u32[]{:S(2)}) collective-permute-start(bf16[2,768,768]{2,1,0:T(8,128)(2,1)} %get-tuple-element.163), channel_id=1, source_target_pairs={{0,1},{1,0},{2,3},{3,2},{4,5},{5,4},{6,7},{7,6},{8,9},{9,8},{10,11... | collective-permute-start | bytes 7077896 | tf_op jit(solution)/shard_map/ppermute | solution.py:816
  62.9 24.1 %collective-permute-start.9 = (bf16[768,768]{1,0:T(8,128)(2,1)S(1)}, bf16[768,768]{1,0:T(8,128)(2,1)S(1)}, u32[]{:S(2)}, u32[]{:S(2)}) collective-permute-start(bf16[768,768]{1,0:T(8,128)(2,1)S(1)} %get-tuple-element.181), channel_id=1, source_target_pairs={{0,2},{1,5},{2,0},{3,7},{4,6},{5,1},{6,4},{7,3},{8,10},{9,13},{10,... | collective-permute-start | bytes 3538952 | tf_op jit(solution)/shard_map/ppermute | solution.py:761
  75.9 26.7 %collective-permute-start.8 = (bf16[768,768]{1,0:T(8,128)(2,1)S(1)}, bf16[768,768]{1,0:T(8,128)(2,1)S(1)}, u32[]{:S(2)}, u32[]{:S(2)}) collective-permute-start(bf16[768,768]{1,0:T(8,128)(2,1)S(1)} %get-tuple-element.179), channel_id=1, source_target_pairs={{0,2},{1,5},{2,0},{3,7},{4,6},{5,1},{6,4},{7,3},{8,10},{9,13},{10,... | collective-permute-start | bytes 3538952 | tf_op jit(solution)/shard_map/ppermute | solution.py:761
  88.2 14.4 %collective-permute-start.10 = (bf16[384,768]{1,0:T(8,128)(2,1)S(1)}, bf16[384,768]{1,0:T(8,128)(2,1)S(1)}, u32[]{:S(2)}, u32[]{:S(2)}) collective-permute-start(bf16[384,768]{1,0:T(8,128)(2,1)S(1)} %get-tuple-element.184), channel_id=1, source_target_pairs={{0,4},{1,3},{2,6},{3,1},{4,0},{5,7},{6,2},{7,5},{8,12},{9,11},{10,... | collective-permute-start | bytes 1769480 | tf_op jit(solution)/shard_map/ppermute | solution.py:761
  104.6 12.1 %collective-permute-start.11 = (bf16[384,768]{1,0:T(8,128)(2,1)S(1)}, bf16[384,768]{1,0:T(8,128)(2,1)S(1)}, u32[]{:S(2)}, u32[]{:S(2)}) collective-permute-start(bf16[384,768]{1,0:T(8,128)(2,1)S(1)} %get-tuple-element.194), channel_id=1, source_target_pairs={{0,4},{1,3},{2,6},{3,1},{4,0},{5,7},{6,2},{7,5},{8,12},{9,11},{10,... | collective-permute-start | bytes 1769480 | tf_op jit(solution)/shard_map/ppermute | solution.py:761
  104.7 12.0 %collective-permute-start.12 = (bf16[192,768]{1,0:T(8,128)(2,1)S(1)}, bf16[192,768]{1,0:T(8,128)(2,1)S(1)}, u32[]{:S(2)}, u32[]{:S(2)}) collective-permute-start(bf16[192,768]{1,0:T(8,128)(2,1)S(1)} %get-tuple-element.196), channel_id=1, source_target_pairs={{0,8},{1,25},{2,10},{3,27},{4,12},{5,29},{6,14},{7,31},{8,0},{9,17... | collective-permute-start | bytes 884744 | tf_op jit(solution)/shard_map/ppermute | solution.py:761
  106.8 39.9 %collective-permute-start.17 = (bf16[1024,768]{1,0:T(8,128)(2,1)S(1)}, bf16[1024,768]{1,0:T(8,128)(2,1)S(1)}, u32[]{:S(2)}, u32[]{:S(2)}) collective-permute-start(bf16[1024,768]{1,0:T(8,128)(2,1)S(1)} %get-tuple-element.224), channel_id=1, source_target_pairs={{0,1},{1,0},{2,3},{3,2},{4,5},{5,4},{6,7},{7,6},{8,9},{9,8},{10,11... | collective-permute-start | bytes 4718600 | tf_op jit(solution)/shard_map/ppermute | solution.py:816
  116.6 30.1 %collective-permute-start.18 = (bf16[512,768]{1,0:T(8,128)(2,1)S(1)}, bf16[512,768]{1,0:T(8,128)(2,1)S(1)}, u32[]{:S(2)}, u32[]{:S(2)}) collective-permute-start(bf16[512,768]{1,0:T(8,128)(2,1)S(1)} %get-tuple-element.226), channel_id=1, source_target_pairs={{0,1},{1,0},{2,3},{3,2},{4,5},{5,4},{6,7},{7,6},{8,9},{9,8},{10,11... | collective-permute-start | bytes 2359304 | tf_op jit(solution)/shard_map/ppermute | solution.py:816
  117.3 16.0 %collective-permute-start.14 = (bf16[96,768]{1,0:T(8,128)(2,1)S(1)}, bf16[96,768]{1,0:T(8,128)(2,1)S(1)}, u32[]{:S(2)}, u32[]{:S(2)}) collective-permute-start(bf16[96,768]{1,0:T(8,128)(2,1)S(1)} %get-tuple-element.205), channel_id=1, source_target_pairs={{0,24},{1,9},{2,26},{3,11},{4,28},{5,13},{6,30},{7,15},{8,16},{9,1... | collective-permute-start | bytes 442376 | tf_op jit(solution)/shard_map/ppermute | solution.py:761
  120.2 13.1 %collective-permute-start.13 = (bf16[192,768]{1,0:T(8,128)(2,1)S(1)}, bf16[192,768]{1,0:T(8,128)(2,1)S(1)}, u32[]{:S(2)}, u32[]{:S(2)}) collective-permute-start(bf16[192,768]{1,0:T(8,128)(2,1)S(1)} %get-tuple-element.203), channel_id=1, source_target_pairs={{0,8},{1,25},{2,10},{3,27},{4,12},{5,29},{6,14},{7,31},{8,0},{9,17... | collective-permute-start | bytes 884744 | tf_op jit(solution)/shard_map/ppermute | solution.py:761
  134.0 12.7 %collective-permute-start.15 = (bf16[96,768]{1,0:T(8,128)(2,1)S(1)}, bf16[96,768]{1,0:T(8,128)(2,1)S(1)}, u32[]{:S(2)}, u32[]{:S(2)}) collective-permute-start(bf16[96,768]{1,0:T(8,128)(2,1)S(1)} %get-tuple-element.221), channel_id=1, source_target_pairs={{0,24},{1,9},{2,26},{3,11},{4,28},{5,13},{6,30},{7,15},{8,16},{9,1... | collective-permute-start | bytes 442376 | tf_op jit(solution)/shard_map/ppermute | solution.py:761
  135.3 11.4 %collective-permute-start.16 = (bf16[96,768]{1,0:T(8,128)(2,1)S(1)}, bf16[96,768]{1,0:T(8,128)(2,1)S(1)}, u32[]{:S(2)}, u32[]{:S(2)}) collective-permute-start(bf16[96,768]{1,0:T(8,128)(2,1)S(1)} %get-tuple-element.222.mine_ref), channel_id=1, source_target_pairs={{0,24},{1,9},{2,26},{3,11},{4,28},{5,13},{6,30},{7,15},{8,16},{9,1... | collective-permute-start | bytes 442376 | tf_op jit(solution)/shard_map/ppermute | solution.py:761
  148.0 16.3 %collective-permute-start.22 = (bf16[768,768]{1,0:T(8,128)(2,1)S(1)}, bf16[768,768]{1,0:T(8,128)(2,1)S(1)}, u32[]{:S(2)}, u32[]{:S(2)}) collective-permute-start(bf16[768,768]{1,0:T(8,128)(2,1)S(1)} %get-tuple-element.236), channel_id=1, source_target_pairs={{0,2},{1,5},{2,0},{3,7},{4,6},{5,1},{6,4},{7,3},{8,10},{9,13},{10,... | collective-permute-start | bytes 3538952 | tf_op jit(solution)/shard_map/ppermute | solution.py:761
  150.1 11.8 %collective-permute-start.21 = (bf16[192,768]{1,0:T(8,128)(2,1)S(1)}, bf16[192,768]{1,0:T(8,128)(2,1)S(1)}, u32[]{:S(2)}, u32[]{:S(2)}) collective-permute-start(bf16[192,768]{1,0:T(8,128)(2,1)S(1)} %bitcast.66), channel_id=1, source_target_pairs={{0,8},{1,25},{2,10},{3,27},{4,12},{5,29},{6,14},{7,31},{8,0},{9,17... | collective-permute-start | bytes 884744 | tf_op jit(solution)/shard_map/ppermute | solution.py:761
  150.3 11.7 %collective-permute-start.20 = (bf16[96,768]{1,0:T(8,128)(2,1)S(1)}, bf16[96,768]{1,0:T(8,128)(2,1)S(1)}, u32[]{:S(2)}, u32[]{:S(2)}) collective-permute-start(bf16[96,768]{1,0:T(8,128)(2,1)S(1)} %get-tuple-element.233.mine_ref), channel_id=1, source_target_pairs={{0,24},{1,9},{2,26},{3,11},{4,28},{5,13},{6,30},{7,15},{8,16},{9,1... | collective-permute-start | bytes 442376 | tf_op jit(solution)/shard_map/ppermute | solution.py:761
  166.1 10.3 %collective-permute-start.25 = (bf16[384,768]{1,0:T(8,128)(2,1)S(1)}, bf16[384,768]{1,0:T(8,128)(2,1)S(1)}, u32[]{:S(2)}, u32[]{:S(2)}) collective-permute-start(bf16[384,768]{1,0:T(8,128)(2,1)S(1)} %bitcast.59), channel_id=1, source_target_pairs={{0,4},{1,3},{2,6},{3,1},{4,0},{5,7},{6,2},{7,5},{8,12},{9,11},{10,... | collective-permute-start | bytes 1769480 | tf_op jit(solution)/shard_map/ppermute | solution.py:761
  167.7 14.7 %collective-permute-start.26 = (bf16[384,768]{1,0:T(8,128)(2,1)S(1)}, bf16[384,768]{1,0:T(8,128)(2,1)S(1)}, u32[]{:S(2)}, u32[]{:S(2)}) collective-permute-start(bf16[384,768]{1,0:T(8,128)(2,1)S(1)} %get-tuple-element.245), channel_id=1, source_target_pairs={{0,4},{1,3},{2,6},{3,1},{4,0},{5,7},{6,2},{7,5},{8,12},{9,11},{10,... | collective-permute-start | bytes 1769480 | tf_op jit(solution)/shard_map/ppermute | solution.py:761
  168.8 7.7 %collective-permute-start.24 = (bf16[192,768]{1,0:T(8,128)(2,1)S(1)}, bf16[192,768]{1,0:T(8,128)(2,1)S(1)}, u32[]{:S(2)}, u32[]{:S(2)}) collective-permute-start(bf16[192,768]{1,0:T(8,128)(2,1)S(1)} %bitcast.68), channel_id=1, source_target_pairs={{0,8},{1,25},{2,10},{3,27},{4,12},{5,29},{6,14},{7,31},{8,0},{9,17... | collective-permute-start | bytes 884744 | tf_op jit(solution)/shard_map/ppermute | solution.py:761
  168.9 1.2 collective-permute-start.19
  170.1 3.8 %collective-permute-start.23 = (f32[2,768]{1,0:T(2,128)S(1)}, f32[2,768]{1,0:T(2,128)S(1)}, u32[]{:S(2)}, u32[]{:S(2)}) collective-permute-start(f32[2,768]{1,0:T(2,128)S(1)} %get-tuple-element.241.a_ref), channel_id=1, source_target_pairs={{0,2},{1,3},{2,0},{3,1},{4,6},{5,7},{6,4},{7,5},{8,10},{9,11},{10,... | collective-permute-start | bytes 18440 | tf_op jit(solution)/shard_map/ppermute | solution.py:758
  182.4 7.5 %copy-start.1 = (bf16[1536,768]{1,0:T(8,128)(2,1)S(1)}, bf16[1536,768]{1,0:T(8,128)(2,1)}, u32[]{:S(2)}) copy-start(bf16[1536,768]{1,0:T(8,128)(2,1)} %copy-done) | copy-start | bytes 7077892
  184.7 15.6 %collective-permute-start.29 = (bf16[384,768]{1,0:T(8,128)(2,1)S(1)}, bf16[384,768]{1,0:T(8,128)(2,1)S(1)}, u32[]{:S(2)}, u32[]{:S(2)}) collective-permute-start(bf16[384,768]{1,0:T(8,128)(2,1)S(1)} %bitcast.57), channel_id=1, source_target_pairs={{0,4},{1,3},{2,6},{3,1},{4,0},{5,7},{6,2},{7,5},{8,12},{9,11},{10,... | collective-permute-start | bytes 1769480 | tf_op jit(solution)/shard_map/ppermute | solution.py:761
  186.3 13.0 %collective-permute-start.28 = (f32[4,32,768]{2,1,0:T(8,128)S(1)}, f32[4,32,768]{2,1,0:T(8,128)S(1)}, u32[]{:S(2)}, u32[]{:S(2)}) collective-permute-start(f32[4,32,768]{2,1,0:T(8,128)S(1)} %get-tuple-element.255.mine_ref), channel_id=1, source_target_pairs={{0,1},{1,0},{2,3},{3,2},{4,5},{5,4},{6,7},{7,6},{8,9},{9,8},{10,11... | collective-permute-start | bytes 1179656 | tf_op jit(solution)/shard_map/ppermute | solution.py:816
  186.3 13.9 %collective-permute-start.27 = (bf16[192,768]{1,0:T(8,128)(2,1)S(1)}, bf16[192,768]{1,0:T(8,128)(2,1)S(1)}, u32[]{:S(2)}, u32[]{:S(2)}) collective-permute-start(bf16[192,768]{1,0:T(8,128)(2,1)S(1)} %get-tuple-element.254), channel_id=1, source_target_pairs={{0,8},{1,25},{2,10},{3,27},{4,12},{5,29},{6,14},{7,31},{8,0},{9,17... | collective-permute-start | bytes 884744 | tf_op jit(solution)/shard_map/ppermute | solution.py:761
  186.3 23.1 %collective-permute-start.32 = (bf16[768,768]{1,0:T(8,128)(2,1)S(1)}, bf16[768,768]{1,0:T(8,128)(2,1)S(1)}, u32[]{:S(2)}, u32[]{:S(2)}) collective-permute-start(bf16[768,768]{1,0:T(8,128)(2,1)S(1)} %bitcast.45), channel_id=1, source_target_pairs={{0,2},{1,5},{2,0},{3,7},{4,6},{5,1},{6,4},{7,3},{8,10},{9,13},{10,... | collective-permute-start | bytes 3538952 | tf_op jit(solution)/shard_map/ppermute | solution.py:761
  187.8 12.4 %collective-permute-start.30 = (f32[2,768]{1,0:T(2,128)S(1)}, f32[2,768]{1,0:T(2,128)S(1)}, u32[]{:S(2)}, u32[]{:S(2)}) collective-permute-start(f32[2,768]{1,0:T(2,128)S(1)} %get-tuple-element.259.a_ref), channel_id=1, source_target_pairs={{0,8},{1,9},{2,10},{3,11},{4,12},{5,13},{6,14},{7,15},{8,0},{9,1},... | collective-permute-start | bytes 18440 | tf_op jit(solution)/shard_map/ppermute | solution.py:758
  201.7 16.3 %collective-permute-start.35 = (bf16[768,768]{1,0:T(8,128)(2,1)S(1)}, bf16[768,768]{1,0:T(8,128)(2,1)S(1)}, u32[]{:S(2)}, u32[]{:S(2)}) collective-permute-start(bf16[768,768]{1,0:T(8,128)(2,1)S(1)} %bitcast.51), channel_id=1, source_target_pairs={{0,2},{1,5},{2,0},{3,7},{4,6},{5,1},{6,4},{7,3},{8,10},{9,13},{10,... | collective-permute-start | bytes 3538952 | tf_op jit(solution)/shard_map/ppermute | solution.py:761
  202.4 7.1 %collective-permute-start.31 = (bf16[96,768]{1,0:T(8,128)(2,1)S(1)}, bf16[96,768]{1,0:T(8,128)(2,1)S(1)}, u32[]{:S(2)}, u32[]{:S(2)}) collective-permute-start(bf16[96,768]{1,0:T(8,128)(2,1)S(1)} %get-tuple-element.261), channel_id=1, source_target_pairs={{0,24},{1,9},{2,26},{3,11},{4,28},{5,13},{6,30},{7,15},{8,16},{9,1... | collective-permute-start | bytes 442376 | tf_op jit(solution)/shard_map/ppermute | solution.py:761
  203.6 5.1 %collective-permute-start.33 = (f32[2,768]{1,0:T(2,128)S(1)}, f32[2,768]{1,0:T(2,128)S(1)}, u32[]{:S(2)}, u32[]{:S(2)}) collective-permute-start(f32[2,768]{1,0:T(2,128)S(1)} %get-tuple-element.266.a_ref), channel_id=1, source_target_pairs={{0,16},{1,17},{2,18},{3,19},{4,20},{5,21},{6,22},{7,23},{8,24},{9,... | collective-permute-start | bytes 18440 | tf_op jit(solution)/shard_map/ppermute | solution.py:758
  209.5 7.0 %collective-permute-start.34 = (bf16[96,768]{1,0:T(8,128)(2,1)S(1)}, bf16[96,768]{1,0:T(8,128)(2,1)S(1)}, u32[]{:S(2)}, u32[]{:S(2)}) collective-permute-start(bf16[96,768]{1,0:T(8,128)(2,1)S(1)} %get-tuple-element.267.mine_ref), channel_id=1, source_target_pairs={{0,24},{1,9},{2,26},{3,11},{4,28},{5,13},{6,30},{7,15},{8,16},{9,1... | collective-permute-start | bytes 442376 | tf_op jit(solution)/shard_map/ppermute | solution.py:761
  210.8 4.1 %collective-permute-start.36 = (f32[2,768]{1,0:T(2,128)S(1)}, f32[2,768]{1,0:T(2,128)S(1)}, u32[]{:S(2)}, u32[]{:S(2)}) collective-permute-start(f32[2,768]{1,0:T(2,128)S(1)} %get-tuple-element.271.a_ref), channel_id=1, source_target_pairs={{0,4},{1,5},{2,6},{3,7},{4,0},{5,1},{6,2},{7,3},{8,12},{9,13},{10,... | collective-permute-start | bytes 18440 | tf_op jit(solution)/shard_map/ppermute | solution.py:758
  218.6 9.9 %collective-permute-start.37 = (bf16[192,768]{1,0:T(8,128)(2,1)S(1)}, bf16[192,768]{1,0:T(8,128)(2,1)S(1)}, u32[]{:S(2)}, u32[]{:S(2)}) collective-permute-start(bf16[192,768]{1,0:T(8,128)(2,1)S(1)} %bitcast.71), channel_id=1, source_target_pairs={{0,8},{1,25},{2,10},{3,27},{4,12},{5,29},{6,14},{7,31},{8,0},{9,17... | collective-permute-start | bytes 884744 | tf_op jit(solution)/shard_map/ppermute | solution.py:761
  229.2 9.9 %collective-permute-start.38 = (bf16[384,768]{1,0:T(8,128)(2,1)S(1)}, bf16[384,768]{1,0:T(8,128)(2,1)S(1)}, u32[]{:S(2)}, u32[]{:S(2)}) collective-permute-start(bf16[384,768]{1,0:T(8,128)(2,1)S(1)} %bitcast.62), channel_id=1, source_target_pairs={{0,4},{1,3},{2,6},{3,1},{4,0},{5,7},{6,2},{7,5},{8,12},{9,11},{10,... | collective-permute-start | bytes 1769480 | tf_op jit(solution)/shard_map/ppermute | solution.py:761
  240.0 16.3 %collective-permute-start.39 = (bf16[768,768]{1,0:T(8,128)(2,1)S(1)}, bf16[768,768]{1,0:T(8,128)(2,1)S(1)}, u32[]{:S(2)}, u32[]{:S(2)}) collective-permute-start(bf16[768,768]{1,0:T(8,128)(2,1)S(1)} %bitcast.76), channel_id=1, source_target_pairs={{0,2},{1,5},{2,0},{3,7},{4,6},{5,1},{6,4},{7,3},{8,10},{9,13},{10,... | collective-permute-start | bytes 3538952 | tf_op jit(solution)/shard_map/ppermute | solution.py:761
